TPU v7x, 32 devices: a whole 2x2x4 slice. The times are simulated.
32 devices in a mesh: section: 2 (over y), row: 4 (over x, core), col: 4 (over z).
Axes of the slice: x: 2, y: 2, z: 4, core: 2. Of those that a mesh axis runs over, the one named last changes fastest.
Arguments:
- x_down: bfloat16 [2, 1024, 8192], P('section', 'row', 'col'), may hold values from -30 to 30
- gain_down: float32 [2, 8192], P('section', 'col'), may hold values from 0.1 to 1.9
- wq_down: bfloat16 [2, 8192, 4096], P('section', 'col', 'row'), may hold values from -2 to 2
- wk_down: bfloat16 [2, 8192, 512], P('section', 'col', 'row'), may hold values from -1 to 1
- wv_down: bfloat16 [2, 8192, 512], P('section', 'col', 'row'), may hold values from -0.0625 to 0.0625
- wo_down: bfloat16 [2, 4096, 8192], P('section', 'row', 'col'), may hold values from -0.09375 to 0.09375
- x_up: bfloat16 [2, 1024, 8192], P('section', 'row', 'col'), may hold values from -30 to 30
- gain_up: float32 [2, 8192], P('section', 'col'), may hold values from 0.1 to 1.9
- wq_up: bfloat16 [2, 8192, 4096], P('section', 'col', 'row'), may hold values from -2 to 2
- wk_up: bfloat16 [2, 8192, 512], P('section', 'col', 'row'), may hold values from -1 to 1
- wv_up: bfloat16 [2, 8192, 512], P('section', 'col', 'row'), may hold values from -0.0625 to 0.0625
- wo_up: bfloat16 [2, 4096, 8192], P('section', 'row', 'col'), may hold values from -0.09375 to 0.09375
Outputs:
- next_down: bfloat16 [2, 1024, 8192], P('section', 'row', 'col')
- next_up: bfloat16 [2, 1024, 8192], P('section', 'row', 'col')
All inputs are finite; a program needn't handle non-finite values.
Results may differ from a plain program's by a relative error of at most 0.0055.
Values may be sent and summed in bfloat16 or wider, within the bound.
No kernel may reach another device: no remote copies, remote signals or barrier semaphores. Data moves between devices by JAX's collectives and lax.ppermute only.
A program may use at most 128 MiB of HBM per device.

v0:
```python
import functools

import jax
import jax.numpy as jnp
from jax import lax
from jax.experimental import pallas as pl
from jax.experimental.pallas import tpu as pltpu
from jax.sharding import PartitionSpec as P

HD = 128
EPSILON = 1e-05
HIDDEN = -1e30
LOG2E = 1.4426950408889634
BF16 = jnp.bfloat16
F32 = jnp.float32


def swapped(value, axis, bit):
    return lax.ppermute(value, axis, [(i, i ^ (1 << bit)) for i in range(lax.axis_size(axis))])


def crossed(value, axis, bits):
    return lax.ppermute(value, axis, [(i, i ^ bits) for i in range(lax.axis_size(axis))])


def from_behind(value, axis, steps):
    count = lax.axis_size(axis)
    return lax.ppermute(value, axis, [(i, (i + steps) % count) for i in range(count)])


def bits_of(axis):
    return lax.axis_size(axis).bit_length() - 1


def my_bit(axis, bit):
    return (lax.axis_index(axis) >> bit) & 1


def pick(value, index, dim):
    return lax.dynamic_index_in_dim(value, index, dim, keepdims=False)


def tie(value, *deps):
    return lax.optimization_barrier((value, deps))[0]


class Chain:
    def __init__(self):
        self.token = None

    def enter(self, *values):
        out = values if self.token is None else tie(values, self.token)
        return out[0] if len(values) == 1 else out

    def leave(self, array):
        self.token = array


def turn(value, cosine, sine):
    return value * cosine + pltpu.roll(value, HD // 2, 1) * sine


def rows_of(keeps, arrivals, inverse, columns):
    parts = [k[:, columns] + a[:, columns].astype(F32) for k, a in zip(keeps, arrivals)]
    return jnp.concatenate(parts, axis=0) * inverse[...]


def kv_kernel(qw, kvw, keep_a, keep_b, arr_a, arr_b, inverse, cosine, sine, out):
    for start in range(0, 2 * kvw, HD):
        columns = slice(qw + start, qw + start + HD)
        value = rows_of((keep_a, keep_b), (arr_a, arr_b), inverse, columns)
        if start < kvw:
            value = turn(value, cosine[...], sine[...])
        out[:, start : start + HD] = value.astype(BF16)


def attention_kernel(
    qw, kvw, count, keep_a, keep_b, arr_a, arr_b, inverse, cosine, sine, q_pos, k_pos, *rest
):
    pairs, (out, keys, values, bias) = rest[:count], rest[count:]
    rows = pairs[0].shape[0]
    for i, pair in enumerate(pairs):
        keys[i * rows : (i + 1) * rows] = pair[:, :kvw]
        values[i * rows : (i + 1) * rows] = pair[:, kvw:]
    bias[...] = jnp.where(q_pos[...] >= k_pos[...], 0.0, HIDDEN)
    group = (qw // HD) // (kvw // HD)
    for head in range(qw // HD):
        columns = slice(head * HD, (head + 1) * HD)
        kv_columns = slice(head // group * HD, (head // group + 1) * HD)
        query = rows_of((keep_a, keep_b), (arr_a, arr_b), inverse, columns)
        query = turn(query, cosine[...], sine[...]).astype(BF16)
        scores = lax.dot_general(
            query, keys[:, kv_columns], (((1,), (1,)), ((), ())), preferred_element_type=F32
        )
        scores = scores + bias[...]
        top = jnp.max(scores, axis=1, keepdims=True)
        probs = jnp.exp2((scores - top) * (LOG2E / HD**0.5))
        total = jnp.sum(probs, axis=1, keepdims=True)
        mixed = jnp.dot(probs.astype(BF16), values[:, kv_columns], preferred_element_type=F32)
        out[:, columns] = (mixed / total).astype(BF16)


def gather(block, axis):
    blocks = {0: block}
    for bit in range(1, bits_of(axis)):
        for o in list(blocks):
            blocks[o | 1 << bit] = swapped(blocks[o], axis, bit)
    return blocks


class Cascade:
    def __init__(self, x, gain, wq, wk, wv, wo):
        self.x, self.gain, self.wo = x, gain, wo
        if wk.shape[1] < HD:
            other_k, other_v = swapped((wk, wv), "row", 0)
            even = lax.axis_index("row") % 2 == 0
            wk = jnp.where(even, jnp.concatenate([wk, other_k], 1), jnp.concatenate([other_k, wk], 1))
            wv = jnp.where(even, jnp.concatenate([wv, other_v], 1), jnp.concatenate([other_v, wv], 1))
        self.qw, self.kvw = wq.shape[1], wk.shape[1]
        self.w = jnp.concatenate([wq, wk, wv], axis=1)
        self.n_row, self.n_col = lax.axis_size("row"), lax.axis_size("col")
        self.sub = x.shape[0] // self.n_col
        self.keep, self.arrived = [], []

    def halves(self, block_list):
        low = my_bit("col", 0)
        blocks = jnp.stack(block_list).reshape(len(block_list), self.n_col // 2, 2, self.sub, -1)
        return pick(blocks, 1 - low, 2), pick(blocks, low, 2)

    def project(self, half):
        scaled = (half.astype(F32) * self.gain).astype(BF16)
        rows = scaled.reshape(-1, scaled.shape[-1])
        out = jnp.dot(rows, self.w, preferred_element_type=F32)
        return out.reshape(half.shape[:-1] + (-1,))

    def halve(self, total, arrived, bit):
        mine = my_bit("col", bit)
        shape = (total.shape[0], -1, 2) + total.shape[2:]
        total, arrived = total.reshape(shape), arrived.reshape(shape)

        def part(which):
            return pick(total, which, 2) + pick(arrived, which, 2).astype(F32)

        return part(mine), part(1 - mine).astype(BF16)

    def flat(self, value):
        return value.reshape(-1, value.shape[-1])

    def kernel_rows(self):
        return [self.flat(v) for v in self.keep] + [self.flat(v) for v in self.arrived]


def whole(body, out_shape, scratch=(), flops=0, exps=0, moved=0):
    return pl.pallas_call(
        body,
        out_shape=out_shape,
        scratch_shapes=list(scratch),
        compiler_params=pltpu.CompilerParams(vmem_limit_bytes=40 * 1024 * 1024),
        cost_estimate=pl.CostEstimate(flops=flops, transcendentals=exps, bytes_accessed=moved),
    )


def on_device(*arrays):
    arrays = [a[0] for a in arrays]
    half = len(arrays) // 2
    d, u = Cascade(*arrays[:half]), Cascade(*arrays[half:])
    n_row, n_col, sub = d.n_row, d.n_col, d.sub
    block = n_col * sub
    features = d.x.shape[1] * n_col
    rows = n_row * sub
    qw, kvw = d.qw, d.kvw
    z, r = lax.axis_index("col"), lax.axis_index("row")
    chain = Chain()

    order = [o for o in range(n_row) if o < 2] + [o for o in range(n_row) if o >= 2]
    starts = (r ^ jnp.array(order, jnp.int32)) * block
    offsets = jnp.arange(sub, dtype=jnp.int32)
    q_pos = (starts[:, None] + z * sub + offsets).astype(F32).reshape(rows, 1)
    owners = (z ^ jnp.arange(n_col, dtype=jnp.int32)) * sub
    k_pos = (owners[:, None, None] + starts[:, None] + offsets).astype(F32).reshape(1, -1)
    width = HD // 2
    inverse_freq = 10000.0 ** (-jnp.arange(width, dtype=F32) / width)
    angles = q_pos * inverse_freq
    cosine = jnp.concatenate([jnp.cos(angles)] * 2, axis=1)
    sine = jnp.sin(angles)
    sine = jnp.concatenate([-sine, sine], axis=1)

    d_blocks = gather(d.x, "row")
    d_blocks[1] = swapped(d.x, "row", 0)

    def send_first(c, group, blocks_):
        send, kept = c.halves(chain.enter(*blocks_))
        product = c.project(send).astype(BF16)
        return product, kept

    def keep_first(c, kept, token):
        return c.project(tie(kept, token))

    def second(c, total, arrived):
        total, arrived = chain.enter(total, arrived)
        kept, product = c.halve(total, arrived, 1)
        arrived = swapped(product, "col", 1)
        chain.leave(product)
        for bit in range(2, bits_of("col")):
            kept, product = c.halve(kept, arrived, bit)
            arrived = swapped(product, "col", bit)
        c.keep.append(kept)
        c.arrived.append(arrived)

    def settle(c):
        c.arrived[-1] = chain.enter(c.arrived[-1])
        chain.leave(c.arrived[-1])

    def take_far(blocks_):
        values = chain.enter(*[blocks_[o] for o in far])
        values = list(values) if len(far) > 1 else [values]
        for o, value in zip(far, values):
            blocks_[o] = value
            blocks_[o | 1] = swapped(value, "row", 0)
        chain.leave(values[-1])
        return values

    far = [o for o in d_blocks if o >= 2]
    far_order = [o for o in order if o >= 2]

    product, kept = send_first(d, 0, [d_blocks[0], d_blocks[1]])
    d_arr_a = swapped(product, "col", 0)
    d_tot_a = keep_first(d, kept, product)
    u_near = swapped(tie(u.x, product), "row", 0)
    chain.leave(d_tot_a)
    squares = jnp.stack([jnp.sum(jnp.square(chain.enter(c.x).astype(F32)), axis=1) for c in (d, u)])
    other = swapped(squares, "col", 0)
    chain.leave(squares)
    u_prod_a, kept = send_first(u, 0, [u.x, u_near])
    u_kept = kept
    chain.leave(u_prod_a)
    second(d, d_tot_a, d_arr_a)
    u_arr_a = swapped(tie(u_prod_a, chain.token), "col", 0)

    d_far = take_far(d_blocks)
    u_blocks = gather(tie(u.x, *d_far), "row")
    squares, other = chain.enter(squares, other)
    squares = squares + other
    other = swapped(squares, "col", 1)
    chain.leave(squares)
    u_tot_a = u.project(chain.enter(u_kept))
    chain.leave(u_tot_a)
    product, kept = send_first(d, 1, [d_blocks[o] for o in far_order])
    d_arr_b = swapped(product, "col", 0)
    d_tot_b = keep_first(d, kept, product)
    chain.leave(d_tot_b)
    settle(d)
    squares, other = chain.enter(squares, other)
    squares = squares + other
    for bit in range(2, bits_of("col")):
        squares = squares + swapped(squares, "col", bit)
    chain.leave(squares)
    sq = gather(squares, "row")
    second(u, u_tot_a, u_arr_a)

    take_far(u_blocks)
    second(d, d_tot_b, d_arr_b)
    for o in list(sq):
        sq[o | 1] = swapped(tie(sq[o], chain.token), "row", 0)
    u_prod_b, kept = send_first(u, 1, [u_blocks[o] for o in far_order])
    u_arr_b = swapped(u_prod_b, "col", 0)
    u_tot_b = keep_first(u, kept, u_prod_b)
    chain.leave(u_tot_b)
    settle(u)

    sums = jnp.stack([sq[o] for o in order])
    sums = pick(sums.reshape(n_row, 2, n_col, sub), z, 2)
    inverse = lax.rsqrt(sums / features + EPSILON).transpose(1, 0, 2).reshape(2, rows, 1)

    def make_pairs(c, scale):
        inputs = chain.enter(*c.kernel_rows())
        pair = whole(
            functools.partial(kv_kernel, qw, kvw),
            jax.ShapeDtypeStruct((rows, 2 * kvw), BF16),
            moved=2 * rows * (qw + 2 * kvw) * 6,
        )(*inputs, scale, cosine, sine)
        chain.leave(pair)
        return inputs, [pair] + [crossed(pair, "col", o) for o in range(1, n_col)]

    def attend(c, inputs, scale, pairs):
        pairs = chain.enter(*pairs)
        keys = rows * n_col
        out = whole(
            functools.partial(attention_kernel, qw, kvw, n_col),
            jax.ShapeDtypeStruct((rows, qw), BF16),
            scratch=[pltpu.VMEM((keys, kvw), BF16), pltpu.VMEM((keys, kvw), BF16), pltpu.VMEM((rows, keys), F32)],
            flops=4 * rows * keys * qw,
            exps=rows * keys * qw // HD,
            moved=rows * qw * 8,
        )(*inputs, scale, cosine, sine, q_pos, k_pos, *pairs)
        chain.leave(out)
        return out

    d_inputs, d_pairs = make_pairs(d, inverse[0])
    second(u, u_tot_b, u_arr_b)
    d_att = attend(d, d_inputs, inverse[0], d_pairs)
    d_got = gather(d_att, "col")
    d_got[1] = swapped(d_att, "col", 0)

    def out_first(c, pieces):
        pieces = chain.enter(*pieces)
        pieces = pieces if isinstance(pieces, (list, tuple)) else [pieces]
        shaped = jnp.stack([p.reshape(n_row // 2, 2, sub, qw) for p in pieces], axis=2)

        def dot(value):
            out = jnp.dot(value.reshape(-1, qw), c.wo, preferred_element_type=F32)
            return out.reshape(n_row // 2, -1, c.wo.shape[1])

        product = dot(shaped[:, 1]).astype(BF16)
        arrived = swapped(product, "row", 0)
        kept = dot(tie(shaped[:, 0], product))
        chain.leave(kept)
        return kept, arrived

    def out_second(kept, arrived):
        kept, arrived = chain.enter(kept, arrived)
        for bit in range(1, bits_of("row")):
            total = (kept + arrived.astype(F32)).reshape(-1, 2, *kept.shape[1:])
            product = total[:, 1].astype(BF16)
            kept, arrived = total[:, 0], swapped(product, "row", bit)
        chain.leave(product)
        return kept, arrived

    def out_third(c, kept, arrived, which, steps):
        kept, arrived = chain.enter(kept, arrived)
        residual = c.x.reshape(n_col, sub, -1)
        own = jnp.stack([pick(residual, z ^ o, 0) for o in which]).astype(F32)
        total = kept[0] + arrived[0].astype(F32)
        fresh = (own + total.reshape(own.shape)).astype(BF16)
        chain.leave(fresh)
        return from_behind(fresh, "section", steps)

    def finish(c, groups, *sent):
        by_name = {o: piece[i] for names, piece in zip(groups, sent) for i, o in enumerate(names)}
        both = jnp.stack([by_name[o] for o in range(n_col)])
        both = both.reshape((2,) * bits_of("col") + (sub, -1))
        for bit in range(bits_of("col")):
            dim = bits_of("col") - 1 - bit
            both = jnp.where(my_bit("col", bit) == 0, both, jnp.flip(both, dim))
        return both.reshape(c.x.shape)[None]

    def far_pieces(got):
        names = [o for o in got if o >= 2]
        values = chain.enter(*[got[o] for o in names])
        values = list(values) if len(names) > 1 else [values]
        chain.leave(values[-1])
        for o, value in zip(names, values):
            got[o] = value
            got[o | 1] = swapped(value, "col", 0)

    far_names = [[o for o in range(2, n_col) if o % 2 == 0], [o for o in range(2, n_col) if o % 2]]
    of_d, of_u = [[0, 1]] + far_names, [[0], [1]] + far_names

    def first(c, got, names):
        return out_first(c, [got[o] for o in names])

    def landed(sent):
        sent = chain.enter(sent)
        chain.leave(sent)
        return sent

    u_inputs, u_pairs = make_pairs(u, inverse[1])
    far_pieces(d_got)
    d_p = first(d, d_got, of_d[0])
    d_p = out_second(*d_p)
    u_att = attend(u, u_inputs, inverse[1], u_pairs)
    u_got = gather(u_att, "col")
    u_got[1] = swapped(u_att, "col", 0)
    d_p = out_third(d, *d_p, of_d[0], 1)
    d_m = first(d, d_got, of_d[1])
    d_m = out_second(*d_m)
    d_q = first(d, d_got, of_d[2])
    d_q = out_second(*d_q)
    u_o = first(u, u_got, of_u[0])
    u_o = out_second(*u_o)
    d_m = out_third(d, *d_m, of_d[1], 1)
    d_q = out_third(d, *d_q, of_d[2], 1)
    d_p = landed(d_p)
    d_m = landed(d_m)
    u_p = first(u, u_got, of_u[1])
    u_p = out_second(*u_p)
    far_pieces(u_got)
    u_m = first(u, u_got, of_u[2])
    u_m = out_second(*u_m)
    u_o = out_third(u, *u_o, of_u[0], -1)
    d_q = landed(d_q)
    u_p = out_third(u, *u_p, of_u[1], -1)
    u_q = first(u, u_got, of_u[3])
    u_q = out_second(*u_q)
    u_o = landed(u_o)
    u_m = out_third(u, *u_m, of_u[2], -1)
    u_p = landed(u_p)
    u_q = out_third(u, *u_q, of_u[3], -1)
    return finish(d, of_d, d_p, d_m, d_q), finish(u, of_u, u_o, u_p, u_m, u_q)


def solution(mesh):
    tokens = P("section", "row", "col")
    into, out_of = P("section", "col", "row"), P("section", "row", "col")
    one = (tokens, P("section", "col"), into, into, into, out_of)
    return jax.shard_map(
        on_device, mesh=mesh, in_specs=one + one, out_specs=(tokens, tokens), check_vma=False
    )
```

profile of v0, /device:TPU:0, one launch (start us, length us, event | category | flops | bytes accessed | tf_op | source)
XLA Modules:
  0.0 280.7 jit_solution(1035657934826221508)
XLA Ops:
  1.1 2.6 collective-permute-start.3
  4.4 1.1 fusion.80
  5.7 4.4 %convolution_convert_fusion.3 = bf16[2,2,64,1280]{3,2,1,0:T(8,128)(2,1)S(1)} fusion(s32[]{:T(128)S(6)} %select_n.81, bf16[1,2,2,64,2048]{4,3,2,1,0:T(8,128)(2,1)} %bitcast.298, bf16[1,2,2,64,2048]{4,3,2,1,0:T(8,128)(2,1)S(1)} %bitcast.319, f32[2048]{0:T(1024)} %bitcast.360, bf16[2048,128]{1,0:T(8,128)(2,1)} %bitcast.344, bf16[2048,128]{1,0:T(8,128)(2,1)} %bitcast.348, ...), kind=kOutput, calls=%fused_computation.34 | convolution fusion | flops 1360330752 | bytes 8003588 | tf_op jit(solution)/shard_map/dot_general | solution.py:133
  10.4 1.6 fusion.53
  11.9 2.2 collective-permute-start.1
  14.8 1.6 convolution_convert_fusion.2
  16.4 13.0 %collective-permute-done.1 = bf16[2,2,64,1280]{3,2,1,0:T(8,128)(2,1)S(1)} collective-permute-done((bf16[2,2,64,1280]{3,2,1,0:T(8,128)(2,1)S(1)}, bf16[2,2,64,1280]{3,2,1,0:T(8,128)(2,1)S(1)}, u32[]{:S(2)}, u32[]{:S(2)}) %collective-permute-start.1) | collective-permute-done | bytes 655392 | tf_op jit(solution)/shard_map/ppermute | solution.py:19
  29.7 1.8 collective-permute-start.5
  31.5 2.6 collective-permute-start.10
  34.1 2.0 collective-permute-start.9
  36.2 1.6 collective-permute-start.8
  37.8 1.5 collective-permute-start.7
  39.3 1.6 fusion.54
  40.9 2.6 convolution_convert_fusion.1
  43.6 1.1 fusion.70
  45.2 1.6 fusion.55
  46.8 2.5 collective-permute-done.10
  49.3 11.6 %collective-permute-done.8 = bf16[2,2,64,1280]{3,2,1,0:T(8,128)(2,1)S(1)} collective-permute-done((bf16[2,2,64,1280]{3,2,1,0:T(8,128)(2,1)S(1)}, bf16[2,2,64,1280]{3,2,1,0:T(8,128)(2,1)S(1)}, u32[]{:S(2)}, u32[]{:S(2)}) %collective-permute-start.8) | collective-permute-done | bytes 655392 | tf_op jit(solution)/shard_map/ppermute | solution.py:19
  61.9 1.5 collective-permute-start.15
  63.4 9.5 %collective-permute-done.6 = bf16[2,2,64,1280]{3,2,1,0:T(8,128)(2,1)S(1)} collective-permute-done((bf16[2,2,64,1280]{3,2,1,0:T(8,128)(2,1)S(1)}, bf16[2,2,64,1280]{3,2,1,0:T(8,128)(2,1)S(1)}, u32[]{:S(2)}, u32[]{:S(2)}) %collective-permute-start.6) | collective-permute-done | bytes 655392 | tf_op jit(solution)/shard_map/ppermute | solution.py:19
  75.5 2.9 %collective-permute-start.11 = (bf16[2,1,64,1280]{3,2,1,0:T(8,128)(2,1)}, bf16[2,1,64,1280]{3,2,1,0:T(8,128)(2,1)S(1)}, u32[]{:S(2)}, u32[]{:S(2)}) collective-permute-start(bf16[2,1,64,1280]{3,2,1,0:T(8,128)(2,1)} %get-tuple-element.206), channel_id=1, source_target_pairs={{0,2},{1,3},{2,0},{3,1},{4,6},{5,7},{6,4},{7,5},{8,10},{9,11},{10,... | collective-permute-start | bytes 983048 | tf_op jit(solution)/shard_map/ppermute | solution.py:19
  78.8 4.8 %convolution_convert_fusion = bf16[2,2,64,1280]{3,2,1,0:T(8,128)(2,1)S(1)} fusion(s32[]{:T(128)S(6)} %select_n.81, bf16[1,2,2,64,2048]{4,3,2,1,0:T(8,128)(2,1)} %bitcast.35, bf16[1,2,2,64,2048]{4,3,2,1,0:T(8,128)(2,1)} %bitcast.36, f32[2048]{0:T(1024)S(1)} %bitcast.366, bf16[2048,128]{1,0:T(8,128)(2,1)} %bitcast.352, bf16[2048,128]{1,0:T(8,128)(2,1)} %bitcast.356, ...), kind=kOutput, calls=%fused_computation.31 | convolution fusion | flops 1360330752 | bytes 8003588 | tf_op jit(solution)/shard_map/dot_general | solution.py:133
  83.7 1.3 fusion.65
  85.0 1.6 fusion.56
  86.6 12.7 %collective-permute-done.12 = bf16[2,1,64,1280]{3,2,1,0:T(8,128)(2,1)S(1)} collective-permute-done((bf16[2,1,64,1280]{3,2,1,0:T(8,128)(2,1)}, bf16[2,1,64,1280]{3,2,1,0:T(8,128)(2,1)S(1)}, u32[]{:S(2)}, u32[]{:S(2)}) %collective-permute-start.12) | collective-permute-done | bytes 327712 | tf_op jit(solution)/shard_map/ppermute | solution.py:19
  99.3 6.9 %collective-permute-done.11 = bf16[2,1,64,1280]{3,2,1,0:T(8,128)(2,1)S(1)} collective-permute-done((bf16[2,1,64,1280]{3,2,1,0:T(8,128)(2,1)}, bf16[2,1,64,1280]{3,2,1,0:T(8,128)(2,1)S(1)}, u32[]{:S(2)}, u32[]{:S(2)}) %collective-permute-start.11) | collective-permute-done | bytes 327712 | tf_op jit(solution)/shard_map/ppermute | solution.py:19
  106.5 2.0 collective-permute-start.18
  108.5 2.4 collective-permute-start.19
  110.9 9.8 %collective-permute-done.20 = bf16[2,2,64,1280]{3,2,1,0:T(8,128)(2,1)S(1)} collective-permute-done((bf16[2,2,64,1280]{3,2,1,0:T(8,128)(2,1)S(1)}, bf16[2,2,64,1280]{3,2,1,0:T(8,128)(2,1)S(1)}, u32[]{:S(2)}, u32[]{:S(2)}) %collective-permute-start.20) | collective-permute-done | bytes 655392 | tf_op jit(solution)/shard_map/ppermute | solution.py:19
  124.1 4.5 %shard_map.141 = bf16[256,1024]{1,0:T(8,128)(2,1)S(1)} custom-call(f32[128,1280]{1,0:T(8,128)S(1)} %bitcast.279, f32[128,1280]{1,0:T(8,128)S(1)} %bitcast.283, bf16[128,1280]{1,0:T(8,128)(2,1)S(1)} %bitcast.290, bf16[128,1280]{1,0:T(8,128)(2,1)S(1)} %bitcast.294, f32[256,1]{1,0:T(8,128)S(1)} %squeeze.177.inverse, f32[256,128]{1,0:T(8,128)S(1)} %pad_maximum_fusion.3.cosine, ...), custom_call_target="tpu_custom_call" | custom-call | flops 1073741824 | bytes 2097152 | tf_op jit(solution)/shard_map/pallas_call | solution.py:288
  128.8 2.8 collective-permute-start.23
  131.7 35.3 %collective-permute-done.23 = bf16[2,1,64,1280]{3,2,1,0:T(8,128)(2,1)S(1)} collective-permute-done((bf16[2,1,64,1280]{3,2,1,0:T(8,128)(2,1)}, bf16[2,1,64,1280]{3,2,1,0:T(8,128)(2,1)S(1)}, u32[]{:S(2)}, u32[]{:S(2)}) %collective-permute-start.23) | collective-permute-done | bytes 327712 | tf_op jit(solution)/shard_map/ppermute | solution.py:19
  168.2 1.3 pad_maximum_fusion.2
  170.3 2.2 fusion.28
  172.6 1.1 constant_dynamic-slice_fusion.1
  174.6 3.5 %collective-permute-start.28 = (bf16[256,256]{1,0:T(8,128)(2,1)S(1)}, bf16[256,256]{1,0:T(8,128)(2,1)S(1)}, u32[]{:S(2)}, u32[]{:S(2)}) collective-permute-start(bf16[256,256]{1,0:T(8,128)(2,1)S(1)} %shard_map.142.rest_0_), channel_id=1, source_target_pairs={{0,3},{1,2},{2,1},{3,0},{4,7},{5,6},{6,5},{7,4},{8,11},{9,10},{10,... | collective-permute-start | bytes 393224 | tf_op jit(solution)/shard_map/ppermute | solution.py:23
  178.1 3.5 %fusion.24 = f32[2,128,2048]{2,1,0:T(8,128)S(1)} fusion(bf16[2,128,1024]{2,1,0:T(8,128)(2,1)S(1)} %bitcast.315, bf16[1,1024,2048]{2,1,0:T(8,128)(2,1)} %param.18), kind=kOutput, calls=%fused_computation.26 | convolution fusion | flops 1073741824 | bytes 6815744 | tf_op jit(solution)/shard_map/dot_general | solution.py:311
  181.6 1.6 add_bitcast_fusion
  183.3 1.6 collective-permute-start.25
  184.8 1.8 collective-permute-done.27.rest_2_
  186.7 14.6 %shard_map.143 = bf16[256,1024]{1,0:T(8,128)(2,1)S(1)} custom-call(f32[128,1280]{1,0:T(8,128)S(1)} %bitcast.277, f32[128,1280]{1,0:T(8,128)S(1)} %bitcast.281, bf16[128,1280]{1,0:T(8,128)(2,1)S(1)} %bitcast.288, bf16[128,1280]{1,0:T(8,128)(2,1)S(1)} %bitcast.292, f32[256,1]{1,0:T(8,128)S(1)} %squeeze.178.inverse, f32[256,128]{1,0:T(8,128)S(1)} %pad_maximum_fusion.3.cosine, ...), custom_call_target="tpu_custom_call" | custom-call | flops 1073741824 | bytes 2097152 | tf_op jit(solution)/shard_map/pallas_call | solution.py:288
  201.4 3.0 %collective-permute-start.40 = (bf16[256,1024]{1,0:T(8,128)(2,1)S(1)}, bf16[256,1024]{1,0:T(8,128)(2,1)S(1)}, u32[]{:S(2)}, u32[]{:S(2)}) collective-permute-start(bf16[256,1024]{1,0:T(8,128)(2,1)S(1)} %shard_map.143), channel_id=1, source_target_pairs={{0,1},{1,0},{2,3},{3,2},{4,5},{5,4},{6,7},{7,6},{8,9},{9,8},{10,11... | collective-permute-start | bytes 1572872 | tf_op jit(solution)/shard_map/ppermute | solution.py:19
  204.7 1.6 collective-permute-start.29
  206.3 1.7 fusion.31
  210.9 1.6 collective-permute-start.34
  213.3 1.1 collective-permute-done.32
  218.0 1.5 collective-permute-done.34
  219.5 1.9 collective-permute-start.38
  221.5 5.0 %collective-permute-done.33 = bf16[1,64,2048]{2,1,0:T(8,128)(2,1)S(1)} collective-permute-done((bf16[1,64,2048]{2,1,0:T(8,128)(2,1)S(1)}, bf16[1,64,2048]{2,1,0:T(8,128)(2,1)S(1)}, u32[]{:S(2)}, u32[]{:S(2)}) %collective-permute-start.33) | collective-permute-done | bytes 262176 | tf_op jit(solution)/shard_map/ppermute | solution.py:19
  227.1 1.6 collective-permute-start.37
  228.7 7.0 %collective-permute-done.36 = bf16[1,64,2048]{2,1,0:T(8,128)(2,1)S(1)} collective-permute-done((bf16[1,64,2048]{2,1,0:T(8,128)(2,1)S(1)}, bf16[1,64,2048]{2,1,0:T(8,128)(2,1)S(1)}, u32[]{:S(2)}, u32[]{:S(2)}) %collective-permute-start.36) | collective-permute-done | bytes 262176 | tf_op jit(solution)/shard_map/ppermute | solution.py:28
  237.3 1.1 collective-permute-done.41
  240.0 1.9 collective-permute-start.44
  242.7 1.1 collective-permute-done.42
  244.1 3.7 %collective-permute-done.45 = bf16[1,64,2048]{2,1,0:T(8,128)(2,1)S(1)} collective-permute-done((bf16[1,64,2048]{2,1,0:T(8,128)(2,1)S(1)}, bf16[1,64,2048]{2,1,0:T(8,128)(2,1)S(1)}, u32[]{:S(2)}, u32[]{:S(2)}) %collective-permute-start.45) | collective-permute-done | bytes 262176 | tf_op jit(solution)/shard_map/ppermute | solution.py:19
  247.9 6.0 %collective-permute-done.44 = bf16[256,1024]{1,0:T(8,128)(2,1)S(1)} collective-permute-done((bf16[256,1024]{1,0:T(8,128)(2,1)S(1)}, bf16[256,1024]{1,0:T(8,128)(2,1)S(1)}, u32[]{:S(2)}, u32[]{:S(2)}) %collective-permute-start.44) | collective-permute-done | bytes 524320 | tf_op jit(solution)/shard_map/ppermute | solution.py:19
  255.2 1.5 collective-permute-start.48
  256.7 1.6 collective-permute-start.47
  261.0 3.0 %collective-permute-done.43 = bf16[1,64,2048]{2,1,0:T(8,128)(2,1)S(1)} collective-permute-done((bf16[1,64,2048]{2,1,0:T(8,128)(2,1)S(1)}, bf16[1,64,2048]{2,1,0:T(8,128)(2,1)S(1)}, u32[]{:S(2)}, u32[]{:S(2)}) %collective-permute-start.43) | collective-permute-done | bytes 262176 | tf_op jit(solution)/shard_map/ppermute | solution.py:28
  264.6 5.0 %collective-permute-done.47 = bf16[1,64,2048]{2,1,0:T(8,128)(2,1)S(1)} collective-permute-done((bf16[1,64,2048]{2,1,0:T(8,128)(2,1)S(1)}, bf16[1,64,2048]{2,1,0:T(8,128)(2,1)S(1)}, u32[]{:S(2)}, u32[]{:S(2)}) %collective-permute-start.47) | collective-permute-done | bytes 262176 | tf_op jit(solution)/shard_map/ppermute | solution.py:28
  270.3 1.2 reverse_select_fusion.2
  271.5 3.7 %collective-permute-done.49 = bf16[1,64,2048]{2,1,0:T(8,128)(2,1)S(1)} collective-permute-done((bf16[1,64,2048]{2,1,0:T(8,128)(2,1)S(1)}, bf16[1,64,2048]{2,1,0:T(8,128)(2,1)S(1)}, u32[]{:S(2)}, u32[]{:S(2)}) %collective-permute-start.49) | collective-permute-done | bytes 262176 | tf_op jit(solution)/shard_map/ppermute | solution.py:28
  275.2 3.8 %collective-permute-done.51 = bf16[1,64,2048]{2,1,0:T(8,128)(2,1)S(1)} collective-permute-done((bf16[1,64,2048]{2,1,0:T(8,128)(2,1)S(1)}, bf16[1,64,2048]{2,1,0:T(8,128)(2,1)S(1)}, u32[]{:S(2)}, u32[]{:S(2)}) %collective-permute-start.51) | collective-permute-done | bytes 262176 | tf_op jit(solution)/shard_map/ppermute | solution.py:28
  279.3 1.2 reverse_select_fusion
  (198 shorter events, 32.0 us)
Async XLA Ops:
  0.6 3.8 %collective-permute-start = (bf16[256,2048]{1,0:T(8,128)(2,1)}, bf16[256,2048]{1,0:T(8,128)(2,1)S(1)}, u32[]{:S(2)}, u32[]{:S(2)}) collective-permute-start(bf16[256,2048]{1,0:T(8,128)(2,1)} %bitcast.295), channel_id=1, source_target_pairs={{0,4},{4,0},{8,12},{12,8},{1,5},{5,1},{9,13},{13,9},{2,6},{6,2},{1... | collective-permute-start | bytes 3145736 | tf_op jit(solution)/shard_map/ppermute | solution.py:19
  1.1 28.3 %collective-permute-start.3 = (bf16[256,2048]{1,0:T(8,128)(2,1)}, bf16[256,2048]{1,0:T(8,128)(2,1)}, u32[]{:S(2)}, u32[]{:S(2)}) collective-permute-start(bf16[256,2048]{1,0:T(8,128)(2,1)} %bitcast.296), channel_id=1, source_target_pairs={{0,8},{4,12},{8,0},{12,4},{1,9},{5,13},{9,1},{13,5},{2,10},{6,14},... | collective-permute-start | bytes 3145736 | tf_op jit(solution)/shard_map/ppermute | solution.py:19
  5.6 4.7 %copy-start.16 = (bf16[1,2048,1024]{2,1,0:T(8,128)(2,1)S(1)}, bf16[1,2048,1024]{2,1,0:T(8,128)(2,1)}, u32[]{:S(2)}) copy-start(bf16[1,2048,1024]{2,1,0:T(8,128)(2,1)} %param.15) | copy-start | bytes 12582916
  10.1 4.6 %collective-permute-start.2 = (bf16[256,2048]{1,0:T(8,128)(2,1)S(1)}, bf16[256,2048]{1,0:T(8,128)(2,1)S(1)}, u32[]{:S(2)}, u32[]{:S(2)}) collective-permute-start(bf16[256,2048]{1,0:T(8,128)(2,1)S(1)} %bitcast.303), channel_id=1, source_target_pairs={{0,4},{4,0},{8,12},{12,8},{1,5},{5,1},{9,13},{13,9},{2,6},{6,2},{1... | collective-permute-start | bytes 3145736 | tf_op jit(solution)/shard_map/ppermute | solution.py:19
  11.9 17.4 %collective-permute-start.1 = (bf16[2,2,64,1280]{3,2,1,0:T(8,128)(2,1)S(1)}, bf16[2,2,64,1280]{3,2,1,0:T(8,128)(2,1)S(1)}, u32[]{:S(2)}, u32[]{:S(2)}) collective-permute-start(bf16[2,2,64,1280]{3,2,1,0:T(8,128)(2,1)S(1)} %convolution_convert_fusion.3), channel_id=1, source_target_pairs={{0,1},{1,0},{2,3},{3,2},{4,5},{5,4},{6,7},{7,6},{8,9},{9,8},{10,11... | collective-permute-start | bytes 1966088 | tf_op jit(solution)/shard_map/ppermute | solution.py:19
  29.5 11.4 %collective-permute-start.4 = (bf16[256,2048]{1,0:T(8,128)(2,1)}, bf16[256,2048]{1,0:T(8,128)(2,1)S(1)}, u32[]{:S(2)}, u32[]{:S(2)}) collective-permute-start(bf16[256,2048]{1,0:T(8,128)(2,1)} %collective-permute-done.3), channel_id=1, source_target_pairs={{0,4},{4,0},{8,12},{12,8},{1,5},{5,1},{9,13},{13,9},{2,6},{6,2},{1... | collective-permute-start | bytes 3145736 | tf_op jit(solution)/shard_map/ppermute | solution.py:19
  29.7 4.4 %collective-permute-start.5 = (f32[2,256]{1,0:T(2,128)S(1)}, f32[2,256]{1,0:T(2,128)S(1)}, u32[]{:S(2)}, u32[]{:S(2)}) collective-permute-start(f32[2,256]{1,0:T(2,128)S(1)} %pad_maximum_fusion.5), channel_id=1, source_target_pairs={{0,1},{1,0},{2,3},{3,2},{4,5},{5,4},{6,7},{7,6},{8,9},{9,8},{10,11... | collective-permute-start | bytes 6152 | tf_op jit(solution)/shard_map/ppermute | solution.py:19
  31.5 17.8 %collective-permute-start.10 = (bf16[2,1,64,1280]{3,2,1,0:T(8,128)(2,1)S(1)}, bf16[2,1,64,1280]{3,2,1,0:T(8,128)(2,1)S(1)}, u32[]{:S(2)}, u32[]{:S(2)}) collective-permute-start(bf16[2,1,64,1280]{3,2,1,0:T(8,128)(2,1)S(1)} %get-tuple-element.208), channel_id=1, source_target_pairs={{0,2},{1,3},{2,0},{3,1},{4,6},{5,7},{6,4},{7,5},{8,10},{9,11},{10,... | collective-permute-start | bytes 983048 | tf_op jit(solution)/shard_map/ppermute | solution.py:19
  34.1 15.2 %collective-permute-start.9 = (f32[2,256]{1,0:T(2,128)S(1)}, f32[2,256]{1,0:T(2,128)S(1)}, u32[]{:S(2)}, u32[]{:S(2)}) collective-permute-start(f32[2,256]{1,0:T(2,128)S(1)} %add.259), channel_id=1, source_target_pairs={{0,2},{1,3},{2,0},{3,1},{4,6},{5,7},{6,4},{7,5},{8,10},{9,11},{10,... | collective-permute-start | bytes 6152 | tf_op jit(solution)/shard_map/ppermute | solution.py:19
  36.2 24.7 %collective-permute-start.8 = (bf16[2,2,64,1280]{3,2,1,0:T(8,128)(2,1)S(1)}, bf16[2,2,64,1280]{3,2,1,0:T(8,128)(2,1)S(1)}, u32[]{:S(2)}, u32[]{:S(2)}) collective-permute-start(bf16[2,2,64,1280]{3,2,1,0:T(8,128)(2,1)S(1)} %convolution_convert_fusion.2), channel_id=1, source_target_pairs={{0,1},{1,0},{2,3},{3,2},{4,5},{5,4},{6,7},{7,6},{8,9},{9,8},{10,11... | collective-permute-start | bytes 1966088 | tf_op jit(solution)/shard_map/ppermute | solution.py:19
  37.8 24.0 %collective-permute-start.7 = (bf16[256,2048]{1,0:T(8,128)(2,1)S(1)}, bf16[256,2048]{1,0:T(8,128)(2,1)}, u32[]{:S(2)}, u32[]{:S(2)}) collective-permute-start(bf16[256,2048]{1,0:T(8,128)(2,1)S(1)} %bitcast.307), channel_id=1, source_target_pairs={{0,8},{4,12},{8,0},{12,4},{1,9},{5,13},{9,1},{13,5},{2,10},{6,14},... | collective-permute-start | bytes 3145736 | tf_op jit(solution)/shard_map/ppermute | solution.py:19
  44.7 28.3 %collective-permute-start.6 = (bf16[2,2,64,1280]{3,2,1,0:T(8,128)(2,1)S(1)}, bf16[2,2,64,1280]{3,2,1,0:T(8,128)(2,1)S(1)}, u32[]{:S(2)}, u32[]{:S(2)}) collective-permute-start(bf16[2,2,64,1280]{3,2,1,0:T(8,128)(2,1)S(1)} %convolution_convert_fusion.1), channel_id=1, source_target_pairs={{0,1},{1,0},{2,3},{3,2},{4,5},{5,4},{6,7},{7,6},{8,9},{9,8},{10,11... | collective-permute-start | bytes 1966088 | tf_op jit(solution)/shard_map/ppermute | solution.py:19
  49.2 57.0 %copy-start.3 = (bf16[2,1,64,1280]{3,2,1,0:T(8,128)(2,1)}, bf16[2,1,64,1280]{3,2,1,0:T(8,128)(2,1)S(1)}, u32[]{:S(2)}) copy-start(bf16[2,1,64,1280]{3,2,1,0:T(8,128)(2,1)S(1)} %collective-permute-done.10) | copy-start | bytes 983044
  61.8 17.0 %collective-permute-start.13 = (bf16[256,2048]{1,0:T(8,128)(2,1)}, bf16[256,2048]{1,0:T(8,128)(2,1)}, u32[]{:S(2)}, u32[]{:S(2)}) collective-permute-start(bf16[256,2048]{1,0:T(8,128)(2,1)} %collective-permute-done.7), channel_id=1, source_target_pairs={{0,4},{4,0},{8,12},{12,8},{1,5},{5,1},{9,13},{13,9},{2,6},{6,2},{1... | collective-permute-start | bytes 3145736 | tf_op jit(solution)/shard_map/ppermute | solution.py:19
  61.9 11.9 %collective-permute-start.15 = (f32[2,256]{1,0:T(2,128)S(1)}, f32[2,256]{1,0:T(2,128)S(1)}, u32[]{:S(2)}, u32[]{:S(2)}) collective-permute-start(f32[2,256]{1,0:T(2,128)S(1)} %add.260), channel_id=1, source_target_pairs={{0,8},{4,12},{8,0},{12,4},{1,9},{5,13},{9,1},{13,5},{2,10},{6,14},... | collective-permute-start | bytes 6152 | tf_op jit(solution)/shard_map/ppermute | solution.py:19
  73.8 4.6 %collective-permute-start.14 = (f32[2,256]{1,0:T(2,128)S(1)}, f32[2,256]{1,0:T(2,128)S(1)}, u32[]{:S(2)}, u32[]{:S(2)}) collective-permute-start(f32[2,256]{1,0:T(2,128)S(1)} %add.260), channel_id=1, source_target_pairs={{0,4},{4,0},{8,12},{12,8},{1,5},{5,1},{9,13},{13,9},{2,6},{6,2},{1... | collective-permute-start | bytes 6152 | tf_op jit(solution)/shard_map/ppermute | solution.py:19
  73.8 4.7 %collective-permute-start.16 = (f32[2,256]{1,0:T(2,128)S(1)}, f32[2,256]{1,0:T(2,128)S(1)}, u32[]{:S(2)}, u32[]{:S(2)}) collective-permute-start(f32[2,256]{1,0:T(2,128)S(1)} %collective-permute-done.15), channel_id=1, source_target_pairs={{0,4},{4,0},{8,12},{12,8},{1,5},{5,1},{9,13},{13,9},{2,6},{6,2},{1... | collective-permute-start | bytes 6152 | tf_op jit(solution)/shard_map/ppermute | solution.py:19
  75.4 23.9 %collective-permute-start.12 = (bf16[2,1,64,1280]{3,2,1,0:T(8,128)(2,1)}, bf16[2,1,64,1280]{3,2,1,0:T(8,128)(2,1)S(1)}, u32[]{:S(2)}, u32[]{:S(2)}) collective-permute-start(bf16[2,1,64,1280]{3,2,1,0:T(8,128)(2,1)} %get-tuple-element.205), channel_id=1, source_target_pairs={{0,2},{1,3},{2,0},{3,1},{4,6},{5,7},{6,4},{7,5},{8,10},{9,11},{10,... | collective-permute-start | bytes 983048 | tf_op jit(solution)/shard_map/ppermute | solution.py:19
  75.5 30.8 %collective-permute-start.11 = (bf16[2,1,64,1280]{3,2,1,0:T(8,128)(2,1)}, bf16[2,1,64,1280]{3,2,1,0:T(8,128)(2,1)S(1)}, u32[]{:S(2)}, u32[]{:S(2)}) collective-permute-start(bf16[2,1,64,1280]{3,2,1,0:T(8,128)(2,1)} %get-tuple-element.206), channel_id=1, source_target_pairs={{0,2},{1,3},{2,0},{3,1},{4,6},{5,7},{6,4},{7,5},{8,10},{9,11},{10,... | collective-permute-start | bytes 983048 | tf_op jit(solution)/shard_map/ppermute | solution.py:19
  78.8 6.2 %copy-start.18 = (bf16[1,2048,1024]{2,1,0:T(8,128)(2,1)S(1)}, bf16[1,2048,1024]{2,1,0:T(8,128)(2,1)}, u32[]{:S(2)}) copy-start(bf16[1,2048,1024]{2,1,0:T(8,128)(2,1)} %param.21) | copy-start | bytes 12582916
  78.8 6.2 %copy-start.22 = (bf16[1,2048,128]{2,1,0:T(8,128)(2,1)S(1)}, bf16[1,2048,128]{2,1,0:T(8,128)(2,1)}, u32[]{:S(2)}) copy-start(bf16[1,2048,128]{2,1,0:T(8,128)(2,1)} %param.23) | copy-start | bytes 1572868
  78.8 6.2 %copy-start.24 = (bf16[1,2048,128]{2,1,0:T(8,128)(2,1)S(1)}, bf16[1,2048,128]{2,1,0:T(8,128)(2,1)}, u32[]{:S(2)}) copy-start(bf16[1,2048,128]{2,1,0:T(8,128)(2,1)} %param.22) | copy-start | bytes 1572868
  83.6 37.1 %collective-permute-start.20 = (bf16[2,2,64,1280]{3,2,1,0:T(8,128)(2,1)S(1)}, bf16[2,2,64,1280]{3,2,1,0:T(8,128)(2,1)S(1)}, u32[]{:S(2)}, u32[]{:S(2)}) collective-permute-start(bf16[2,2,64,1280]{3,2,1,0:T(8,128)(2,1)S(1)} %convolution_convert_fusion), channel_id=1, source_target_pairs={{0,1},{1,0},{2,3},{3,2},{4,5},{5,4},{6,7},{7,6},{8,9},{9,8},{10,11... | collective-permute-start | bytes 1966088 | tf_op jit(solution)/shard_map/ppermute | solution.py:19
  86.6 35.5 %copy-start.7 = (f32[256,1]{1,0:T(8,128)S(1)}, f32[256,1]{1,0:T(8,128)}, u32[]{:S(2)}) copy-start(f32[256,1]{1,0:T(8,128)} %convert_element_type.470.q_pos) | copy-start | bytes 3076
  99.3 11.6 %copy-start = (bf16[2,1,64,1280]{3,2,1,0:T(8,128)(2,1)}, bf16[2,1,64,1280]{3,2,1,0:T(8,128)(2,1)S(1)}, u32[]{:S(2)}) copy-start(bf16[2,1,64,1280]{3,2,1,0:T(8,128)(2,1)S(1)} %collective-permute-done.12) | copy-start | bytes 983044
  106.3 15.9 %copy-start.5 = (bf16[2,1,64,1280]{3,2,1,0:T(8,128)(2,1)}, bf16[2,1,64,1280]{3,2,1,0:T(8,128)(2,1)S(1)}, u32[]{:S(2)}) copy-start(bf16[2,1,64,1280]{3,2,1,0:T(8,128)(2,1)S(1)} %collective-permute-done.11) | copy-start | bytes 983044
  106.5 15.7 %collective-permute-start.17 = (bf16[256,256]{1,0:T(8,128)(2,1)S(1)}, bf16[256,256]{1,0:T(8,128)(2,1)S(1)}, u32[]{:S(2)}, u32[]{:S(2)}) collective-permute-start(bf16[256,256]{1,0:T(8,128)(2,1)S(1)} %shard_map.140.rest_0_), channel_id=1, source_target_pairs={{0,1},{1,0},{2,3},{3,2},{4,5},{5,4},{6,7},{7,6},{8,9},{9,8},{10,11... | collective-permute-start | bytes 393224 | tf_op jit(solution)/shard_map/ppermute | solution.py:23
  106.5 15.6 %collective-permute-start.18 = (bf16[256,256]{1,0:T(8,128)(2,1)S(1)}, bf16[256,256]{1,0:T(8,128)(2,1)S(1)}, u32[]{:S(2)}, u32[]{:S(2)}) collective-permute-start(bf16[256,256]{1,0:T(8,128)(2,1)S(1)} %shard_map.140.rest_0_), channel_id=1, source_target_pairs={{0,2},{1,3},{2,0},{3,1},{4,6},{5,7},{6,4},{7,5},{8,10},{9,11},{10,... | collective-permute-start | bytes 393224 | tf_op jit(solution)/shard_map/ppermute | solution.py:23
  108.5 13.6 %collective-permute-start.19 = (bf16[256,256]{1,0:T(8,128)(2,1)S(1)}, bf16[256,256]{1,0:T(8,128)(2,1)S(1)}, u32[]{:S(2)}, u32[]{:S(2)}) collective-permute-start(bf16[256,256]{1,0:T(8,128)(2,1)S(1)} %shard_map.140.rest_0_), channel_id=1, source_target_pairs={{0,3},{1,2},{2,1},{3,0},{4,7},{5,6},{6,5},{7,4},{8,11},{9,10},{10,... | collective-permute-start | bytes 393224 | tf_op jit(solution)/shard_map/ppermute | solution.py:23
  128.5 39.6 %collective-permute-start.22 = (bf16[256,1024]{1,0:T(8,128)(2,1)S(1)}, bf16[256,1024]{1,0:T(8,128)(2,1)}, u32[]{:S(2)}, u32[]{:S(2)}) collective-permute-start(bf16[256,1024]{1,0:T(8,128)(2,1)S(1)} %shard_map.141), channel_id=1, source_target_pairs={{0,2},{1,3},{2,0},{3,1},{4,6},{5,7},{6,4},{7,5},{8,10},{9,11},{10,... | collective-permute-start | bytes 1572872 | tf_op jit(solution)/shard_map/ppermute | solution.py:19
  128.6 39.6 %collective-permute-start.21 = (bf16[256,1024]{1,0:T(8,128)(2,1)S(1)}, bf16[256,1024]{1,0:T(8,128)(2,1)}, u32[]{:S(2)}, u32[]{:S(2)}) collective-permute-start(bf16[256,1024]{1,0:T(8,128)(2,1)S(1)} %shard_map.141), channel_id=1, source_target_pairs={{0,1},{1,0},{2,3},{3,2},{4,5},{5,4},{6,7},{7,6},{8,9},{9,8},{10,11... | collective-permute-start | bytes 1572872 | tf_op jit(solution)/shard_map/ppermute | solution.py:19
  128.8 38.2 %collective-permute-start.23 = (bf16[2,1,64,1280]{3,2,1,0:T(8,128)(2,1)}, bf16[2,1,64,1280]{3,2,1,0:T(8,128)(2,1)S(1)}, u32[]{:S(2)}, u32[]{:S(2)}) collective-permute-start(bf16[2,1,64,1280]{3,2,1,0:T(8,128)(2,1)} %get-tuple-element.203), channel_id=1, source_target_pairs={{0,2},{1,3},{2,0},{3,1},{4,6},{5,7},{6,4},{7,5},{8,10},{9,11},{10,... | collective-permute-start | bytes 983048 | tf_op jit(solution)/shard_map/ppermute | solution.py:19
  172.6 9.1 %collective-permute-start.24 = (bf16[2,128,2048]{2,1,0:T(8,128)(2,1)}, bf16[2,128,2048]{2,1,0:T(8,128)(2,1)}, u32[]{:S(2)}, u32[]{:S(2)}) collective-permute-start(bf16[2,128,2048]{2,1,0:T(8,128)(2,1)} %fusion.28), channel_id=1, source_target_pairs={{0,4},{4,0},{8,12},{12,8},{1,5},{5,1},{9,13},{13,9},{2,6},{6,2},{1... | collective-permute-start | bytes 3145736 | tf_op jit(solution)/shard_map/ppermute | solution.py:19
  173.6 11.2 %collective-permute-start.26 = (bf16[256,256]{1,0:T(8,128)(2,1)S(1)}, bf16[256,256]{1,0:T(8,128)(2,1)S(1)}, u32[]{:S(2)}, u32[]{:S(2)}) collective-permute-start(bf16[256,256]{1,0:T(8,128)(2,1)S(1)} %shard_map.142.rest_0_), channel_id=1, source_target_pairs={{0,1},{1,0},{2,3},{3,2},{4,5},{5,4},{6,7},{7,6},{8,9},{9,8},{10,11... | collective-permute-start | bytes 393224 | tf_op jit(solution)/shard_map/ppermute | solution.py:23
  173.7 13.0 %collective-permute-start.27 = (bf16[256,256]{1,0:T(8,128)(2,1)S(1)}, bf16[256,256]{1,0:T(8,128)(2,1)S(1)}, u32[]{:S(2)}, u32[]{:S(2)}) collective-permute-start(bf16[256,256]{1,0:T(8,128)(2,1)S(1)} %shard_map.142.rest_0_), channel_id=1, source_target_pairs={{0,2},{1,3},{2,0},{3,1},{4,6},{5,7},{6,4},{7,5},{8,10},{9,11},{10,... | collective-permute-start | bytes 393224 | tf_op jit(solution)/shard_map/ppermute | solution.py:23
  174.6 12.1 %collective-permute-start.28 = (bf16[256,256]{1,0:T(8,128)(2,1)S(1)}, bf16[256,256]{1,0:T(8,128)(2,1)S(1)}, u32[]{:S(2)}, u32[]{:S(2)}) collective-permute-start(bf16[256,256]{1,0:T(8,128)(2,1)S(1)} %shard_map.142.rest_0_), channel_id=1, source_target_pairs={{0,3},{1,2},{2,1},{3,0},{4,7},{5,6},{6,5},{7,4},{8,11},{9,10},{10,... | collective-permute-start | bytes 393224 | tf_op jit(solution)/shard_map/ppermute | solution.py:23
  178.1 32.0 %collective-permute-start.30 = (bf16[256,1024]{1,0:T(8,128)(2,1)}, bf16[256,1024]{1,0:T(8,128)(2,1)S(1)}, u32[]{:S(2)}, u32[]{:S(2)}) collective-permute-start(bf16[256,1024]{1,0:T(8,128)(2,1)} %collective-permute-done.22), channel_id=1, source_target_pairs={{0,1},{1,0},{2,3},{3,2},{4,5},{5,4},{6,7},{7,6},{8,9},{9,8},{10,11... | collective-permute-start | bytes 1572872 | tf_op jit(solution)/shard_map/ppermute | solution.py:19
  181.6 5.1 %copy-start.2 = (bf16[2,1,64,1280]{3,2,1,0:T(8,128)(2,1)S(1)}, bf16[2,1,64,1280]{3,2,1,0:T(8,128)(2,1)}, u32[]{:S(2)}) copy-start(bf16[2,1,64,1280]{3,2,1,0:T(8,128)(2,1)} %copy-done) | copy-start | bytes 983044
  181.6 5.1 %copy-start.8 = (f32[256,1]{1,0:T(8,128)S(1)}, f32[256,1]{1,0:T(8,128)}, u32[]{:S(2)}) copy-start(f32[256,1]{1,0:T(8,128)} %convert_element_type.470.q_pos) | copy-start | bytes 3076
  183.3 21.2 %collective-permute-start.25 = (bf16[1,128,2048]{2,1,0:T(8,128)(2,1)S(1)}, bf16[1,128,2048]{2,1,0:T(8,128)(2,1)S(1)}, u32[]{:S(2)}, u32[]{:S(2)}) collective-permute-start(bf16[1,128,2048]{2,1,0:T(8,128)(2,1)S(1)} %fusion.91), channel_id=1, source_target_pairs={{0,8},{4,12},{8,0},{12,4},{1,9},{5,13},{9,1},{13,5},{2,10},{6,14},... | collective-permute-start | bytes 1572872 | tf_op jit(solution)/shard_map/ppermute | solution.py:19
  201.4 5.0 %copy-start.11 = (bf16[1,1024,2048]{2,1,0:T(8,128)(2,1)S(1)}, bf16[1,1024,2048]{2,1,0:T(8,128)(2,1)}, u32[]{:S(2)}) copy-start(bf16[1,1024,2048]{2,1,0:T(8,128)(2,1)} %param.18) | copy-start | bytes 12582916
  201.4 34.4 %collective-permute-start.40 = (bf16[256,1024]{1,0:T(8,128)(2,1)S(1)}, bf16[256,1024]{1,0:T(8,128)(2,1)S(1)}, u32[]{:S(2)}, u32[]{:S(2)}) collective-permute-start(bf16[256,1024]{1,0:T(8,128)(2,1)S(1)} %shard_map.143), channel_id=1, source_target_pairs={{0,1},{1,0},{2,3},{3,2},{4,5},{5,4},{6,7},{7,6},{8,9},{9,8},{10,11... | collective-permute-start | bytes 1572872 | tf_op jit(solution)/shard_map/ppermute | solution.py:19
  204.4 34.2 %collective-permute-start.39 = (bf16[256,1024]{1,0:T(8,128)(2,1)S(1)}, bf16[256,1024]{1,0:T(8,128)(2,1)S(1)}, u32[]{:S(2)}, u32[]{:S(2)}) collective-permute-start(bf16[256,1024]{1,0:T(8,128)(2,1)S(1)} %shard_map.143), channel_id=1, source_target_pairs={{0,2},{1,3},{2,0},{3,1},{4,6},{5,7},{6,4},{7,5},{8,10},{9,11},{10,... | collective-permute-start | bytes 1572872 | tf_op jit(solution)/shard_map/ppermute | solution.py:19
  204.7 22.4 %collective-permute-start.29 = (bf16[2,64,2048]{2,1,0:T(8,128)(2,1)S(1)}, bf16[2,64,2048]{2,1,0:T(8,128)(2,1)S(1)}, u32[]{:S(2)}, u32[]{:S(2)}) collective-permute-start(bf16[2,64,2048]{2,1,0:T(8,128)(2,1)S(1)} %add_convert_fusion), channel_id=1, source_target_pairs={{0,16},{16,0},{1,17},{17,1},{2,18},{18,2},{3,19},{19,3},{4,20},{20... | collective-permute-start | bytes 1572872 | tf_op jit(solution)/shard_map/ppermute | solution.py:28
  208.0 2.0 collective-permute-start.31
  210.9 8.6 %collective-permute-start.34 = (bf16[1,64,2048]{2,1,0:T(8,128)(2,1)S(1)}, bf16[1,64,2048]{2,1,0:T(8,128)(2,1)S(1)}, u32[]{:S(2)}, u32[]{:S(2)}) collective-permute-start(bf16[1,64,2048]{2,1,0:T(8,128)(2,1)S(1)} %fusion.92), channel_id=1, source_target_pairs={{0,8},{4,12},{8,0},{12,4},{1,9},{5,13},{9,1},{13,5},{2,10},{6,14},... | collective-permute-start | bytes 786440 | tf_op jit(solution)/shard_map/ppermute | solution.py:19
  212.5 1.9 collective-permute-start.32
  215.4 6.1 %copy-start.13 = (bf16[1,256,2048]{2,1,0:T(8,128)(2,1)S(1)}, bf16[1,256,2048]{2,1,0:T(8,128)(2,1)}, u32[]{:S(2)}) copy-start(bf16[1,256,2048]{2,1,0:T(8,128)(2,1)} %param.13) | copy-start | bytes 3145732
  215.4 2.0 collective-permute-start.35
  217.4 9.1 %collective-permute-start.33 = (bf16[1,64,2048]{2,1,0:T(8,128)(2,1)S(1)}, bf16[1,64,2048]{2,1,0:T(8,128)(2,1)S(1)}, u32[]{:S(2)}, u32[]{:S(2)}) collective-permute-start(bf16[1,64,2048]{2,1,0:T(8,128)(2,1)S(1)} %fusion.93), channel_id=1, source_target_pairs={{0,8},{4,12},{8,0},{12,4},{1,9},{5,13},{9,1},{13,5},{2,10},{6,14},... | collective-permute-start | bytes 786440 | tf_op jit(solution)/shard_map/ppermute | solution.py:19
  219.5 24.5 %collective-permute-start.38 = (bf16[1,64,2048]{2,1,0:T(8,128)(2,1)S(1)}, bf16[1,64,2048]{2,1,0:T(8,128)(2,1)S(1)}, u32[]{:S(2)}, u32[]{:S(2)}) collective-permute-start(bf16[1,64,2048]{2,1,0:T(8,128)(2,1)S(1)} %fusion.94), channel_id=1, source_target_pairs={{0,8},{4,12},{8,0},{12,4},{1,9},{5,13},{9,1},{13,5},{2,10},{6,14},... | collective-permute-start | bytes 786440 | tf_op jit(solution)/shard_map/ppermute | solution.py:19
  226.5 9.2 %collective-permute-start.36 = (bf16[1,64,2048]{2,1,0:T(8,128)(2,1)S(1)}, bf16[1,64,2048]{2,1,0:T(8,128)(2,1)S(1)}, u32[]{:S(2)}, u32[]{:S(2)}) collective-permute-start(bf16[1,64,2048]{2,1,0:T(8,128)(2,1)S(1)} %add_convert_fusion.10), channel_id=1, source_target_pairs={{0,16},{16,0},{1,17},{17,1},{2,18},{18,2},{3,19},{19,3},{4,20},{20... | collective-permute-start | bytes 786440 | tf_op jit(solution)/shard_map/ppermute | solution.py:28
  227.1 17.0 %collective-permute-start.37 = (bf16[1,64,2048]{2,1,0:T(8,128)(2,1)S(1)}, bf16[1,64,2048]{2,1,0:T(8,128)(2,1)S(1)}, u32[]{:S(2)}, u32[]{:S(2)}) collective-permute-start(bf16[1,64,2048]{2,1,0:T(8,128)(2,1)S(1)} %add_convert_fusion.9), channel_id=1, source_target_pairs={{0,16},{16,0},{1,17},{17,1},{2,18},{18,2},{3,19},{19,3},{4,20},{20... | collective-permute-start | bytes 786440 | tf_op jit(solution)/shard_map/ppermute | solution.py:28
  236.5 2.0 collective-permute-start.41
  239.4 8.4 %collective-permute-start.45 = (bf16[1,64,2048]{2,1,0:T(8,128)(2,1)S(1)}, bf16[1,64,2048]{2,1,0:T(8,128)(2,1)S(1)}, u32[]{:S(2)}, u32[]{:S(2)}) collective-permute-start(bf16[1,64,2048]{2,1,0:T(8,128)(2,1)S(1)} %fusion.95), channel_id=1, source_target_pairs={{0,8},{4,12},{8,0},{12,4},{1,9},{5,13},{9,1},{13,5},{2,10},{6,14},... | collective-permute-start | bytes 786440 | tf_op jit(solution)/shard_map/ppermute | solution.py:19
  240.0 13.9 %collective-permute-start.44 = (bf16[256,1024]{1,0:T(8,128)(2,1)S(1)}, bf16[256,1024]{1,0:T(8,128)(2,1)S(1)}, u32[]{:S(2)}, u32[]{:S(2)}) collective-permute-start(bf16[256,1024]{1,0:T(8,128)(2,1)S(1)} %collective-permute-done.39), channel_id=1, source_target_pairs={{0,1},{1,0},{2,3},{3,2},{4,5},{5,4},{6,7},{7,6},{8,9},{9,8},{10,11... | collective-permute-start | bytes 1572872 | tf_op jit(solution)/shard_map/ppermute | solution.py:19
  241.9 1.9 collective-permute-start.42
  254.6 9.3 %collective-permute-start.43 = (bf16[1,64,2048]{2,1,0:T(8,128)(2,1)S(1)}, bf16[1,64,2048]{2,1,0:T(8,128)(2,1)S(1)}, u32[]{:S(2)}, u32[]{:S(2)}) collective-permute-start(bf16[1,64,2048]{2,1,0:T(8,128)(2,1)S(1)} %add_convert_fusion.8), channel_id=1, source_target_pairs={{0,16},{16,0},{1,17},{17,1},{2,18},{18,2},{3,19},{19,3},{4,20},{20... | collective-permute-start | bytes 786440 | tf_op jit(solution)/shard_map/ppermute | solution.py:28
  255.2 8.7 %collective-permute-start.48 = (bf16[1,64,2048]{2,1,0:T(8,128)(2,1)S(1)}, bf16[1,64,2048]{2,1,0:T(8,128)(2,1)S(1)}, u32[]{:S(2)}, u32[]{:S(2)}) collective-permute-start(bf16[1,64,2048]{2,1,0:T(8,128)(2,1)S(1)} %fusion.96), channel_id=1, source_target_pairs={{0,8},{4,12},{8,0},{12,4},{1,9},{5,13},{9,1},{13,5},{2,10},{6,14},... | collective-permute-start | bytes 786440 | tf_op jit(solution)/shard_map/ppermute | solution.py:19
  256.7 12.8 %collective-permute-start.47 = (bf16[1,64,2048]{2,1,0:T(8,128)(2,1)S(1)}, bf16[1,64,2048]{2,1,0:T(8,128)(2,1)S(1)}, u32[]{:S(2)}, u32[]{:S(2)}) collective-permute-start(bf16[1,64,2048]{2,1,0:T(8,128)(2,1)S(1)} %add_convert_fusion.7), channel_id=1, source_target_pairs={{0,16},{16,0},{1,17},{17,1},{2,18},{18,2},{3,19},{19,3},{4,20},{20... | collective-permute-start | bytes 786440 | tf_op jit(solution)/shard_map/ppermute | solution.py:28
  258.3 1.9 collective-permute-start.46
  260.4 9.2 %collective-permute-start.50 = (bf16[1,64,2048]{2,1,0:T(8,128)(2,1)S(1)}, bf16[1,64,2048]{2,1,0:T(8,128)(2,1)S(1)}, u32[]{:S(2)}, u32[]{:S(2)}) collective-permute-start(bf16[1,64,2048]{2,1,0:T(8,128)(2,1)S(1)} %fusion.97), channel_id=1, source_target_pairs={{0,8},{4,12},{8,0},{12,4},{1,9},{5,13},{9,1},{13,5},{2,10},{6,14},... | collective-permute-start | bytes 786440 | tf_op jit(solution)/shard_map/ppermute | solution.py:19
  264.0 11.1 %collective-permute-start.49 = (bf16[1,64,2048]{2,1,0:T(8,128)(2,1)S(1)}, bf16[1,64,2048]{2,1,0:T(8,128)(2,1)S(1)}, u32[]{:S(2)}, u32[]{:S(2)}) collective-permute-start(bf16[1,64,2048]{2,1,0:T(8,128)(2,1)S(1)} %add_convert_fusion.6), channel_id=1, source_target_pairs={{0,16},{16,0},{1,17},{17,1},{2,18},{18,2},{3,19},{19,3},{4,20},{20... | collective-permute-start | bytes 786440 | tf_op jit(solution)/shard_map/ppermute | solution.py:28
  269.7 9.2 %collective-permute-start.51 = (bf16[1,64,2048]{2,1,0:T(8,128)(2,1)S(1)}, bf16[1,64,2048]{2,1,0:T(8,128)(2,1)S(1)}, u32[]{:S(2)}, u32[]{:S(2)}) collective-permute-start(bf16[1,64,2048]{2,1,0:T(8,128)(2,1)S(1)} %add_convert_fusion.5), channel_id=1, source_target_pairs={{0,16},{16,0},{1,17},{17,1},{2,18},{18,2},{3,19},{19,3},{4,20},{20... | collective-permute-start | bytes 786440 | tf_op jit(solution)/shard_map/ppermute | solution.py:28
  (15 other events, 55.1 us)
where the time goes:
time: 286 us; the launch traced here: 281 us
  waiting for transfers between devices  148 us (52%)
  starting transfers between devices  53.1 us (19%)
  matrix products  35 us (12%)
  Pallas kernels  19.5 us (7%)
  other arithmetic  15.3 us (5%)
  local copies, waits for them, and re-layouts  8.16 us (3%)
    ppermute x39, waiting for transfers between devices, swapped(): lax.ppermute(value, axis, [(i, i ^ 1 << bit) for i in range(lax.axis_size...  123 us
    ppermute x39, starting transfers between devices, swapped(): lax.ppermute(value, axis, [(i, i ^ 1 << bit) for i in range(lax.axis_size...  37.2 us
    ppermute x7, waiting for transfers between devices, from_behind(): lax.ppermute(value, axis, [(i, (i + steps) % count) for i in range(count)])  22.4 us
    dot_general x8, matrix products, project(): out = jnp.dot(rows, self.w, preferred_element_type=F32)  19.7 us
    pallas_call x2, Pallas kernels, attend(): whole(functools.partial(attention_kernel, qw, kvw, n_col), jax.ShapeDtype...  19.1 us
    dot_general x14, matrix products, dot(): out = jnp.dot(value.reshape(-1, qw), c.wo, preferred_element_type=F32)  15.3 us
    ppermute x6, starting transfers between devices, crossed(): lax.ppermute(value, axis, [(i, i ^ bits) for i in range(lax.axis_size(axi...  8.89 us
    ppermute x7, starting transfers between devices, from_behind(): lax.ppermute(value, axis, [(i, (i + steps) % count) for i in range(count)])  6.96 us
  transfers between devices with their start and end apart: 52, of which 25 were waited for; matrix products, arithmetic and copies ran while one was open for 17% of the time, Pallas kernels for 5%

commit v1 on v0

--- a/solution.py
+++ b/solution.py
@@ -381,13 +381,13 @@
     d_m = out_third(d, *d_m, of_d[1], 1)
     d_q = out_third(d, *d_q, of_d[2], 1)
     d_p = landed(d_p)
-    d_m = landed(d_m)
     u_p = first(u, u_got, of_u[1])
     u_p = out_second(*u_p)
     far_pieces(u_got)
     u_m = first(u, u_got, of_u[2])
     u_m = out_second(*u_m)
     u_o = out_third(u, *u_o, of_u[0], -1)
+    d_m = landed(d_m)
     d_q = landed(d_q)
     u_p = out_third(u, *u_p, of_u[1], -1)
     u_q = first(u, u_got, of_u[3])

time: 286 us -> 282 us (0.986)
  waiting for transfers between devices: 148 us -> 143 us
    ppermute x7, waiting for transfers between devices: 22.4 us -> 17 us  [from_behind(): lax.ppermute(value, axis, [(i, (i + steps) % count) for i in range(count)])]
  transfers between devices with their start and end apart: 52 -> 52, of which waited for: 25 -> 27; matrix products, arithmetic and copies ran while one was open for 17% -> 18% of each run, Pallas kernels for 5% -> 5%
where the time goes in v1:
time: 282 us; the launch traced here: 277 us
  waiting for transfers between devices  143 us (51%)
  starting transfers between devices  54.2 us (19%)
  matrix products  35 us (12%)
  Pallas kernels  19.5 us (7%)
  other arithmetic  15.3 us (5%)
  local copies, waits for them, and re-layouts  8.16 us (3%)
    ppermute x39, waiting for transfers between devices, swapped(): lax.ppermute(value, axis, [(i, i ^ 1 << bit) for i in range(lax.axis_size...  123 us
    ppermute x39, starting transfers between devices, swapped(): lax.ppermute(value, axis, [(i, i ^ 1 << bit) for i in range(lax.axis_size...  36.4 us
    dot_general x8, matrix products, project(): out = jnp.dot(rows, self.w, preferred_element_type=F32)  19.7 us
    pallas_call x2, Pallas kernels, attend(): whole(functools.partial(attention_kernel, qw, kvw, n_col), jax.ShapeDtype...  19.1 us
    ppermute x7, waiting for transfers between devices, from_behind(): lax.ppermute(value, axis, [(i, (i + steps) % count) for i in range(count)])  17 us
    dot_general x14, matrix products, dot(): out = jnp.dot(value.reshape(-1, qw), c.wo, preferred_element_type=F32)  15.3 us
    ppermute x7, starting transfers between devices, from_behind(): lax.ppermute(value, axis, [(i, (i + steps) % count) for i in range(count)])  8.94 us
    ppermute x6, starting transfers between devices, crossed(): lax.ppermute(value, axis, [(i, i ^ bits) for i in range(lax.axis_size(axi...  8.89 us
  transfers between devices with their start and end apart: 52, of which 27 were waited for; matrix products, arithmetic and copies ran while one was open for 18% of the time, Pallas kernels for 5%

profile of v1, /device:TPU:0, one launch (start us, length us, event | category | flops | bytes accessed | tf_op | source)
XLA Modules:
  0.0 276.9 jit_solution(14969618984488897640)
XLA Ops:
  1.1 2.6 collective-permute-start.3
  4.4 1.1 fusion.80
  5.7 4.4 %convolution_convert_fusion.3 = bf16[2,2,64,1280]{3,2,1,0:T(8,128)(2,1)S(1)} fusion(s32[]{:T(128)S(6)} %select_n.81, bf16[1,2,2,64,2048]{4,3,2,1,0:T(8,128)(2,1)} %bitcast.298, bf16[1,2,2,64,2048]{4,3,2,1,0:T(8,128)(2,1)S(1)} %bitcast.319, f32[2048]{0:T(1024)} %bitcast.360, bf16[2048,128]{1,0:T(8,128)(2,1)} %bitcast.344, bf16[2048,128]{1,0:T(8,128)(2,1)} %bitcast.348, ...), kind=kOutput, calls=%fused_computation.34 | convolution fusion | flops 1360330752 | bytes 8003588 | tf_op jit(solution)/shard_map/dot_general | solution.py:133
  10.4 1.6 fusion.53
  11.9 2.2 collective-permute-start.1
  14.8 1.6 convolution_convert_fusion.2
  16.4 13.0 %collective-permute-done.1 = bf16[2,2,64,1280]{3,2,1,0:T(8,128)(2,1)S(1)} collective-permute-done((bf16[2,2,64,1280]{3,2,1,0:T(8,128)(2,1)S(1)}, bf16[2,2,64,1280]{3,2,1,0:T(8,128)(2,1)S(1)}, u32[]{:S(2)}, u32[]{:S(2)}) %collective-permute-start.1) | collective-permute-done | bytes 655392 | tf_op jit(solution)/shard_map/ppermute | solution.py:19
  29.7 1.8 collective-permute-start.5
  31.5 2.6 collective-permute-start.10
  34.1 2.0 collective-permute-start.9
  36.2 1.6 collective-permute-start.8
  37.8 1.5 collective-permute-start.7
  39.3 1.6 fusion.54
  40.9 2.6 convolution_convert_fusion.1
  43.6 1.1 fusion.70
  45.2 1.6 fusion.55
  46.8 2.5 collective-permute-done.10
  49.3 11.6 %collective-permute-done.8 = bf16[2,2,64,1280]{3,2,1,0:T(8,128)(2,1)S(1)} collective-permute-done((bf16[2,2,64,1280]{3,2,1,0:T(8,128)(2,1)S(1)}, bf16[2,2,64,1280]{3,2,1,0:T(8,128)(2,1)S(1)}, u32[]{:S(2)}, u32[]{:S(2)}) %collective-permute-start.8) | collective-permute-done | bytes 655392 | tf_op jit(solution)/shard_map/ppermute | solution.py:19
  61.9 1.5 collective-permute-start.15
  63.4 9.5 %collective-permute-done.6 = bf16[2,2,64,1280]{3,2,1,0:T(8,128)(2,1)S(1)} collective-permute-done((bf16[2,2,64,1280]{3,2,1,0:T(8,128)(2,1)S(1)}, bf16[2,2,64,1280]{3,2,1,0:T(8,128)(2,1)S(1)}, u32[]{:S(2)}, u32[]{:S(2)}) %collective-permute-start.6) | collective-permute-done | bytes 655392 | tf_op jit(solution)/shard_map/ppermute | solution.py:19
  75.5 2.9 %collective-permute-start.11 = (bf16[2,1,64,1280]{3,2,1,0:T(8,128)(2,1)}, bf16[2,1,64,1280]{3,2,1,0:T(8,128)(2,1)S(1)}, u32[]{:S(2)}, u32[]{:S(2)}) collective-permute-start(bf16[2,1,64,1280]{3,2,1,0:T(8,128)(2,1)} %get-tuple-element.206), channel_id=1, source_target_pairs={{0,2},{1,3},{2,0},{3,1},{4,6},{5,7},{6,4},{7,5},{8,10},{9,11},{10,... | collective-permute-start | bytes 983048 | tf_op jit(solution)/shard_map/ppermute | solution.py:19
  78.8 4.8 %convolution_convert_fusion = bf16[2,2,64,1280]{3,2,1,0:T(8,128)(2,1)S(1)} fusion(s32[]{:T(128)S(6)} %select_n.81, bf16[1,2,2,64,2048]{4,3,2,1,0:T(8,128)(2,1)} %bitcast.35, bf16[1,2,2,64,2048]{4,3,2,1,0:T(8,128)(2,1)} %bitcast.36, f32[2048]{0:T(1024)S(1)} %bitcast.366, bf16[2048,128]{1,0:T(8,128)(2,1)} %bitcast.352, bf16[2048,128]{1,0:T(8,128)(2,1)} %bitcast.356, ...), kind=kOutput, calls=%fused_computation.31 | convolution fusion | flops 1360330752 | bytes 8003588 | tf_op jit(solution)/shard_map/dot_general | solution.py:133
  83.7 1.3 fusion.65
  85.0 1.6 fusion.56
  86.6 12.7 %collective-permute-done.12 = bf16[2,1,64,1280]{3,2,1,0:T(8,128)(2,1)S(1)} collective-permute-done((bf16[2,1,64,1280]{3,2,1,0:T(8,128)(2,1)}, bf16[2,1,64,1280]{3,2,1,0:T(8,128)(2,1)S(1)}, u32[]{:S(2)}, u32[]{:S(2)}) %collective-permute-start.12) | collective-permute-done | bytes 327712 | tf_op jit(solution)/shard_map/ppermute | solution.py:19
  99.3 6.9 %collective-permute-done.11 = bf16[2,1,64,1280]{3,2,1,0:T(8,128)(2,1)S(1)} collective-permute-done((bf16[2,1,64,1280]{3,2,1,0:T(8,128)(2,1)}, bf16[2,1,64,1280]{3,2,1,0:T(8,128)(2,1)S(1)}, u32[]{:S(2)}, u32[]{:S(2)}) %collective-permute-start.11) | collective-permute-done | bytes 327712 | tf_op jit(solution)/shard_map/ppermute | solution.py:19
  106.5 2.0 collective-permute-start.18
  108.5 2.4 collective-permute-start.19
  110.9 9.8 %collective-permute-done.20 = bf16[2,2,64,1280]{3,2,1,0:T(8,128)(2,1)S(1)} collective-permute-done((bf16[2,2,64,1280]{3,2,1,0:T(8,128)(2,1)S(1)}, bf16[2,2,64,1280]{3,2,1,0:T(8,128)(2,1)S(1)}, u32[]{:S(2)}, u32[]{:S(2)}) %collective-permute-start.20) | collective-permute-done | bytes 655392 | tf_op jit(solution)/shard_map/ppermute | solution.py:19
  124.1 4.5 %shard_map.141 = bf16[256,1024]{1,0:T(8,128)(2,1)S(1)} custom-call(f32[128,1280]{1,0:T(8,128)S(1)} %bitcast.279, f32[128,1280]{1,0:T(8,128)S(1)} %bitcast.283, bf16[128,1280]{1,0:T(8,128)(2,1)S(1)} %bitcast.290, bf16[128,1280]{1,0:T(8,128)(2,1)S(1)} %bitcast.294, f32[256,1]{1,0:T(8,128)S(1)} %squeeze.177.inverse, f32[256,128]{1,0:T(8,128)S(1)} %pad_maximum_fusion.3.cosine, ...), custom_call_target="tpu_custom_call" | custom-call | flops 1073741824 | bytes 2097152 | tf_op jit(solution)/shard_map/pallas_call | solution.py:288
  128.8 2.8 %collective-permute-start.23 = (bf16[2,1,64,1280]{3,2,1,0:T(8,128)(2,1)}, bf16[2,1,64,1280]{3,2,1,0:T(8,128)(2,1)S(1)}, u32[]{:S(2)}, u32[]{:S(2)}) collective-permute-start(bf16[2,1,64,1280]{3,2,1,0:T(8,128)(2,1)} %get-tuple-element.203), channel_id=1, source_target_pairs={{0,2},{1,3},{2,0},{3,1},{4,6},{5,7},{6,4},{7,5},{8,10},{9,11},{10,... | collective-permute-start | bytes 983048 | tf_op jit(solution)/shard_map/ppermute | solution.py:19
  131.7 35.3 %collective-permute-done.23 = bf16[2,1,64,1280]{3,2,1,0:T(8,128)(2,1)S(1)} collective-permute-done((bf16[2,1,64,1280]{3,2,1,0:T(8,128)(2,1)}, bf16[2,1,64,1280]{3,2,1,0:T(8,128)(2,1)S(1)}, u32[]{:S(2)}, u32[]{:S(2)}) %collective-permute-start.23) | collective-permute-done | bytes 327712 | tf_op jit(solution)/shard_map/ppermute | solution.py:19
  168.2 1.3 pad_maximum_fusion.2
  170.3 2.2 fusion.28
  174.6 3.5 %collective-permute-start.28 = (bf16[256,256]{1,0:T(8,128)(2,1)S(1)}, bf16[256,256]{1,0:T(8,128)(2,1)S(1)}, u32[]{:S(2)}, u32[]{:S(2)}) collective-permute-start(bf16[256,256]{1,0:T(8,128)(2,1)S(1)} %shard_map.142.rest_0_), channel_id=1, source_target_pairs={{0,3},{1,2},{2,1},{3,0},{4,7},{5,6},{6,5},{7,4},{8,11},{9,10},{10,... | collective-permute-start | bytes 393224 | tf_op jit(solution)/shard_map/ppermute | solution.py:23
  178.1 3.5 %fusion.24 = f32[2,128,2048]{2,1,0:T(8,128)S(1)} fusion(bf16[2,128,1024]{2,1,0:T(8,128)(2,1)S(1)} %bitcast.315, bf16[1,1024,2048]{2,1,0:T(8,128)(2,1)} %param.18), kind=kOutput, calls=%fused_computation.26 | convolution fusion | flops 1073741824 | bytes 6815744 | tf_op jit(solution)/shard_map/dot_general | solution.py:311
  181.6 1.6 add_bitcast_fusion
  183.3 1.6 collective-permute-start.25
  184.8 1.8 collective-permute-done.27.rest_2_
  186.7 14.6 %shard_map.143 = bf16[256,1024]{1,0:T(8,128)(2,1)S(1)} custom-call(f32[128,1280]{1,0:T(8,128)S(1)} %bitcast.277, f32[128,1280]{1,0:T(8,128)S(1)} %bitcast.281, bf16[128,1280]{1,0:T(8,128)(2,1)S(1)} %bitcast.288, bf16[128,1280]{1,0:T(8,128)(2,1)S(1)} %bitcast.292, f32[256,1]{1,0:T(8,128)S(1)} %squeeze.178.inverse, f32[256,128]{1,0:T(8,128)S(1)} %pad_maximum_fusion.3.cosine, ...), custom_call_target="tpu_custom_call" | custom-call | flops 1073741824 | bytes 2097152 | tf_op jit(solution)/shard_map/pallas_call | solution.py:288
  201.4 3.0 %collective-permute-start.39 = (bf16[256,1024]{1,0:T(8,128)(2,1)S(1)}, bf16[256,1024]{1,0:T(8,128)(2,1)S(1)}, u32[]{:S(2)}, u32[]{:S(2)}) collective-permute-start(bf16[256,1024]{1,0:T(8,128)(2,1)S(1)} %shard_map.143), channel_id=1, source_target_pairs={{0,1},{1,0},{2,3},{3,2},{4,5},{5,4},{6,7},{7,6},{8,9},{9,8},{10,11... | collective-permute-start | bytes 1572872 | tf_op jit(solution)/shard_map/ppermute | solution.py:19
  204.7 1.6 collective-permute-start.29
  206.3 1.7 fusion.31
  210.9 1.6 collective-permute-start.34
  213.3 1.1 collective-permute-done.32
  218.0 1.5 collective-permute-done.34
  219.6 6.1 %collective-permute-done.33 = bf16[1,64,2048]{2,1,0:T(8,128)(2,1)S(1)} collective-permute-done((bf16[1,64,2048]{2,1,0:T(8,128)(2,1)S(1)}, bf16[1,64,2048]{2,1,0:T(8,128)(2,1)S(1)}, u32[]{:S(2)}, u32[]{:S(2)}) %collective-permute-start.33) | collective-permute-done | bytes 262176 | tf_op jit(solution)/shard_map/ppermute | solution.py:19
  227.0 1.6 collective-permute-start.37
  228.6 1.5 collective-permute-start.36
  231.4 1.1 collective-permute-done.40
  234.8 1.1 collective-permute-done.41
  235.9 1.5 collective-permute-start.44
  237.8 3.5 %collective-permute-done.42 = bf16[1,64,2048]{2,1,0:T(8,128)(2,1)S(1)} collective-permute-done((bf16[1,64,2048]{2,1,0:T(8,128)(2,1)S(1)}, bf16[1,64,2048]{2,1,0:T(8,128)(2,1)S(1)}, u32[]{:S(2)}, u32[]{:S(2)}) %collective-permute-start.42) | collective-permute-done | bytes 262176 | tf_op jit(solution)/shard_map/ppermute | solution.py:28
  242.0 8.0 %collective-permute-done.44 = bf16[256,1024]{1,0:T(8,128)(2,1)S(1)} collective-permute-done((bf16[256,1024]{1,0:T(8,128)(2,1)S(1)}, bf16[256,1024]{1,0:T(8,128)(2,1)S(1)}, u32[]{:S(2)}, u32[]{:S(2)}) %collective-permute-start.44) | collective-permute-done | bytes 524320 | tf_op jit(solution)/shard_map/ppermute | solution.py:19
  250.7 1.6 collective-permute-start.43
  252.3 1.5 collective-permute-start.48
  257.0 3.0 %collective-permute-done.43 = bf16[1,64,2048]{2,1,0:T(8,128)(2,1)S(1)} collective-permute-done((bf16[1,64,2048]{2,1,0:T(8,128)(2,1)S(1)}, bf16[1,64,2048]{2,1,0:T(8,128)(2,1)S(1)}, u32[]{:S(2)}, u32[]{:S(2)}) %collective-permute-start.43) | collective-permute-done | bytes 262176 | tf_op jit(solution)/shard_map/ppermute | solution.py:28
  260.1 1.6 collective-permute-start.49
  261.7 3.9 %collective-permute-done.47 = bf16[1,64,2048]{2,1,0:T(8,128)(2,1)S(1)} collective-permute-done((bf16[1,64,2048]{2,1,0:T(8,128)(2,1)S(1)}, bf16[1,64,2048]{2,1,0:T(8,128)(2,1)S(1)}, u32[]{:S(2)}, u32[]{:S(2)}) %collective-permute-start.47) | collective-permute-done | bytes 262176 | tf_op jit(solution)/shard_map/ppermute | solution.py:28
  265.8 1.6 collective-permute-start.51
  267.4 1.2 reverse_select_fusion.2
  268.6 2.7 collective-permute-done.49
  271.2 3.9 %collective-permute-done.51 = bf16[1,64,2048]{2,1,0:T(8,128)(2,1)S(1)} collective-permute-done((bf16[1,64,2048]{2,1,0:T(8,128)(2,1)S(1)}, bf16[1,64,2048]{2,1,0:T(8,128)(2,1)S(1)}, u32[]{:S(2)}, u32[]{:S(2)}) %collective-permute-start.51) | collective-permute-done | bytes 262176 | tf_op jit(solution)/shard_map/ppermute | solution.py:28
  275.5 1.2 reverse_select_fusion
  (198 shorter events, 33.0 us)
Async XLA Ops:
  0.6 3.8 %collective-permute-start = (bf16[256,2048]{1,0:T(8,128)(2,1)}, bf16[256,2048]{1,0:T(8,128)(2,1)S(1)}, u32[]{:S(2)}, u32[]{:S(2)}) collective-permute-start(bf16[256,2048]{1,0:T(8,128)(2,1)} %bitcast.295), channel_id=1, source_target_pairs={{0,4},{4,0},{8,12},{12,8},{1,5},{5,1},{9,13},{13,9},{2,6},{6,2},{1... | collective-permute-start | bytes 3145736 | tf_op jit(solution)/shard_map/ppermute | solution.py:19
  1.1 28.3 %collective-permute-start.3 = (bf16[256,2048]{1,0:T(8,128)(2,1)}, bf16[256,2048]{1,0:T(8,128)(2,1)}, u32[]{:S(2)}, u32[]{:S(2)}) collective-permute-start(bf16[256,2048]{1,0:T(8,128)(2,1)} %bitcast.296), channel_id=1, source_target_pairs={{0,8},{4,12},{8,0},{12,4},{1,9},{5,13},{9,1},{13,5},{2,10},{6,14},... | collective-permute-start | bytes 3145736 | tf_op jit(solution)/shard_map/ppermute | solution.py:19
  5.6 4.7 %copy-start.16 = (bf16[1,2048,1024]{2,1,0:T(8,128)(2,1)S(1)}, bf16[1,2048,1024]{2,1,0:T(8,128)(2,1)}, u32[]{:S(2)}) copy-start(bf16[1,2048,1024]{2,1,0:T(8,128)(2,1)} %param.15) | copy-start | bytes 12582916
  5.6 4.7 %copy-start.19 = (bf16[1,2048,128]{2,1,0:T(8,128)(2,1)S(1)}, bf16[1,2048,128]{2,1,0:T(8,128)(2,1)}, u32[]{:S(2)}) copy-start(bf16[1,2048,128]{2,1,0:T(8,128)(2,1)} %param.17) | copy-start | bytes 1572868
  10.1 4.6 %collective-permute-start.2 = (bf16[256,2048]{1,0:T(8,128)(2,1)S(1)}, bf16[256,2048]{1,0:T(8,128)(2,1)S(1)}, u32[]{:S(2)}, u32[]{:S(2)}) collective-permute-start(bf16[256,2048]{1,0:T(8,128)(2,1)S(1)} %bitcast.303), channel_id=1, source_target_pairs={{0,4},{4,0},{8,12},{12,8},{1,5},{5,1},{9,13},{13,9},{2,6},{6,2},{1... | collective-permute-start | bytes 3145736 | tf_op jit(solution)/shard_map/ppermute | solution.py:19
  11.9 17.4 %collective-permute-start.1 = (bf16[2,2,64,1280]{3,2,1,0:T(8,128)(2,1)S(1)}, bf16[2,2,64,1280]{3,2,1,0:T(8,128)(2,1)S(1)}, u32[]{:S(2)}, u32[]{:S(2)}) collective-permute-start(bf16[2,2,64,1280]{3,2,1,0:T(8,128)(2,1)S(1)} %convolution_convert_fusion.3), channel_id=1, source_target_pairs={{0,1},{1,0},{2,3},{3,2},{4,5},{5,4},{6,7},{7,6},{8,9},{9,8},{10,11... | collective-permute-start | bytes 1966088 | tf_op jit(solution)/shard_map/ppermute | solution.py:19
  29.5 11.4 %collective-permute-start.4 = (bf16[256,2048]{1,0:T(8,128)(2,1)}, bf16[256,2048]{1,0:T(8,128)(2,1)S(1)}, u32[]{:S(2)}, u32[]{:S(2)}) collective-permute-start(bf16[256,2048]{1,0:T(8,128)(2,1)} %collective-permute-done.3), channel_id=1, source_target_pairs={{0,4},{4,0},{8,12},{12,8},{1,5},{5,1},{9,13},{13,9},{2,6},{6,2},{1... | collective-permute-start | bytes 3145736 | tf_op jit(solution)/shard_map/ppermute | solution.py:19
  29.7 4.4 %collective-permute-start.5 = (f32[2,256]{1,0:T(2,128)S(1)}, f32[2,256]{1,0:T(2,128)S(1)}, u32[]{:S(2)}, u32[]{:S(2)}) collective-permute-start(f32[2,256]{1,0:T(2,128)S(1)} %pad_maximum_fusion.5), channel_id=1, source_target_pairs={{0,1},{1,0},{2,3},{3,2},{4,5},{5,4},{6,7},{7,6},{8,9},{9,8},{10,11... | collective-permute-start | bytes 6152 | tf_op jit(solution)/shard_map/ppermute | solution.py:19
  31.5 17.8 %collective-permute-start.10 = (bf16[2,1,64,1280]{3,2,1,0:T(8,128)(2,1)S(1)}, bf16[2,1,64,1280]{3,2,1,0:T(8,128)(2,1)S(1)}, u32[]{:S(2)}, u32[]{:S(2)}) collective-permute-start(bf16[2,1,64,1280]{3,2,1,0:T(8,128)(2,1)S(1)} %get-tuple-element.208), channel_id=1, source_target_pairs={{0,2},{1,3},{2,0},{3,1},{4,6},{5,7},{6,4},{7,5},{8,10},{9,11},{10,... | collective-permute-start | bytes 983048 | tf_op jit(solution)/shard_map/ppermute | solution.py:19
  34.1 15.2 %collective-permute-start.9 = (f32[2,256]{1,0:T(2,128)S(1)}, f32[2,256]{1,0:T(2,128)S(1)}, u32[]{:S(2)}, u32[]{:S(2)}) collective-permute-start(f32[2,256]{1,0:T(2,128)S(1)} %add.259), channel_id=1, source_target_pairs={{0,2},{1,3},{2,0},{3,1},{4,6},{5,7},{6,4},{7,5},{8,10},{9,11},{10,... | collective-permute-start | bytes 6152 | tf_op jit(solution)/shard_map/ppermute | solution.py:19
  36.2 24.7 %collective-permute-start.8 = (bf16[2,2,64,1280]{3,2,1,0:T(8,128)(2,1)S(1)}, bf16[2,2,64,1280]{3,2,1,0:T(8,128)(2,1)S(1)}, u32[]{:S(2)}, u32[]{:S(2)}) collective-permute-start(bf16[2,2,64,1280]{3,2,1,0:T(8,128)(2,1)S(1)} %convolution_convert_fusion.2), channel_id=1, source_target_pairs={{0,1},{1,0},{2,3},{3,2},{4,5},{5,4},{6,7},{7,6},{8,9},{9,8},{10,11... | collective-permute-start | bytes 1966088 | tf_op jit(solution)/shard_map/ppermute | solution.py:19
  37.8 24.0 %collective-permute-start.7 = (bf16[256,2048]{1,0:T(8,128)(2,1)S(1)}, bf16[256,2048]{1,0:T(8,128)(2,1)}, u32[]{:S(2)}, u32[]{:S(2)}) collective-permute-start(bf16[256,2048]{1,0:T(8,128)(2,1)S(1)} %bitcast.307), channel_id=1, source_target_pairs={{0,8},{4,12},{8,0},{12,4},{1,9},{5,13},{9,1},{13,5},{2,10},{6,14},... | collective-permute-start | bytes 3145736 | tf_op jit(solution)/shard_map/ppermute | solution.py:19
  44.7 28.3 %collective-permute-start.6 = (bf16[2,2,64,1280]{3,2,1,0:T(8,128)(2,1)S(1)}, bf16[2,2,64,1280]{3,2,1,0:T(8,128)(2,1)S(1)}, u32[]{:S(2)}, u32[]{:S(2)}) collective-permute-start(bf16[2,2,64,1280]{3,2,1,0:T(8,128)(2,1)S(1)} %convolution_convert_fusion.1), channel_id=1, source_target_pairs={{0,1},{1,0},{2,3},{3,2},{4,5},{5,4},{6,7},{7,6},{8,9},{9,8},{10,11... | collective-permute-start | bytes 1966088 | tf_op jit(solution)/shard_map/ppermute | solution.py:19
  49.2 57.0 %copy-start.3 = (bf16[2,1,64,1280]{3,2,1,0:T(8,128)(2,1)}, bf16[2,1,64,1280]{3,2,1,0:T(8,128)(2,1)S(1)}, u32[]{:S(2)}) copy-start(bf16[2,1,64,1280]{3,2,1,0:T(8,128)(2,1)S(1)} %collective-permute-done.10) | copy-start | bytes 983044
  61.8 17.0 %collective-permute-start.13 = (bf16[256,2048]{1,0:T(8,128)(2,1)}, bf16[256,2048]{1,0:T(8,128)(2,1)}, u32[]{:S(2)}, u32[]{:S(2)}) collective-permute-start(bf16[256,2048]{1,0:T(8,128)(2,1)} %collective-permute-done.7), channel_id=1, source_target_pairs={{0,4},{4,0},{8,12},{12,8},{1,5},{5,1},{9,13},{13,9},{2,6},{6,2},{1... | collective-permute-start | bytes 3145736 | tf_op jit(solution)/shard_map/ppermute | solution.py:19
  61.9 11.9 %collective-permute-start.15 = (f32[2,256]{1,0:T(2,128)S(1)}, f32[2,256]{1,0:T(2,128)S(1)}, u32[]{:S(2)}, u32[]{:S(2)}) collective-permute-start(f32[2,256]{1,0:T(2,128)S(1)} %add.260), channel_id=1, source_target_pairs={{0,8},{4,12},{8,0},{12,4},{1,9},{5,13},{9,1},{13,5},{2,10},{6,14},... | collective-permute-start | bytes 6152 | tf_op jit(solution)/shard_map/ppermute | solution.py:19
  73.8 4.6 %collective-permute-start.14 = (f32[2,256]{1,0:T(2,128)S(1)}, f32[2,256]{1,0:T(2,128)S(1)}, u32[]{:S(2)}, u32[]{:S(2)}) collective-permute-start(f32[2,256]{1,0:T(2,128)S(1)} %add.260), channel_id=1, source_target_pairs={{0,4},{4,0},{8,12},{12,8},{1,5},{5,1},{9,13},{13,9},{2,6},{6,2},{1... | collective-permute-start | bytes 6152 | tf_op jit(solution)/shard_map/ppermute | solution.py:19
  73.8 4.7 %collective-permute-start.16 = (f32[2,256]{1,0:T(2,128)S(1)}, f32[2,256]{1,0:T(2,128)S(1)}, u32[]{:S(2)}, u32[]{:S(2)}) collective-permute-start(f32[2,256]{1,0:T(2,128)S(1)} %collective-permute-done.15), channel_id=1, source_target_pairs={{0,4},{4,0},{8,12},{12,8},{1,5},{5,1},{9,13},{13,9},{2,6},{6,2},{1... | collective-permute-start | bytes 6152 | tf_op jit(solution)/shard_map/ppermute | solution.py:19
  75.4 23.9 %collective-permute-start.12 = (bf16[2,1,64,1280]{3,2,1,0:T(8,128)(2,1)}, bf16[2,1,64,1280]{3,2,1,0:T(8,128)(2,1)S(1)}, u32[]{:S(2)}, u32[]{:S(2)}) collective-permute-start(bf16[2,1,64,1280]{3,2,1,0:T(8,128)(2,1)} %get-tuple-element.205), channel_id=1, source_target_pairs={{0,2},{1,3},{2,0},{3,1},{4,6},{5,7},{6,4},{7,5},{8,10},{9,11},{10,... | collective-permute-start | bytes 983048 | tf_op jit(solution)/shard_map/ppermute | solution.py:19
  75.5 30.8 %collective-permute-start.11 = (bf16[2,1,64,1280]{3,2,1,0:T(8,128)(2,1)}, bf16[2,1,64,1280]{3,2,1,0:T(8,128)(2,1)S(1)}, u32[]{:S(2)}, u32[]{:S(2)}) collective-permute-start(bf16[2,1,64,1280]{3,2,1,0:T(8,128)(2,1)} %get-tuple-element.206), channel_id=1, source_target_pairs={{0,2},{1,3},{2,0},{3,1},{4,6},{5,7},{6,4},{7,5},{8,10},{9,11},{10,... | collective-permute-start | bytes 983048 | tf_op jit(solution)/shard_map/ppermute | solution.py:19
  78.8 6.2 %copy-start.18 = (bf16[1,2048,1024]{2,1,0:T(8,128)(2,1)S(1)}, bf16[1,2048,1024]{2,1,0:T(8,128)(2,1)}, u32[]{:S(2)}) copy-start(bf16[1,2048,1024]{2,1,0:T(8,128)(2,1)} %param.21) | copy-start | bytes 12582916
  78.8 6.2 %copy-start.22 = (bf16[1,2048,128]{2,1,0:T(8,128)(2,1)S(1)}, bf16[1,2048,128]{2,1,0:T(8,128)(2,1)}, u32[]{:S(2)}) copy-start(bf16[1,2048,128]{2,1,0:T(8,128)(2,1)} %param.23) | copy-start | bytes 1572868
  78.8 6.2 %copy-start.24 = (bf16[1,2048,128]{2,1,0:T(8,128)(2,1)S(1)}, bf16[1,2048,128]{2,1,0:T(8,128)(2,1)}, u32[]{:S(2)}) copy-start(bf16[1,2048,128]{2,1,0:T(8,128)(2,1)} %param.22) | copy-start | bytes 1572868
  83.6 37.1 %collective-permute-start.20 = (bf16[2,2,64,1280]{3,2,1,0:T(8,128)(2,1)S(1)}, bf16[2,2,64,1280]{3,2,1,0:T(8,128)(2,1)S(1)}, u32[]{:S(2)}, u32[]{:S(2)}) collective-permute-start(bf16[2,2,64,1280]{3,2,1,0:T(8,128)(2,1)S(1)} %convolution_convert_fusion), channel_id=1, source_target_pairs={{0,1},{1,0},{2,3},{3,2},{4,5},{5,4},{6,7},{7,6},{8,9},{9,8},{10,11... | collective-permute-start | bytes 1966088 | tf_op jit(solution)/shard_map/ppermute | solution.py:19
  86.6 35.5 %copy-start.7 = (f32[256,1]{1,0:T(8,128)S(1)}, f32[256,1]{1,0:T(8,128)}, u32[]{:S(2)}) copy-start(f32[256,1]{1,0:T(8,128)} %convert_element_type.470.q_pos) | copy-start | bytes 3076
  99.3 11.6 %copy-start = (bf16[2,1,64,1280]{3,2,1,0:T(8,128)(2,1)}, bf16[2,1,64,1280]{3,2,1,0:T(8,128)(2,1)S(1)}, u32[]{:S(2)}) copy-start(bf16[2,1,64,1280]{3,2,1,0:T(8,128)(2,1)S(1)} %collective-permute-done.12) | copy-start | bytes 983044
  106.3 15.9 %copy-start.5 = (bf16[2,1,64,1280]{3,2,1,0:T(8,128)(2,1)}, bf16[2,1,64,1280]{3,2,1,0:T(8,128)(2,1)S(1)}, u32[]{:S(2)}) copy-start(bf16[2,1,64,1280]{3,2,1,0:T(8,128)(2,1)S(1)} %collective-permute-done.11) | copy-start | bytes 983044
  106.5 15.7 %collective-permute-start.17 = (bf16[256,256]{1,0:T(8,128)(2,1)S(1)}, bf16[256,256]{1,0:T(8,128)(2,1)S(1)}, u32[]{:S(2)}, u32[]{:S(2)}) collective-permute-start(bf16[256,256]{1,0:T(8,128)(2,1)S(1)} %shard_map.140.rest_0_), channel_id=1, source_target_pairs={{0,1},{1,0},{2,3},{3,2},{4,5},{5,4},{6,7},{7,6},{8,9},{9,8},{10,11... | collective-permute-start | bytes 393224 | tf_op jit(solution)/shard_map/ppermute | solution.py:23
  106.5 15.6 %collective-permute-start.18 = (bf16[256,256]{1,0:T(8,128)(2,1)S(1)}, bf16[256,256]{1,0:T(8,128)(2,1)S(1)}, u32[]{:S(2)}, u32[]{:S(2)}) collective-permute-start(bf16[256,256]{1,0:T(8,128)(2,1)S(1)} %shard_map.140.rest_0_), channel_id=1, source_target_pairs={{0,2},{1,3},{2,0},{3,1},{4,6},{5,7},{6,4},{7,5},{8,10},{9,11},{10,... | collective-permute-start | bytes 393224 | tf_op jit(solution)/shard_map/ppermute | solution.py:23
  108.5 13.6 %collective-permute-start.19 = (bf16[256,256]{1,0:T(8,128)(2,1)S(1)}, bf16[256,256]{1,0:T(8,128)(2,1)S(1)}, u32[]{:S(2)}, u32[]{:S(2)}) collective-permute-start(bf16[256,256]{1,0:T(8,128)(2,1)S(1)} %shard_map.140.rest_0_), channel_id=1, source_target_pairs={{0,3},{1,2},{2,1},{3,0},{4,7},{5,6},{6,5},{7,4},{8,11},{9,10},{10,... | collective-permute-start | bytes 393224 | tf_op jit(solution)/shard_map/ppermute | solution.py:23
  128.5 39.6 %collective-permute-start.22 = (bf16[256,1024]{1,0:T(8,128)(2,1)S(1)}, bf16[256,1024]{1,0:T(8,128)(2,1)}, u32[]{:S(2)}, u32[]{:S(2)}) collective-permute-start(bf16[256,1024]{1,0:T(8,128)(2,1)S(1)} %shard_map.141), channel_id=1, source_target_pairs={{0,2},{1,3},{2,0},{3,1},{4,6},{5,7},{6,4},{7,5},{8,10},{9,11},{10,... | collective-permute-start | bytes 1572872 | tf_op jit(solution)/shard_map/ppermute | solution.py:19
  128.6 39.6 %collective-permute-start.21 = (bf16[256,1024]{1,0:T(8,128)(2,1)S(1)}, bf16[256,1024]{1,0:T(8,128)(2,1)}, u32[]{:S(2)}, u32[]{:S(2)}) collective-permute-start(bf16[256,1024]{1,0:T(8,128)(2,1)S(1)} %shard_map.141), channel_id=1, source_target_pairs={{0,1},{1,0},{2,3},{3,2},{4,5},{5,4},{6,7},{7,6},{8,9},{9,8},{10,11... | collective-permute-start | bytes 1572872 | tf_op jit(solution)/shard_map/ppermute | solution.py:19
  128.8 38.2 %collective-permute-start.23 = (bf16[2,1,64,1280]{3,2,1,0:T(8,128)(2,1)}, bf16[2,1,64,1280]{3,2,1,0:T(8,128)(2,1)S(1)}, u32[]{:S(2)}, u32[]{:S(2)}) collective-permute-start(bf16[2,1,64,1280]{3,2,1,0:T(8,128)(2,1)} %get-tuple-element.203), channel_id=1, source_target_pairs={{0,2},{1,3},{2,0},{3,1},{4,6},{5,7},{6,4},{7,5},{8,10},{9,11},{10,... | collective-permute-start | bytes 983048 | tf_op jit(solution)/shard_map/ppermute | solution.py:19
  172.6 9.1 %collective-permute-start.24 = (bf16[2,128,2048]{2,1,0:T(8,128)(2,1)}, bf16[2,128,2048]{2,1,0:T(8,128)(2,1)}, u32[]{:S(2)}, u32[]{:S(2)}) collective-permute-start(bf16[2,128,2048]{2,1,0:T(8,128)(2,1)} %fusion.28), channel_id=1, source_target_pairs={{0,4},{4,0},{8,12},{12,8},{1,5},{5,1},{9,13},{13,9},{2,6},{6,2},{1... | collective-permute-start | bytes 3145736 | tf_op jit(solution)/shard_map/ppermute | solution.py:19
  173.6 11.2 %collective-permute-start.26 = (bf16[256,256]{1,0:T(8,128)(2,1)S(1)}, bf16[256,256]{1,0:T(8,128)(2,1)S(1)}, u32[]{:S(2)}, u32[]{:S(2)}) collective-permute-start(bf16[256,256]{1,0:T(8,128)(2,1)S(1)} %shard_map.142.rest_0_), channel_id=1, source_target_pairs={{0,1},{1,0},{2,3},{3,2},{4,5},{5,4},{6,7},{7,6},{8,9},{9,8},{10,11... | collective-permute-start | bytes 393224 | tf_op jit(solution)/shard_map/ppermute | solution.py:23
  173.7 13.0 %collective-permute-start.27 = (bf16[256,256]{1,0:T(8,128)(2,1)S(1)}, bf16[256,256]{1,0:T(8,128)(2,1)S(1)}, u32[]{:S(2)}, u32[]{:S(2)}) collective-permute-start(bf16[256,256]{1,0:T(8,128)(2,1)S(1)} %shard_map.142.rest_0_), channel_id=1, source_target_pairs={{0,2},{1,3},{2,0},{3,1},{4,6},{5,7},{6,4},{7,5},{8,10},{9,11},{10,... | collective-permute-start | bytes 393224 | tf_op jit(solution)/shard_map/ppermute | solution.py:23
  174.6 12.1 %collective-permute-start.28 = (bf16[256,256]{1,0:T(8,128)(2,1)S(1)}, bf16[256,256]{1,0:T(8,128)(2,1)S(1)}, u32[]{:S(2)}, u32[]{:S(2)}) collective-permute-start(bf16[256,256]{1,0:T(8,128)(2,1)S(1)} %shard_map.142.rest_0_), channel_id=1, source_target_pairs={{0,3},{1,2},{2,1},{3,0},{4,7},{5,6},{6,5},{7,4},{8,11},{9,10},{10,... | collective-permute-start | bytes 393224 | tf_op jit(solution)/shard_map/ppermute | solution.py:23
  178.1 32.0 %collective-permute-start.30 = (bf16[256,1024]{1,0:T(8,128)(2,1)}, bf16[256,1024]{1,0:T(8,128)(2,1)S(1)}, u32[]{:S(2)}, u32[]{:S(2)}) collective-permute-start(bf16[256,1024]{1,0:T(8,128)(2,1)} %collective-permute-done.22), channel_id=1, source_target_pairs={{0,1},{1,0},{2,3},{3,2},{4,5},{5,4},{6,7},{7,6},{8,9},{9,8},{10,11... | collective-permute-start | bytes 1572872 | tf_op jit(solution)/shard_map/ppermute | solution.py:19
  181.6 5.1 %copy-start.2 = (bf16[2,1,64,1280]{3,2,1,0:T(8,128)(2,1)S(1)}, bf16[2,1,64,1280]{3,2,1,0:T(8,128)(2,1)}, u32[]{:S(2)}) copy-start(bf16[2,1,64,1280]{3,2,1,0:T(8,128)(2,1)} %copy-done) | copy-start | bytes 983044
  181.6 5.1 %copy-start.8 = (f32[256,1]{1,0:T(8,128)S(1)}, f32[256,1]{1,0:T(8,128)}, u32[]{:S(2)}) copy-start(f32[256,1]{1,0:T(8,128)} %convert_element_type.470.q_pos) | copy-start | bytes 3076
  183.3 21.2 %collective-permute-start.25 = (bf16[1,128,2048]{2,1,0:T(8,128)(2,1)S(1)}, bf16[1,128,2048]{2,1,0:T(8,128)(2,1)S(1)}, u32[]{:S(2)}, u32[]{:S(2)}) collective-permute-start(bf16[1,128,2048]{2,1,0:T(8,128)(2,1)S(1)} %fusion.91), channel_id=1, source_target_pairs={{0,8},{4,12},{8,0},{12,4},{1,9},{5,13},{9,1},{13,5},{2,10},{6,14},... | collective-permute-start | bytes 1572872 | tf_op jit(solution)/shard_map/ppermute | solution.py:19
  201.4 5.0 %copy-start.11 = (bf16[1,1024,2048]{2,1,0:T(8,128)(2,1)S(1)}, bf16[1,1024,2048]{2,1,0:T(8,128)(2,1)}, u32[]{:S(2)}) copy-start(bf16[1,1024,2048]{2,1,0:T(8,128)(2,1)} %param.18) | copy-start | bytes 12582916
  201.4 24.9 %collective-permute-start.39 = (bf16[256,1024]{1,0:T(8,128)(2,1)S(1)}, bf16[256,1024]{1,0:T(8,128)(2,1)S(1)}, u32[]{:S(2)}, u32[]{:S(2)}) collective-permute-start(bf16[256,1024]{1,0:T(8,128)(2,1)S(1)} %shard_map.143), channel_id=1, source_target_pairs={{0,1},{1,0},{2,3},{3,2},{4,5},{5,4},{6,7},{7,6},{8,9},{9,8},{10,11... | collective-permute-start | bytes 1572872 | tf_op jit(solution)/shard_map/ppermute | solution.py:19
  204.4 28.3 %collective-permute-start.38 = (bf16[256,1024]{1,0:T(8,128)(2,1)S(1)}, bf16[256,1024]{1,0:T(8,128)(2,1)S(1)}, u32[]{:S(2)}, u32[]{:S(2)}) collective-permute-start(bf16[256,1024]{1,0:T(8,128)(2,1)S(1)} %shard_map.143), channel_id=1, source_target_pairs={{0,2},{1,3},{2,0},{3,1},{4,6},{5,7},{6,4},{7,5},{8,10},{9,11},{10,... | collective-permute-start | bytes 1572872 | tf_op jit(solution)/shard_map/ppermute | solution.py:19
  204.7 21.1 %collective-permute-start.29 = (bf16[2,64,2048]{2,1,0:T(8,128)(2,1)S(1)}, bf16[2,64,2048]{2,1,0:T(8,128)(2,1)S(1)}, u32[]{:S(2)}, u32[]{:S(2)}) collective-permute-start(bf16[2,64,2048]{2,1,0:T(8,128)(2,1)S(1)} %add_convert_fusion), channel_id=1, source_target_pairs={{0,16},{16,0},{1,17},{17,1},{2,18},{18,2},{3,19},{19,3},{4,20},{20... | collective-permute-start | bytes 1572872 | tf_op jit(solution)/shard_map/ppermute | solution.py:28
  208.0 2.0 collective-permute-start.31
  210.9 8.6 %collective-permute-start.34 = (bf16[1,64,2048]{2,1,0:T(8,128)(2,1)S(1)}, bf16[1,64,2048]{2,1,0:T(8,128)(2,1)S(1)}, u32[]{:S(2)}, u32[]{:S(2)}) collective-permute-start(bf16[1,64,2048]{2,1,0:T(8,128)(2,1)S(1)} %fusion.92), channel_id=1, source_target_pairs={{0,8},{4,12},{8,0},{12,4},{1,9},{5,13},{9,1},{13,5},{2,10},{6,14},... | collective-permute-start | bytes 786440 | tf_op jit(solution)/shard_map/ppermute | solution.py:19
  212.5 1.9 collective-permute-start.32
  215.4 2.0 collective-permute-start.35
  217.4 8.3 %collective-permute-start.33 = (bf16[1,64,2048]{2,1,0:T(8,128)(2,1)S(1)}, bf16[1,64,2048]{2,1,0:T(8,128)(2,1)S(1)}, u32[]{:S(2)}, u32[]{:S(2)}) collective-permute-start(bf16[1,64,2048]{2,1,0:T(8,128)(2,1)S(1)} %fusion.93), channel_id=1, source_target_pairs={{0,8},{4,12},{8,0},{12,4},{1,9},{5,13},{9,1},{13,5},{2,10},{6,14},... | collective-permute-start | bytes 786440 | tf_op jit(solution)/shard_map/ppermute | solution.py:19
  227.0 10.6 %collective-permute-start.37 = (bf16[1,64,2048]{2,1,0:T(8,128)(2,1)S(1)}, bf16[1,64,2048]{2,1,0:T(8,128)(2,1)S(1)}, u32[]{:S(2)}, u32[]{:S(2)}) collective-permute-start(bf16[1,64,2048]{2,1,0:T(8,128)(2,1)S(1)} %fusion.94), channel_id=1, source_target_pairs={{0,8},{4,12},{8,0},{12,4},{1,9},{5,13},{9,1},{13,5},{2,10},{6,14},... | collective-permute-start | bytes 786440 | tf_op jit(solution)/shard_map/ppermute | solution.py:19
  228.6 9.2 %collective-permute-start.36 = (bf16[1,64,2048]{2,1,0:T(8,128)(2,1)S(1)}, bf16[1,64,2048]{2,1,0:T(8,128)(2,1)S(1)}, u32[]{:S(2)}, u32[]{:S(2)}) collective-permute-start(bf16[1,64,2048]{2,1,0:T(8,128)(2,1)S(1)} %add_convert_fusion.10), channel_id=1, source_target_pairs={{0,16},{16,0},{1,17},{17,1},{2,18},{18,2},{3,19},{19,3},{4,20},{20... | collective-permute-start | bytes 786440 | tf_op jit(solution)/shard_map/ppermute | solution.py:28
  230.1 11.2 %collective-permute-start.42 = (bf16[1,64,2048]{2,1,0:T(8,128)(2,1)S(1)}, bf16[1,64,2048]{2,1,0:T(8,128)(2,1)S(1)}, u32[]{:S(2)}, u32[]{:S(2)}) collective-permute-start(bf16[1,64,2048]{2,1,0:T(8,128)(2,1)S(1)} %add_convert_fusion.9), channel_id=1, source_target_pairs={{0,16},{16,0},{1,17},{17,1},{2,18},{18,2},{3,19},{19,3},{4,20},{20... | collective-permute-start | bytes 786440 | tf_op jit(solution)/shard_map/ppermute | solution.py:28
  230.6 1.9 collective-permute-start.40
  233.4 8.4 %collective-permute-start.45 = (bf16[1,64,2048]{2,1,0:T(8,128)(2,1)S(1)}, bf16[1,64,2048]{2,1,0:T(8,128)(2,1)S(1)}, u32[]{:S(2)}, u32[]{:S(2)}) collective-permute-start(bf16[1,64,2048]{2,1,0:T(8,128)(2,1)S(1)} %fusion.95), channel_id=1, source_target_pairs={{0,8},{4,12},{8,0},{12,4},{1,9},{5,13},{9,1},{13,5},{2,10},{6,14},... | collective-permute-start | bytes 786440 | tf_op jit(solution)/shard_map/ppermute | solution.py:19
  234.0 1.9 collective-permute-start.41
  235.9 14.0 %collective-permute-start.44 = (bf16[256,1024]{1,0:T(8,128)(2,1)S(1)}, bf16[256,1024]{1,0:T(8,128)(2,1)S(1)}, u32[]{:S(2)}, u32[]{:S(2)}) collective-permute-start(bf16[256,1024]{1,0:T(8,128)(2,1)S(1)} %collective-permute-done.38), channel_id=1, source_target_pairs={{0,1},{1,0},{2,3},{3,2},{4,5},{5,4},{6,7},{7,6},{8,9},{9,8},{10,11... | collective-permute-start | bytes 1572872 | tf_op jit(solution)/shard_map/ppermute | solution.py:19
  250.7 9.3 %collective-permute-start.43 = (bf16[1,64,2048]{2,1,0:T(8,128)(2,1)S(1)}, bf16[1,64,2048]{2,1,0:T(8,128)(2,1)S(1)}, u32[]{:S(2)}, u32[]{:S(2)}) collective-permute-start(bf16[1,64,2048]{2,1,0:T(8,128)(2,1)S(1)} %add_convert_fusion.8), channel_id=1, source_target_pairs={{0,16},{16,0},{1,17},{17,1},{2,18},{18,2},{3,19},{19,3},{4,20},{20... | collective-permute-start | bytes 786440 | tf_op jit(solution)/shard_map/ppermute | solution.py:28
  252.3 7.7 %collective-permute-start.48 = (bf16[1,64,2048]{2,1,0:T(8,128)(2,1)S(1)}, bf16[1,64,2048]{2,1,0:T(8,128)(2,1)S(1)}, u32[]{:S(2)}, u32[]{:S(2)}) collective-permute-start(bf16[1,64,2048]{2,1,0:T(8,128)(2,1)S(1)} %fusion.96), channel_id=1, source_target_pairs={{0,8},{4,12},{8,0},{12,4},{1,9},{5,13},{9,1},{13,5},{2,10},{6,14},... | collective-permute-start | bytes 786440 | tf_op jit(solution)/shard_map/ppermute | solution.py:19
  253.8 11.8 %collective-permute-start.47 = (bf16[1,64,2048]{2,1,0:T(8,128)(2,1)S(1)}, bf16[1,64,2048]{2,1,0:T(8,128)(2,1)S(1)}, u32[]{:S(2)}, u32[]{:S(2)}) collective-permute-start(bf16[1,64,2048]{2,1,0:T(8,128)(2,1)S(1)} %add_convert_fusion.7), channel_id=1, source_target_pairs={{0,16},{16,0},{1,17},{17,1},{2,18},{18,2},{3,19},{19,3},{4,20},{20... | collective-permute-start | bytes 786440 | tf_op jit(solution)/shard_map/ppermute | solution.py:28
  254.4 1.9 collective-permute-start.46
  256.4 9.2 %collective-permute-start.50 = (bf16[1,64,2048]{2,1,0:T(8,128)(2,1)S(1)}, bf16[1,64,2048]{2,1,0:T(8,128)(2,1)S(1)}, u32[]{:S(2)}, u32[]{:S(2)}) collective-permute-start(bf16[1,64,2048]{2,1,0:T(8,128)(2,1)S(1)} %fusion.97), channel_id=1, source_target_pairs={{0,8},{4,12},{8,0},{12,4},{1,9},{5,13},{9,1},{13,5},{2,10},{6,14},... | collective-permute-start | bytes 786440 | tf_op jit(solution)/shard_map/ppermute | solution.py:19
  260.1 11.1 %collective-permute-start.49 = (bf16[1,64,2048]{2,1,0:T(8,128)(2,1)S(1)}, bf16[1,64,2048]{2,1,0:T(8,128)(2,1)S(1)}, u32[]{:S(2)}, u32[]{:S(2)}) collective-permute-start(bf16[1,64,2048]{2,1,0:T(8,128)(2,1)S(1)} %add_convert_fusion.6), channel_id=1, source_target_pairs={{0,16},{16,0},{1,17},{17,1},{2,18},{18,2},{3,19},{19,3},{4,20},{20... | collective-permute-start | bytes 786440 | tf_op jit(solution)/shard_map/ppermute | solution.py:28
  265.8 9.3 %collective-permute-start.51 = (bf16[1,64,2048]{2,1,0:T(8,128)(2,1)S(1)}, bf16[1,64,2048]{2,1,0:T(8,128)(2,1)S(1)}, u32[]{:S(2)}, u32[]{:S(2)}) collective-permute-start(bf16[1,64,2048]{2,1,0:T(8,128)(2,1)S(1)} %add_convert_fusion.5), channel_id=1, source_target_pairs={{0,16},{16,0},{1,17},{17,1},{2,18},{18,2},{3,19},{19,3},{4,20},{20... | collective-permute-start | bytes 786440 | tf_op jit(solution)/shard_map/ppermute | solution.py:28
  (15 other events, 54.1 us)

commit v2 on v1

--- a/solution.py
+++ b/solution.py
@@ -390,9 +390,9 @@
     d_m = landed(d_m)
     d_q = landed(d_q)
     u_p = out_third(u, *u_p, of_u[1], -1)
+    u_o = landed(u_o)
     u_q = first(u, u_got, of_u[3])
     u_q = out_second(*u_q)
-    u_o = landed(u_o)
     u_m = out_third(u, *u_m, of_u[2], -1)
     u_p = landed(u_p)
     u_q = out_third(u, *u_q, of_u[3], -1)

time: 282 us -> 276 us (0.979)
  waiting for transfers between devices: 143 us -> 136 us
    ppermute x7, waiting for transfers between devices: 17 us -> 10.2 us  [from_behind(): lax.ppermute(value, axis, [(i, (i + steps) % count) for i in range(count)])]
  transfers between devices with their start and end apart: 52 -> 52, of which waited for: 27 -> 25; matrix products, arithmetic and copies ran while one was open for 18% -> 18% of each run, Pallas kernels for 5% -> 6%
where the time goes in v2:
time: 276 us; the launch traced here: 271 us
  waiting for transfers between devices  136 us (49%)
  starting transfers between devices  54.9 us (20%)
  matrix products  35 us (13%)
  Pallas kernels  19.5 us (7%)
  other arithmetic  15.3 us (6%)
  local copies, waits for them, and re-layouts  8.16 us (3%)
    ppermute x39, waiting for transfers between devices, swapped(): lax.ppermute(value, axis, [(i, i ^ 1 << bit) for i in range(lax.axis_size...  123 us
    ppermute x39, starting transfers between devices, swapped(): lax.ppermute(value, axis, [(i, i ^ 1 << bit) for i in range(lax.axis_size...  37 us
    dot_general x8, matrix products, project(): out = jnp.dot(rows, self.w, preferred_element_type=F32)  19.7 us
    pallas_call x2, Pallas kernels, attend(): whole(functools.partial(attention_kernel, qw, kvw, n_col), jax.ShapeDtype...  19.1 us
    dot_general x14, matrix products, dot(): out = jnp.dot(value.reshape(-1, qw), c.wo, preferred_element_type=F32)  15.3 us
    ppermute x7, waiting for transfers between devices, from_behind(): lax.ppermute(value, axis, [(i, (i + steps) % count) for i in range(count)])  10.2 us
    ppermute x7, starting transfers between devices, from_behind(): lax.ppermute(value, axis, [(i, (i + steps) % count) for i in range(count)])  9.06 us
    ppermute x6, starting transfers between devices, crossed(): lax.ppermute(value, axis, [(i, i ^ bits) for i in range(lax.axis_size(axi...  8.89 us
  transfers between devices with their start and end apart: 52, of which 25 were waited for; matrix products, arithmetic and copies ran while one was open for 18% of the time, Pallas kernels for 6%

profile of v2, /device:TPU:0, one launch (start us, length us, event | category | flops | bytes accessed | tf_op | source)
XLA Modules:
  0.0 270.6 jit_solution(4918789212556978634)
XLA Ops:
  1.1 2.6 collective-permute-start.3
  4.4 1.1 fusion.80
  5.7 4.4 %convolution_convert_fusion.3 = bf16[2,2,64,1280]{3,2,1,0:T(8,128)(2,1)S(1)} fusion(s32[]{:T(128)S(6)} %select_n.81, bf16[1,2,2,64,2048]{4,3,2,1,0:T(8,128)(2,1)} %bitcast.298, bf16[1,2,2,64,2048]{4,3,2,1,0:T(8,128)(2,1)S(1)} %bitcast.319, f32[2048]{0:T(1024)} %bitcast.360, bf16[2048,128]{1,0:T(8,128)(2,1)} %bitcast.344, bf16[2048,128]{1,0:T(8,128)(2,1)} %bitcast.348, ...), kind=kOutput, calls=%fused_computation.34 | convolution fusion | flops 1360330752 | bytes 8003588 | tf_op jit(solution)/shard_map/dot_general | solution.py:133
  10.4 1.6 fusion.53
  11.9 2.2 collective-permute-start.1
  14.8 1.6 convolution_convert_fusion.2
  16.4 13.0 %collective-permute-done.1 = bf16[2,2,64,1280]{3,2,1,0:T(8,128)(2,1)S(1)} collective-permute-done((bf16[2,2,64,1280]{3,2,1,0:T(8,128)(2,1)S(1)}, bf16[2,2,64,1280]{3,2,1,0:T(8,128)(2,1)S(1)}, u32[]{:S(2)}, u32[]{:S(2)}) %collective-permute-start.1) | collective-permute-done | bytes 655392 | tf_op jit(solution)/shard_map/ppermute | solution.py:19
  29.7 1.8 collective-permute-start.5
  31.5 2.6 collective-permute-start.10
  34.1 2.0 collective-permute-start.9
  36.2 1.6 collective-permute-start.8
  37.8 1.5 collective-permute-start.7
  39.3 1.6 fusion.54
  40.9 2.6 convolution_convert_fusion.1
  43.6 1.1 fusion.70
  45.2 1.6 fusion.55
  46.8 2.5 collective-permute-done.10
  49.3 11.6 %collective-permute-done.8 = bf16[2,2,64,1280]{3,2,1,0:T(8,128)(2,1)S(1)} collective-permute-done((bf16[2,2,64,1280]{3,2,1,0:T(8,128)(2,1)S(1)}, bf16[2,2,64,1280]{3,2,1,0:T(8,128)(2,1)S(1)}, u32[]{:S(2)}, u32[]{:S(2)}) %collective-permute-start.8) | collective-permute-done | bytes 655392 | tf_op jit(solution)/shard_map/ppermute | solution.py:19
  61.9 1.5 collective-permute-start.15
  63.4 9.5 %collective-permute-done.6 = bf16[2,2,64,1280]{3,2,1,0:T(8,128)(2,1)S(1)} collective-permute-done((bf16[2,2,64,1280]{3,2,1,0:T(8,128)(2,1)S(1)}, bf16[2,2,64,1280]{3,2,1,0:T(8,128)(2,1)S(1)}, u32[]{:S(2)}, u32[]{:S(2)}) %collective-permute-start.6) | collective-permute-done | bytes 655392 | tf_op jit(solution)/shard_map/ppermute | solution.py:19
  75.5 2.9 %collective-permute-start.11 = (bf16[2,1,64,1280]{3,2,1,0:T(8,128)(2,1)}, bf16[2,1,64,1280]{3,2,1,0:T(8,128)(2,1)S(1)}, u32[]{:S(2)}, u32[]{:S(2)}) collective-permute-start(bf16[2,1,64,1280]{3,2,1,0:T(8,128)(2,1)} %get-tuple-element.206), channel_id=1, source_target_pairs={{0,2},{1,3},{2,0},{3,1},{4,6},{5,7},{6,4},{7,5},{8,10},{9,11},{10,... | collective-permute-start | bytes 983048 | tf_op jit(solution)/shard_map/ppermute | solution.py:19
  78.8 4.8 %convolution_convert_fusion = bf16[2,2,64,1280]{3,2,1,0:T(8,128)(2,1)S(1)} fusion(s32[]{:T(128)S(6)} %select_n.81, bf16[1,2,2,64,2048]{4,3,2,1,0:T(8,128)(2,1)} %bitcast.35, bf16[1,2,2,64,2048]{4,3,2,1,0:T(8,128)(2,1)} %bitcast.36, f32[2048]{0:T(1024)S(1)} %bitcast.366, bf16[2048,128]{1,0:T(8,128)(2,1)} %bitcast.352, bf16[2048,128]{1,0:T(8,128)(2,1)} %bitcast.356, ...), kind=kOutput, calls=%fused_computation.31 | convolution fusion | flops 1360330752 | bytes 8003588 | tf_op jit(solution)/shard_map/dot_general | solution.py:133
  83.7 1.3 fusion.65
  85.0 1.6 fusion.56
  86.6 12.7 %collective-permute-done.12 = bf16[2,1,64,1280]{3,2,1,0:T(8,128)(2,1)S(1)} collective-permute-done((bf16[2,1,64,1280]{3,2,1,0:T(8,128)(2,1)}, bf16[2,1,64,1280]{3,2,1,0:T(8,128)(2,1)S(1)}, u32[]{:S(2)}, u32[]{:S(2)}) %collective-permute-start.12) | collective-permute-done | bytes 327712 | tf_op jit(solution)/shard_map/ppermute | solution.py:19
  99.3 6.9 %collective-permute-done.11 = bf16[2,1,64,1280]{3,2,1,0:T(8,128)(2,1)S(1)} collective-permute-done((bf16[2,1,64,1280]{3,2,1,0:T(8,128)(2,1)}, bf16[2,1,64,1280]{3,2,1,0:T(8,128)(2,1)S(1)}, u32[]{:S(2)}, u32[]{:S(2)}) %collective-permute-start.11) | collective-permute-done | bytes 327712 | tf_op jit(solution)/shard_map/ppermute | solution.py:19
  106.5 2.0 collective-permute-start.18
  108.5 2.4 collective-permute-start.19
  110.9 9.8 %collective-permute-done.20 = bf16[2,2,64,1280]{3,2,1,0:T(8,128)(2,1)S(1)} collective-permute-done((bf16[2,2,64,1280]{3,2,1,0:T(8,128)(2,1)S(1)}, bf16[2,2,64,1280]{3,2,1,0:T(8,128)(2,1)S(1)}, u32[]{:S(2)}, u32[]{:S(2)}) %collective-permute-start.20) | collective-permute-done | bytes 655392 | tf_op jit(solution)/shard_map/ppermute | solution.py:19
  124.1 4.5 %shard_map.141 = bf16[256,1024]{1,0:T(8,128)(2,1)S(1)} custom-call(f32[128,1280]{1,0:T(8,128)S(1)} %bitcast.279, f32[128,1280]{1,0:T(8,128)S(1)} %bitcast.283, bf16[128,1280]{1,0:T(8,128)(2,1)S(1)} %bitcast.290, bf16[128,1280]{1,0:T(8,128)(2,1)S(1)} %bitcast.294, f32[256,1]{1,0:T(8,128)S(1)} %squeeze.177.inverse, f32[256,128]{1,0:T(8,128)S(1)} %pad_maximum_fusion.3.cosine, ...), custom_call_target="tpu_custom_call" | custom-call | flops 1073741824 | bytes 2097152 | tf_op jit(solution)/shard_map/pallas_call | solution.py:288
  128.8 2.8 %collective-permute-start.23 = (bf16[2,1,64,1280]{3,2,1,0:T(8,128)(2,1)}, bf16[2,1,64,1280]{3,2,1,0:T(8,128)(2,1)S(1)}, u32[]{:S(2)}, u32[]{:S(2)}) collective-permute-start(bf16[2,1,64,1280]{3,2,1,0:T(8,128)(2,1)} %get-tuple-element.203), channel_id=1, source_target_pairs={{0,2},{1,3},{2,0},{3,1},{4,6},{5,7},{6,4},{7,5},{8,10},{9,11},{10,... | collective-permute-start | bytes 983048 | tf_op jit(solution)/shard_map/ppermute | solution.py:19
  131.7 35.3 %collective-permute-done.23 = bf16[2,1,64,1280]{3,2,1,0:T(8,128)(2,1)S(1)} collective-permute-done((bf16[2,1,64,1280]{3,2,1,0:T(8,128)(2,1)}, bf16[2,1,64,1280]{3,2,1,0:T(8,128)(2,1)S(1)}, u32[]{:S(2)}, u32[]{:S(2)}) %collective-permute-start.23) | collective-permute-done | bytes 327712 | tf_op jit(solution)/shard_map/ppermute | solution.py:19
  168.2 1.3 pad_maximum_fusion.2
  170.3 2.2 fusion.28
  174.6 3.5 %collective-permute-start.28 = (bf16[256,256]{1,0:T(8,128)(2,1)S(1)}, bf16[256,256]{1,0:T(8,128)(2,1)S(1)}, u32[]{:S(2)}, u32[]{:S(2)}) collective-permute-start(bf16[256,256]{1,0:T(8,128)(2,1)S(1)} %shard_map.142.rest_0_), channel_id=1, source_target_pairs={{0,3},{1,2},{2,1},{3,0},{4,7},{5,6},{6,5},{7,4},{8,11},{9,10},{10,... | collective-permute-start | bytes 393224 | tf_op jit(solution)/shard_map/ppermute | solution.py:23
  178.1 3.5 %fusion.24 = f32[2,128,2048]{2,1,0:T(8,128)S(1)} fusion(bf16[2,128,1024]{2,1,0:T(8,128)(2,1)S(1)} %bitcast.315, bf16[1,1024,2048]{2,1,0:T(8,128)(2,1)} %param.18), kind=kOutput, calls=%fused_computation.26 | convolution fusion | flops 1073741824 | bytes 6815744 | tf_op jit(solution)/shard_map/dot_general | solution.py:311
  181.6 1.6 add_bitcast_fusion
  183.3 1.6 collective-permute-start.25
  184.8 1.8 collective-permute-done.27.rest_2_
  186.7 14.6 %shard_map.143 = bf16[256,1024]{1,0:T(8,128)(2,1)S(1)} custom-call(f32[128,1280]{1,0:T(8,128)S(1)} %bitcast.277, f32[128,1280]{1,0:T(8,128)S(1)} %bitcast.281, bf16[128,1280]{1,0:T(8,128)(2,1)S(1)} %bitcast.288, bf16[128,1280]{1,0:T(8,128)(2,1)S(1)} %bitcast.292, f32[256,1]{1,0:T(8,128)S(1)} %squeeze.178.inverse, f32[256,128]{1,0:T(8,128)S(1)} %pad_maximum_fusion.3.cosine, ...), custom_call_target="tpu_custom_call" | custom-call | flops 1073741824 | bytes 2097152 | tf_op jit(solution)/shard_map/pallas_call | solution.py:288
  201.4 3.0 %collective-permute-start.39 = (bf16[256,1024]{1,0:T(8,128)(2,1)S(1)}, bf16[256,1024]{1,0:T(8,128)(2,1)S(1)}, u32[]{:S(2)}, u32[]{:S(2)}) collective-permute-start(bf16[256,1024]{1,0:T(8,128)(2,1)S(1)} %shard_map.143), channel_id=1, source_target_pairs={{0,1},{1,0},{2,3},{3,2},{4,5},{5,4},{6,7},{7,6},{8,9},{9,8},{10,11... | collective-permute-start | bytes 1572872 | tf_op jit(solution)/shard_map/ppermute | solution.py:19
  204.7 1.6 collective-permute-start.29
  206.3 1.7 fusion.31
  210.9 1.6 collective-permute-start.34
  213.3 1.1 collective-permute-done.32
  218.0 1.5 collective-permute-done.34
  219.6 6.1 %collective-permute-done.33 = bf16[1,64,2048]{2,1,0:T(8,128)(2,1)S(1)} collective-permute-done((bf16[1,64,2048]{2,1,0:T(8,128)(2,1)S(1)}, bf16[1,64,2048]{2,1,0:T(8,128)(2,1)S(1)}, u32[]{:S(2)}, u32[]{:S(2)}) %collective-permute-start.33) | collective-permute-done | bytes 262176 | tf_op jit(solution)/shard_map/ppermute | solution.py:19
  227.0 1.6 collective-permute-start.37
  228.6 1.5 collective-permute-start.36
  231.4 1.1 collective-permute-done.40
  234.8 1.1 collective-permute-done.41
  235.9 1.5 collective-permute-start.47
  239.4 2.1 collective-permute-done.42
  242.8 1.6 collective-permute-start.45
  244.7 3.4 %collective-permute-done.43 = bf16[1,64,2048]{2,1,0:T(8,128)(2,1)S(1)} collective-permute-done((bf16[1,64,2048]{2,1,0:T(8,128)(2,1)S(1)}, bf16[1,64,2048]{2,1,0:T(8,128)(2,1)S(1)}, u32[]{:S(2)}, u32[]{:S(2)}) %collective-permute-start.43) | collective-permute-done | bytes 262176 | tf_op jit(solution)/shard_map/ppermute | solution.py:28
  248.1 1.9 collective-permute-done.47
  251.5 1.1 collective-permute-done.48
  252.8 1.6 collective-permute-start.50
  254.4 1.6 collective-permute-start.49
  256.1 5.1 %collective-permute-done.50 = bf16[1,64,2048]{2,1,0:T(8,128)(2,1)S(1)} collective-permute-done((bf16[1,64,2048]{2,1,0:T(8,128)(2,1)S(1)}, bf16[1,64,2048]{2,1,0:T(8,128)(2,1)S(1)}, u32[]{:S(2)}, u32[]{:S(2)}) %collective-permute-start.50) | collective-permute-done | bytes 262176 | tf_op jit(solution)/shard_map/ppermute | solution.py:19
  261.3 1.6 collective-permute-start.51
  262.9 1.3 reverse_select_fusion.2
  264.1 4.7 %collective-permute-done.51 = bf16[1,64,2048]{2,1,0:T(8,128)(2,1)S(1)} collective-permute-done((bf16[1,64,2048]{2,1,0:T(8,128)(2,1)S(1)}, bf16[1,64,2048]{2,1,0:T(8,128)(2,1)S(1)}, u32[]{:S(2)}, u32[]{:S(2)}) %collective-permute-start.51) | collective-permute-done | bytes 262176 | tf_op jit(solution)/shard_map/ppermute | solution.py:28
  269.2 1.2 reverse_select_fusion
  (198 shorter events, 33.1 us)
Async XLA Ops:
  0.6 3.8 %collective-permute-start = (bf16[256,2048]{1,0:T(8,128)(2,1)}, bf16[256,2048]{1,0:T(8,128)(2,1)S(1)}, u32[]{:S(2)}, u32[]{:S(2)}) collective-permute-start(bf16[256,2048]{1,0:T(8,128)(2,1)} %bitcast.295), channel_id=1, source_target_pairs={{0,4},{4,0},{8,12},{12,8},{1,5},{5,1},{9,13},{13,9},{2,6},{6,2},{1... | collective-permute-start | bytes 3145736 | tf_op jit(solution)/shard_map/ppermute | solution.py:19
  1.1 28.3 %collective-permute-start.3 = (bf16[256,2048]{1,0:T(8,128)(2,1)}, bf16[256,2048]{1,0:T(8,128)(2,1)}, u32[]{:S(2)}, u32[]{:S(2)}) collective-permute-start(bf16[256,2048]{1,0:T(8,128)(2,1)} %bitcast.296), channel_id=1, source_target_pairs={{0,8},{4,12},{8,0},{12,4},{1,9},{5,13},{9,1},{13,5},{2,10},{6,14},... | collective-permute-start | bytes 3145736 | tf_op jit(solution)/shard_map/ppermute | solution.py:19
  5.6 4.7 %copy-start.16 = (bf16[1,2048,1024]{2,1,0:T(8,128)(2,1)S(1)}, bf16[1,2048,1024]{2,1,0:T(8,128)(2,1)}, u32[]{:S(2)}) copy-start(bf16[1,2048,1024]{2,1,0:T(8,128)(2,1)} %param.15) | copy-start | bytes 12582916
  10.1 4.6 %collective-permute-start.2 = (bf16[256,2048]{1,0:T(8,128)(2,1)S(1)}, bf16[256,2048]{1,0:T(8,128)(2,1)S(1)}, u32[]{:S(2)}, u32[]{:S(2)}) collective-permute-start(bf16[256,2048]{1,0:T(8,128)(2,1)S(1)} %bitcast.303), channel_id=1, source_target_pairs={{0,4},{4,0},{8,12},{12,8},{1,5},{5,1},{9,13},{13,9},{2,6},{6,2},{1... | collective-permute-start | bytes 3145736 | tf_op jit(solution)/shard_map/ppermute | solution.py:19
  11.9 17.4 %collective-permute-start.1 = (bf16[2,2,64,1280]{3,2,1,0:T(8,128)(2,1)S(1)}, bf16[2,2,64,1280]{3,2,1,0:T(8,128)(2,1)S(1)}, u32[]{:S(2)}, u32[]{:S(2)}) collective-permute-start(bf16[2,2,64,1280]{3,2,1,0:T(8,128)(2,1)S(1)} %convolution_convert_fusion.3), channel_id=1, source_target_pairs={{0,1},{1,0},{2,3},{3,2},{4,5},{5,4},{6,7},{7,6},{8,9},{9,8},{10,11... | collective-permute-start | bytes 1966088 | tf_op jit(solution)/shard_map/ppermute | solution.py:19
  29.5 11.4 %collective-permute-start.4 = (bf16[256,2048]{1,0:T(8,128)(2,1)}, bf16[256,2048]{1,0:T(8,128)(2,1)S(1)}, u32[]{:S(2)}, u32[]{:S(2)}) collective-permute-start(bf16[256,2048]{1,0:T(8,128)(2,1)} %collective-permute-done.3), channel_id=1, source_target_pairs={{0,4},{4,0},{8,12},{12,8},{1,5},{5,1},{9,13},{13,9},{2,6},{6,2},{1... | collective-permute-start | bytes 3145736 | tf_op jit(solution)/shard_map/ppermute | solution.py:19
  29.7 4.4 %collective-permute-start.5 = (f32[2,256]{1,0:T(2,128)S(1)}, f32[2,256]{1,0:T(2,128)S(1)}, u32[]{:S(2)}, u32[]{:S(2)}) collective-permute-start(f32[2,256]{1,0:T(2,128)S(1)} %pad_maximum_fusion.5), channel_id=1, source_target_pairs={{0,1},{1,0},{2,3},{3,2},{4,5},{5,4},{6,7},{7,6},{8,9},{9,8},{10,11... | collective-permute-start | bytes 6152 | tf_op jit(solution)/shard_map/ppermute | solution.py:19
  31.5 17.8 %collective-permute-start.10 = (bf16[2,1,64,1280]{3,2,1,0:T(8,128)(2,1)S(1)}, bf16[2,1,64,1280]{3,2,1,0:T(8,128)(2,1)S(1)}, u32[]{:S(2)}, u32[]{:S(2)}) collective-permute-start(bf16[2,1,64,1280]{3,2,1,0:T(8,128)(2,1)S(1)} %get-tuple-element.208), channel_id=1, source_target_pairs={{0,2},{1,3},{2,0},{3,1},{4,6},{5,7},{6,4},{7,5},{8,10},{9,11},{10,... | collective-permute-start | bytes 983048 | tf_op jit(solution)/shard_map/ppermute | solution.py:19
  34.1 15.2 %collective-permute-start.9 = (f32[2,256]{1,0:T(2,128)S(1)}, f32[2,256]{1,0:T(2,128)S(1)}, u32[]{:S(2)}, u32[]{:S(2)}) collective-permute-start(f32[2,256]{1,0:T(2,128)S(1)} %add.259), channel_id=1, source_target_pairs={{0,2},{1,3},{2,0},{3,1},{4,6},{5,7},{6,4},{7,5},{8,10},{9,11},{10,... | collective-permute-start | bytes 6152 | tf_op jit(solution)/shard_map/ppermute | solution.py:19
  36.2 24.7 %collective-permute-start.8 = (bf16[2,2,64,1280]{3,2,1,0:T(8,128)(2,1)S(1)}, bf16[2,2,64,1280]{3,2,1,0:T(8,128)(2,1)S(1)}, u32[]{:S(2)}, u32[]{:S(2)}) collective-permute-start(bf16[2,2,64,1280]{3,2,1,0:T(8,128)(2,1)S(1)} %convolution_convert_fusion.2), channel_id=1, source_target_pairs={{0,1},{1,0},{2,3},{3,2},{4,5},{5,4},{6,7},{7,6},{8,9},{9,8},{10,11... | collective-permute-start | bytes 1966088 | tf_op jit(solution)/shard_map/ppermute | solution.py:19
  37.8 24.0 %collective-permute-start.7 = (bf16[256,2048]{1,0:T(8,128)(2,1)S(1)}, bf16[256,2048]{1,0:T(8,128)(2,1)}, u32[]{:S(2)}, u32[]{:S(2)}) collective-permute-start(bf16[256,2048]{1,0:T(8,128)(2,1)S(1)} %bitcast.307), channel_id=1, source_target_pairs={{0,8},{4,12},{8,0},{12,4},{1,9},{5,13},{9,1},{13,5},{2,10},{6,14},... | collective-permute-start | bytes 3145736 | tf_op jit(solution)/shard_map/ppermute | solution.py:19
  44.7 28.3 %collective-permute-start.6 = (bf16[2,2,64,1280]{3,2,1,0:T(8,128)(2,1)S(1)}, bf16[2,2,64,1280]{3,2,1,0:T(8,128)(2,1)S(1)}, u32[]{:S(2)}, u32[]{:S(2)}) collective-permute-start(bf16[2,2,64,1280]{3,2,1,0:T(8,128)(2,1)S(1)} %convolution_convert_fusion.1), channel_id=1, source_target_pairs={{0,1},{1,0},{2,3},{3,2},{4,5},{5,4},{6,7},{7,6},{8,9},{9,8},{10,11... | collective-permute-start | bytes 1966088 | tf_op jit(solution)/shard_map/ppermute | solution.py:19
  49.2 57.0 %copy-start.3 = (bf16[2,1,64,1280]{3,2,1,0:T(8,128)(2,1)}, bf16[2,1,64,1280]{3,2,1,0:T(8,128)(2,1)S(1)}, u32[]{:S(2)}) copy-start(bf16[2,1,64,1280]{3,2,1,0:T(8,128)(2,1)S(1)} %collective-permute-done.10) | copy-start | bytes 983044
  61.8 17.0 %collective-permute-start.13 = (bf16[256,2048]{1,0:T(8,128)(2,1)}, bf16[256,2048]{1,0:T(8,128)(2,1)}, u32[]{:S(2)}, u32[]{:S(2)}) collective-permute-start(bf16[256,2048]{1,0:T(8,128)(2,1)} %collective-permute-done.7), channel_id=1, source_target_pairs={{0,4},{4,0},{8,12},{12,8},{1,5},{5,1},{9,13},{13,9},{2,6},{6,2},{1... | collective-permute-start | bytes 3145736 | tf_op jit(solution)/shard_map/ppermute | solution.py:19
  61.9 11.9 %collective-permute-start.15 = (f32[2,256]{1,0:T(2,128)S(1)}, f32[2,256]{1,0:T(2,128)S(1)}, u32[]{:S(2)}, u32[]{:S(2)}) collective-permute-start(f32[2,256]{1,0:T(2,128)S(1)} %add.260), channel_id=1, source_target_pairs={{0,8},{4,12},{8,0},{12,4},{1,9},{5,13},{9,1},{13,5},{2,10},{6,14},... | collective-permute-start | bytes 6152 | tf_op jit(solution)/shard_map/ppermute | solution.py:19
  73.8 4.6 %collective-permute-start.14 = (f32[2,256]{1,0:T(2,128)S(1)}, f32[2,256]{1,0:T(2,128)S(1)}, u32[]{:S(2)}, u32[]{:S(2)}) collective-permute-start(f32[2,256]{1,0:T(2,128)S(1)} %add.260), channel_id=1, source_target_pairs={{0,4},{4,0},{8,12},{12,8},{1,5},{5,1},{9,13},{13,9},{2,6},{6,2},{1... | collective-permute-start | bytes 6152 | tf_op jit(solution)/shard_map/ppermute | solution.py:19
  73.8 4.7 %collective-permute-start.16 = (f32[2,256]{1,0:T(2,128)S(1)}, f32[2,256]{1,0:T(2,128)S(1)}, u32[]{:S(2)}, u32[]{:S(2)}) collective-permute-start(f32[2,256]{1,0:T(2,128)S(1)} %collective-permute-done.15), channel_id=1, source_target_pairs={{0,4},{4,0},{8,12},{12,8},{1,5},{5,1},{9,13},{13,9},{2,6},{6,2},{1... | collective-permute-start | bytes 6152 | tf_op jit(solution)/shard_map/ppermute | solution.py:19
  75.4 23.9 %collective-permute-start.12 = (bf16[2,1,64,1280]{3,2,1,0:T(8,128)(2,1)}, bf16[2,1,64,1280]{3,2,1,0:T(8,128)(2,1)S(1)}, u32[]{:S(2)}, u32[]{:S(2)}) collective-permute-start(bf16[2,1,64,1280]{3,2,1,0:T(8,128)(2,1)} %get-tuple-element.205), channel_id=1, source_target_pairs={{0,2},{1,3},{2,0},{3,1},{4,6},{5,7},{6,4},{7,5},{8,10},{9,11},{10,... | collective-permute-start | bytes 983048 | tf_op jit(solution)/shard_map/ppermute | solution.py:19
  75.5 30.8 %collective-permute-start.11 = (bf16[2,1,64,1280]{3,2,1,0:T(8,128)(2,1)}, bf16[2,1,64,1280]{3,2,1,0:T(8,128)(2,1)S(1)}, u32[]{:S(2)}, u32[]{:S(2)}) collective-permute-start(bf16[2,1,64,1280]{3,2,1,0:T(8,128)(2,1)} %get-tuple-element.206), channel_id=1, source_target_pairs={{0,2},{1,3},{2,0},{3,1},{4,6},{5,7},{6,4},{7,5},{8,10},{9,11},{10,... | collective-permute-start | bytes 983048 | tf_op jit(solution)/shard_map/ppermute | solution.py:19
  78.8 6.2 %copy-start.18 = (bf16[1,2048,1024]{2,1,0:T(8,128)(2,1)S(1)}, bf16[1,2048,1024]{2,1,0:T(8,128)(2,1)}, u32[]{:S(2)}) copy-start(bf16[1,2048,1024]{2,1,0:T(8,128)(2,1)} %param.21) | copy-start | bytes 12582916
  78.8 6.2 %copy-start.22 = (bf16[1,2048,128]{2,1,0:T(8,128)(2,1)S(1)}, bf16[1,2048,128]{2,1,0:T(8,128)(2,1)}, u32[]{:S(2)}) copy-start(bf16[1,2048,128]{2,1,0:T(8,128)(2,1)} %param.23) | copy-start | bytes 1572868
  78.8 6.2 %copy-start.24 = (bf16[1,2048,128]{2,1,0:T(8,128)(2,1)S(1)}, bf16[1,2048,128]{2,1,0:T(8,128)(2,1)}, u32[]{:S(2)}) copy-start(bf16[1,2048,128]{2,1,0:T(8,128)(2,1)} %param.22) | copy-start | bytes 1572868
  83.6 37.1 %collective-permute-start.20 = (bf16[2,2,64,1280]{3,2,1,0:T(8,128)(2,1)S(1)}, bf16[2,2,64,1280]{3,2,1,0:T(8,128)(2,1)S(1)}, u32[]{:S(2)}, u32[]{:S(2)}) collective-permute-start(bf16[2,2,64,1280]{3,2,1,0:T(8,128)(2,1)S(1)} %convolution_convert_fusion), channel_id=1, source_target_pairs={{0,1},{1,0},{2,3},{3,2},{4,5},{5,4},{6,7},{7,6},{8,9},{9,8},{10,11... | collective-permute-start | bytes 1966088 | tf_op jit(solution)/shard_map/ppermute | solution.py:19
  86.6 35.5 %copy-start.7 = (f32[256,1]{1,0:T(8,128)S(1)}, f32[256,1]{1,0:T(8,128)}, u32[]{:S(2)}) copy-start(f32[256,1]{1,0:T(8,128)} %convert_element_type.470.q_pos) | copy-start | bytes 3076
  99.3 11.6 %copy-start = (bf16[2,1,64,1280]{3,2,1,0:T(8,128)(2,1)}, bf16[2,1,64,1280]{3,2,1,0:T(8,128)(2,1)S(1)}, u32[]{:S(2)}) copy-start(bf16[2,1,64,1280]{3,2,1,0:T(8,128)(2,1)S(1)} %collective-permute-done.12) | copy-start | bytes 983044
  106.3 15.9 %copy-start.5 = (bf16[2,1,64,1280]{3,2,1,0:T(8,128)(2,1)}, bf16[2,1,64,1280]{3,2,1,0:T(8,128)(2,1)S(1)}, u32[]{:S(2)}) copy-start(bf16[2,1,64,1280]{3,2,1,0:T(8,128)(2,1)S(1)} %collective-permute-done.11) | copy-start | bytes 983044
  106.5 15.7 %collective-permute-start.17 = (bf16[256,256]{1,0:T(8,128)(2,1)S(1)}, bf16[256,256]{1,0:T(8,128)(2,1)S(1)}, u32[]{:S(2)}, u32[]{:S(2)}) collective-permute-start(bf16[256,256]{1,0:T(8,128)(2,1)S(1)} %shard_map.140.rest_0_), channel_id=1, source_target_pairs={{0,1},{1,0},{2,3},{3,2},{4,5},{5,4},{6,7},{7,6},{8,9},{9,8},{10,11... | collective-permute-start | bytes 393224 | tf_op jit(solution)/shard_map/ppermute | solution.py:23
  106.5 15.6 %collective-permute-start.18 = (bf16[256,256]{1,0:T(8,128)(2,1)S(1)}, bf16[256,256]{1,0:T(8,128)(2,1)S(1)}, u32[]{:S(2)}, u32[]{:S(2)}) collective-permute-start(bf16[256,256]{1,0:T(8,128)(2,1)S(1)} %shard_map.140.rest_0_), channel_id=1, source_target_pairs={{0,2},{1,3},{2,0},{3,1},{4,6},{5,7},{6,4},{7,5},{8,10},{9,11},{10,... | collective-permute-start | bytes 393224 | tf_op jit(solution)/shard_map/ppermute | solution.py:23
  108.5 13.6 %collective-permute-start.19 = (bf16[256,256]{1,0:T(8,128)(2,1)S(1)}, bf16[256,256]{1,0:T(8,128)(2,1)S(1)}, u32[]{:S(2)}, u32[]{:S(2)}) collective-permute-start(bf16[256,256]{1,0:T(8,128)(2,1)S(1)} %shard_map.140.rest_0_), channel_id=1, source_target_pairs={{0,3},{1,2},{2,1},{3,0},{4,7},{5,6},{6,5},{7,4},{8,11},{9,10},{10,... | collective-permute-start | bytes 393224 | tf_op jit(solution)/shard_map/ppermute | solution.py:23
  128.5 39.6 %collective-permute-start.22 = (bf16[256,1024]{1,0:T(8,128)(2,1)S(1)}, bf16[256,1024]{1,0:T(8,128)(2,1)}, u32[]{:S(2)}, u32[]{:S(2)}) collective-permute-start(bf16[256,1024]{1,0:T(8,128)(2,1)S(1)} %shard_map.141), channel_id=1, source_target_pairs={{0,2},{1,3},{2,0},{3,1},{4,6},{5,7},{6,4},{7,5},{8,10},{9,11},{10,... | collective-permute-start | bytes 1572872 | tf_op jit(solution)/shard_map/ppermute | solution.py:19
  128.6 39.6 %collective-permute-start.21 = (bf16[256,1024]{1,0:T(8,128)(2,1)S(1)}, bf16[256,1024]{1,0:T(8,128)(2,1)}, u32[]{:S(2)}, u32[]{:S(2)}) collective-permute-start(bf16[256,1024]{1,0:T(8,128)(2,1)S(1)} %shard_map.141), channel_id=1, source_target_pairs={{0,1},{1,0},{2,3},{3,2},{4,5},{5,4},{6,7},{7,6},{8,9},{9,8},{10,11... | collective-permute-start | bytes 1572872 | tf_op jit(solution)/shard_map/ppermute | solution.py:19
  128.8 38.2 %collective-permute-start.23 = (bf16[2,1,64,1280]{3,2,1,0:T(8,128)(2,1)}, bf16[2,1,64,1280]{3,2,1,0:T(8,128)(2,1)S(1)}, u32[]{:S(2)}, u32[]{:S(2)}) collective-permute-start(bf16[2,1,64,1280]{3,2,1,0:T(8,128)(2,1)} %get-tuple-element.203), channel_id=1, source_target_pairs={{0,2},{1,3},{2,0},{3,1},{4,6},{5,7},{6,4},{7,5},{8,10},{9,11},{10,... | collective-permute-start | bytes 983048 | tf_op jit(solution)/shard_map/ppermute | solution.py:19
  172.6 9.1 %collective-permute-start.24 = (bf16[2,128,2048]{2,1,0:T(8,128)(2,1)}, bf16[2,128,2048]{2,1,0:T(8,128)(2,1)}, u32[]{:S(2)}, u32[]{:S(2)}) collective-permute-start(bf16[2,128,2048]{2,1,0:T(8,128)(2,1)} %fusion.28), channel_id=1, source_target_pairs={{0,4},{4,0},{8,12},{12,8},{1,5},{5,1},{9,13},{13,9},{2,6},{6,2},{1... | collective-permute-start | bytes 3145736 | tf_op jit(solution)/shard_map/ppermute | solution.py:19
  173.6 11.2 %collective-permute-start.26 = (bf16[256,256]{1,0:T(8,128)(2,1)S(1)}, bf16[256,256]{1,0:T(8,128)(2,1)S(1)}, u32[]{:S(2)}, u32[]{:S(2)}) collective-permute-start(bf16[256,256]{1,0:T(8,128)(2,1)S(1)} %shard_map.142.rest_0_), channel_id=1, source_target_pairs={{0,1},{1,0},{2,3},{3,2},{4,5},{5,4},{6,7},{7,6},{8,9},{9,8},{10,11... | collective-permute-start | bytes 393224 | tf_op jit(solution)/shard_map/ppermute | solution.py:23
  173.7 13.0 %collective-permute-start.27 = (bf16[256,256]{1,0:T(8,128)(2,1)S(1)}, bf16[256,256]{1,0:T(8,128)(2,1)S(1)}, u32[]{:S(2)}, u32[]{:S(2)}) collective-permute-start(bf16[256,256]{1,0:T(8,128)(2,1)S(1)} %shard_map.142.rest_0_), channel_id=1, source_target_pairs={{0,2},{1,3},{2,0},{3,1},{4,6},{5,7},{6,4},{7,5},{8,10},{9,11},{10,... | collective-permute-start | bytes 393224 | tf_op jit(solution)/shard_map/ppermute | solution.py:23
  174.6 12.1 %collective-permute-start.28 = (bf16[256,256]{1,0:T(8,128)(2,1)S(1)}, bf16[256,256]{1,0:T(8,128)(2,1)S(1)}, u32[]{:S(2)}, u32[]{:S(2)}) collective-permute-start(bf16[256,256]{1,0:T(8,128)(2,1)S(1)} %shard_map.142.rest_0_), channel_id=1, source_target_pairs={{0,3},{1,2},{2,1},{3,0},{4,7},{5,6},{6,5},{7,4},{8,11},{9,10},{10,... | collective-permute-start | bytes 393224 | tf_op jit(solution)/shard_map/ppermute | solution.py:23
  178.1 32.0 %collective-permute-start.30 = (bf16[256,1024]{1,0:T(8,128)(2,1)}, bf16[256,1024]{1,0:T(8,128)(2,1)S(1)}, u32[]{:S(2)}, u32[]{:S(2)}) collective-permute-start(bf16[256,1024]{1,0:T(8,128)(2,1)} %collective-permute-done.22), channel_id=1, source_target_pairs={{0,1},{1,0},{2,3},{3,2},{4,5},{5,4},{6,7},{7,6},{8,9},{9,8},{10,11... | collective-permute-start | bytes 1572872 | tf_op jit(solution)/shard_map/ppermute | solution.py:19
  181.6 5.1 %copy-start.2 = (bf16[2,1,64,1280]{3,2,1,0:T(8,128)(2,1)S(1)}, bf16[2,1,64,1280]{3,2,1,0:T(8,128)(2,1)}, u32[]{:S(2)}) copy-start(bf16[2,1,64,1280]{3,2,1,0:T(8,128)(2,1)} %copy-done) | copy-start | bytes 983044
  181.6 5.1 %copy-start.8 = (f32[256,1]{1,0:T(8,128)S(1)}, f32[256,1]{1,0:T(8,128)}, u32[]{:S(2)}) copy-start(f32[256,1]{1,0:T(8,128)} %convert_element_type.470.q_pos) | copy-start | bytes 3076
  183.3 21.2 %collective-permute-start.25 = (bf16[1,128,2048]{2,1,0:T(8,128)(2,1)S(1)}, bf16[1,128,2048]{2,1,0:T(8,128)(2,1)S(1)}, u32[]{:S(2)}, u32[]{:S(2)}) collective-permute-start(bf16[1,128,2048]{2,1,0:T(8,128)(2,1)S(1)} %fusion.91), channel_id=1, source_target_pairs={{0,8},{4,12},{8,0},{12,4},{1,9},{5,13},{9,1},{13,5},{2,10},{6,14},... | collective-permute-start | bytes 1572872 | tf_op jit(solution)/shard_map/ppermute | solution.py:19
  201.4 5.0 %copy-start.11 = (bf16[1,1024,2048]{2,1,0:T(8,128)(2,1)S(1)}, bf16[1,1024,2048]{2,1,0:T(8,128)(2,1)}, u32[]{:S(2)}) copy-start(bf16[1,1024,2048]{2,1,0:T(8,128)(2,1)} %param.18) | copy-start | bytes 12582916
  201.4 24.9 %collective-permute-start.39 = (bf16[256,1024]{1,0:T(8,128)(2,1)S(1)}, bf16[256,1024]{1,0:T(8,128)(2,1)S(1)}, u32[]{:S(2)}, u32[]{:S(2)}) collective-permute-start(bf16[256,1024]{1,0:T(8,128)(2,1)S(1)} %shard_map.143), channel_id=1, source_target_pairs={{0,1},{1,0},{2,3},{3,2},{4,5},{5,4},{6,7},{7,6},{8,9},{9,8},{10,11... | collective-permute-start | bytes 1572872 | tf_op jit(solution)/shard_map/ppermute | solution.py:19
  204.4 28.3 %collective-permute-start.38 = (bf16[256,1024]{1,0:T(8,128)(2,1)S(1)}, bf16[256,1024]{1,0:T(8,128)(2,1)S(1)}, u32[]{:S(2)}, u32[]{:S(2)}) collective-permute-start(bf16[256,1024]{1,0:T(8,128)(2,1)S(1)} %shard_map.143), channel_id=1, source_target_pairs={{0,2},{1,3},{2,0},{3,1},{4,6},{5,7},{6,4},{7,5},{8,10},{9,11},{10,... | collective-permute-start | bytes 1572872 | tf_op jit(solution)/shard_map/ppermute | solution.py:19
  204.7 21.1 %collective-permute-start.29 = (bf16[2,64,2048]{2,1,0:T(8,128)(2,1)S(1)}, bf16[2,64,2048]{2,1,0:T(8,128)(2,1)S(1)}, u32[]{:S(2)}, u32[]{:S(2)}) collective-permute-start(bf16[2,64,2048]{2,1,0:T(8,128)(2,1)S(1)} %add_convert_fusion), channel_id=1, source_target_pairs={{0,16},{16,0},{1,17},{17,1},{2,18},{18,2},{3,19},{19,3},{4,20},{20... | collective-permute-start | bytes 1572872 | tf_op jit(solution)/shard_map/ppermute | solution.py:28
  208.0 2.0 collective-permute-start.31
  210.9 8.6 %collective-permute-start.34 = (bf16[1,64,2048]{2,1,0:T(8,128)(2,1)S(1)}, bf16[1,64,2048]{2,1,0:T(8,128)(2,1)S(1)}, u32[]{:S(2)}, u32[]{:S(2)}) collective-permute-start(bf16[1,64,2048]{2,1,0:T(8,128)(2,1)S(1)} %fusion.92), channel_id=1, source_target_pairs={{0,8},{4,12},{8,0},{12,4},{1,9},{5,13},{9,1},{13,5},{2,10},{6,14},... | collective-permute-start | bytes 786440 | tf_op jit(solution)/shard_map/ppermute | solution.py:19
  212.5 1.9 collective-permute-start.32
  215.4 2.0 collective-permute-start.35
  217.4 8.3 %collective-permute-start.33 = (bf16[1,64,2048]{2,1,0:T(8,128)(2,1)S(1)}, bf16[1,64,2048]{2,1,0:T(8,128)(2,1)S(1)}, u32[]{:S(2)}, u32[]{:S(2)}) collective-permute-start(bf16[1,64,2048]{2,1,0:T(8,128)(2,1)S(1)} %fusion.93), channel_id=1, source_target_pairs={{0,8},{4,12},{8,0},{12,4},{1,9},{5,13},{9,1},{13,5},{2,10},{6,14},... | collective-permute-start | bytes 786440 | tf_op jit(solution)/shard_map/ppermute | solution.py:19
  227.0 10.6 %collective-permute-start.37 = (bf16[1,64,2048]{2,1,0:T(8,128)(2,1)S(1)}, bf16[1,64,2048]{2,1,0:T(8,128)(2,1)S(1)}, u32[]{:S(2)}, u32[]{:S(2)}) collective-permute-start(bf16[1,64,2048]{2,1,0:T(8,128)(2,1)S(1)} %fusion.94), channel_id=1, source_target_pairs={{0,8},{4,12},{8,0},{12,4},{1,9},{5,13},{9,1},{13,5},{2,10},{6,14},... | collective-permute-start | bytes 786440 | tf_op jit(solution)/shard_map/ppermute | solution.py:19
  228.6 10.2 %collective-permute-start.36 = (bf16[1,64,2048]{2,1,0:T(8,128)(2,1)S(1)}, bf16[1,64,2048]{2,1,0:T(8,128)(2,1)S(1)}, u32[]{:S(2)}, u32[]{:S(2)}) collective-permute-start(bf16[1,64,2048]{2,1,0:T(8,128)(2,1)S(1)} %add_convert_fusion.10), channel_id=1, source_target_pairs={{0,16},{16,0},{1,17},{17,1},{2,18},{18,2},{3,19},{19,3},{4,20},{20... | collective-permute-start | bytes 786440 | tf_op jit(solution)/shard_map/ppermute | solution.py:28
  230.1 11.4 %collective-permute-start.42 = (bf16[1,64,2048]{2,1,0:T(8,128)(2,1)S(1)}, bf16[1,64,2048]{2,1,0:T(8,128)(2,1)S(1)}, u32[]{:S(2)}, u32[]{:S(2)}) collective-permute-start(bf16[1,64,2048]{2,1,0:T(8,128)(2,1)S(1)} %add_convert_fusion.9), channel_id=1, source_target_pairs={{0,16},{16,0},{1,17},{17,1},{2,18},{18,2},{3,19},{19,3},{4,20},{20... | collective-permute-start | bytes 786440 | tf_op jit(solution)/shard_map/ppermute | solution.py:28
  230.6 1.9 collective-permute-start.40
  233.4 5.2 %copy-start.15 = (bf16[1,256,2048]{2,1,0:T(8,128)(2,1)S(1)}, bf16[1,256,2048]{2,1,0:T(8,128)(2,1)}, u32[]{:S(2)}) copy-start(bf16[1,256,2048]{2,1,0:T(8,128)(2,1)} %param.19) | copy-start | bytes 3145732
  233.4 9.2 %collective-permute-start.44 = (bf16[1,64,2048]{2,1,0:T(8,128)(2,1)S(1)}, bf16[1,64,2048]{2,1,0:T(8,128)(2,1)S(1)}, u32[]{:S(2)}, u32[]{:S(2)}) collective-permute-start(bf16[1,64,2048]{2,1,0:T(8,128)(2,1)S(1)} %fusion.95), channel_id=1, source_target_pairs={{0,8},{4,12},{8,0},{12,4},{1,9},{5,13},{9,1},{13,5},{2,10},{6,14},... | collective-permute-start | bytes 786440 | tf_op jit(solution)/shard_map/ppermute | solution.py:19
  234.0 1.9 collective-permute-start.41
  235.9 14.0 %collective-permute-start.47 = (bf16[256,1024]{1,0:T(8,128)(2,1)S(1)}, bf16[256,1024]{1,0:T(8,128)(2,1)S(1)}, u32[]{:S(2)}, u32[]{:S(2)}) collective-permute-start(bf16[256,1024]{1,0:T(8,128)(2,1)S(1)} %collective-permute-done.38), channel_id=1, source_target_pairs={{0,1},{1,0},{2,3},{3,2},{4,5},{5,4},{6,7},{7,6},{8,9},{9,8},{10,11... | collective-permute-start | bytes 1572872 | tf_op jit(solution)/shard_map/ppermute | solution.py:19
  237.6 16.7 %collective-permute-start.46 = (bf16[1,64,2048]{2,1,0:T(8,128)(2,1)S(1)}, bf16[1,64,2048]{2,1,0:T(8,128)(2,1)S(1)}, u32[]{:S(2)}, u32[]{:S(2)}) collective-permute-start(bf16[1,64,2048]{2,1,0:T(8,128)(2,1)S(1)} %fusion.96), channel_id=1, source_target_pairs={{0,8},{4,12},{8,0},{12,4},{1,9},{5,13},{9,1},{13,5},{2,10},{6,14},... | collective-permute-start | bytes 786440 | tf_op jit(solution)/shard_map/ppermute | solution.py:19
  238.8 9.3 %collective-permute-start.43 = (bf16[1,64,2048]{2,1,0:T(8,128)(2,1)S(1)}, bf16[1,64,2048]{2,1,0:T(8,128)(2,1)S(1)}, u32[]{:S(2)}, u32[]{:S(2)}) collective-permute-start(bf16[1,64,2048]{2,1,0:T(8,128)(2,1)S(1)} %add_convert_fusion.8), channel_id=1, source_target_pairs={{0,16},{16,0},{1,17},{17,1},{2,18},{18,2},{3,19},{19,3},{4,20},{20... | collective-permute-start | bytes 786440 | tf_op jit(solution)/shard_map/ppermute | solution.py:28
  242.8 13.3 %collective-permute-start.45 = (bf16[1,64,2048]{2,1,0:T(8,128)(2,1)S(1)}, bf16[1,64,2048]{2,1,0:T(8,128)(2,1)S(1)}, u32[]{:S(2)}, u32[]{:S(2)}) collective-permute-start(bf16[1,64,2048]{2,1,0:T(8,128)(2,1)S(1)} %add_convert_fusion.7), channel_id=1, source_target_pairs={{0,16},{16,0},{1,17},{17,1},{2,18},{18,2},{3,19},{19,3},{4,20},{20... | collective-permute-start | bytes 786440 | tf_op jit(solution)/shard_map/ppermute | solution.py:28
  250.7 2.0 collective-permute-start.48
  252.8 8.4 %collective-permute-start.50 = (bf16[1,64,2048]{2,1,0:T(8,128)(2,1)S(1)}, bf16[1,64,2048]{2,1,0:T(8,128)(2,1)S(1)}, u32[]{:S(2)}, u32[]{:S(2)}) collective-permute-start(bf16[1,64,2048]{2,1,0:T(8,128)(2,1)S(1)} %fusion.97), channel_id=1, source_target_pairs={{0,8},{4,12},{8,0},{12,4},{1,9},{5,13},{9,1},{13,5},{2,10},{6,14},... | collective-permute-start | bytes 786440 | tf_op jit(solution)/shard_map/ppermute | solution.py:19
  254.4 9.7 %collective-permute-start.49 = (bf16[1,64,2048]{2,1,0:T(8,128)(2,1)S(1)}, bf16[1,64,2048]{2,1,0:T(8,128)(2,1)S(1)}, u32[]{:S(2)}, u32[]{:S(2)}) collective-permute-start(bf16[1,64,2048]{2,1,0:T(8,128)(2,1)S(1)} %add_convert_fusion.6), channel_id=1, source_target_pairs={{0,16},{16,0},{1,17},{17,1},{2,18},{18,2},{3,19},{19,3},{4,20},{20... | collective-permute-start | bytes 786440 | tf_op jit(solution)/shard_map/ppermute | solution.py:28
  261.3 7.6 %collective-permute-start.51 = (bf16[1,64,2048]{2,1,0:T(8,128)(2,1)S(1)}, bf16[1,64,2048]{2,1,0:T(8,128)(2,1)S(1)}, u32[]{:S(2)}, u32[]{:S(2)}) collective-permute-start(bf16[1,64,2048]{2,1,0:T(8,128)(2,1)S(1)} %add_convert_fusion.5), channel_id=1, source_target_pairs={{0,16},{16,0},{1,17},{17,1},{2,18},{18,2},{3,19},{19,3},{4,20},{20... | collective-permute-start | bytes 786440 | tf_op jit(solution)/shard_map/ppermute | solution.py:28
  (15 other events, 54.6 us)

commit v3 on v2

--- a/solution.py
+++ b/solution.py
@@ -393,8 +393,8 @@
     u_o = landed(u_o)
     u_q = first(u, u_got, of_u[3])
     u_q = out_second(*u_q)
+    u_p = landed(u_p)
     u_m = out_third(u, *u_m, of_u[2], -1)
-    u_p = landed(u_p)
     u_q = out_third(u, *u_q, of_u[3], -1)
     return finish(d, of_d, d_p, d_m, d_q), finish(u, of_u, u_o, u_p, u_m, u_q)
 

time: 276 us -> 276 us (level)
  no operation moved by 1% of the time
where the time goes in v3:
time: 276 us; the launch traced here: 271 us
  waiting for transfers between devices  136 us (49%)
  starting transfers between devices  54.9 us (20%)
  matrix products  35 us (13%)
  Pallas kernels  19.5 us (7%)
  other arithmetic  15.3 us (6%)
  local copies, waits for them, and re-layouts  8.16 us (3%)
    ppermute x39, waiting for transfers between devices, swapped(): lax.ppermute(value, axis, [(i, i ^ 1 << bit) for i in range(lax.axis_size...  123 us
    ppermute x39, starting transfers between devices, swapped(): lax.ppermute(value, axis, [(i, i ^ 1 << bit) for i in range(lax.axis_size...  37 us
    dot_general x8, matrix products, project(): out = jnp.dot(rows, self.w, preferred_element_type=F32)  19.7 us
    pallas_call x2, Pallas kernels, attend(): whole(functools.partial(attention_kernel, qw, kvw, n_col), jax.ShapeDtype...  19.1 us
    dot_general x14, matrix products, dot(): out = jnp.dot(value.reshape(-1, qw), c.wo, preferred_element_type=F32)  15.3 us
    ppermute x7, waiting for transfers between devices, from_behind(): lax.ppermute(value, axis, [(i, (i + steps) % count) for i in range(count)])  10.2 us
    ppermute x7, starting transfers between devices, from_behind(): lax.ppermute(value, axis, [(i, (i + steps) % count) for i in range(count)])  9.06 us
    ppermute x6, starting transfers between devices, crossed(): lax.ppermute(value, axis, [(i, i ^ bits) for i in range(lax.axis_size(axi...  8.89 us
  transfers between devices with their start and end apart: 52, of which 25 were waited for; matrix products, arithmetic and copies ran while one was open for 18% of the time, Pallas kernels for 6%

profile of v3, /device:TPU:0, one launch (start us, length us, event | category | flops | bytes accessed | tf_op | source)
XLA Modules:
  0.0 270.6 jit_solution(16888608777658551587)
XLA Ops:
  1.1 2.6 collective-permute-start.3
  4.4 1.1 fusion.80
  5.7 4.4 %convolution_convert_fusion.3 = bf16[2,2,64,1280]{3,2,1,0:T(8,128)(2,1)S(1)} fusion(s32[]{:T(128)S(6)} %select_n.81, bf16[1,2,2,64,2048]{4,3,2,1,0:T(8,128)(2,1)} %bitcast.298, bf16[1,2,2,64,2048]{4,3,2,1,0:T(8,128)(2,1)S(1)} %bitcast.319, f32[2048]{0:T(1024)} %bitcast.360, bf16[2048,128]{1,0:T(8,128)(2,1)} %bitcast.344, bf16[2048,128]{1,0:T(8,128)(2,1)} %bitcast.348, ...), kind=kOutput, calls=%fused_computation.34 | convolution fusion | flops 1360330752 | bytes 8003588 | tf_op jit(solution)/shard_map/dot_general | solution.py:133
  10.4 1.6 fusion.53
  11.9 2.2 collective-permute-start.1
  14.8 1.6 convolution_convert_fusion.2
  16.4 13.0 %collective-permute-done.1 = bf16[2,2,64,1280]{3,2,1,0:T(8,128)(2,1)S(1)} collective-permute-done((bf16[2,2,64,1280]{3,2,1,0:T(8,128)(2,1)S(1)}, bf16[2,2,64,1280]{3,2,1,0:T(8,128)(2,1)S(1)}, u32[]{:S(2)}, u32[]{:S(2)}) %collective-permute-start.1) | collective-permute-done | bytes 655392 | tf_op jit(solution)/shard_map/ppermute | solution.py:19
  29.7 1.8 collective-permute-start.5
  31.5 2.6 collective-permute-start.10
  34.1 2.0 collective-permute-start.9
  36.2 1.6 collective-permute-start.8
  37.8 1.5 collective-permute-start.7
  39.3 1.6 fusion.54
  40.9 2.6 convolution_convert_fusion.1
  43.6 1.1 fusion.70
  45.2 1.6 fusion.55
  46.8 2.5 collective-permute-done.10
  49.3 11.6 %collective-permute-done.8 = bf16[2,2,64,1280]{3,2,1,0:T(8,128)(2,1)S(1)} collective-permute-done((bf16[2,2,64,1280]{3,2,1,0:T(8,128)(2,1)S(1)}, bf16[2,2,64,1280]{3,2,1,0:T(8,128)(2,1)S(1)}, u32[]{:S(2)}, u32[]{:S(2)}) %collective-permute-start.8) | collective-permute-done | bytes 655392 | tf_op jit(solution)/shard_map/ppermute | solution.py:19
  61.9 1.5 collective-permute-start.15
  63.4 9.5 %collective-permute-done.6 = bf16[2,2,64,1280]{3,2,1,0:T(8,128)(2,1)S(1)} collective-permute-done((bf16[2,2,64,1280]{3,2,1,0:T(8,128)(2,1)S(1)}, bf16[2,2,64,1280]{3,2,1,0:T(8,128)(2,1)S(1)}, u32[]{:S(2)}, u32[]{:S(2)}) %collective-permute-start.6) | collective-permute-done | bytes 655392 | tf_op jit(solution)/shard_map/ppermute | solution.py:19
  75.5 2.9 %collective-permute-start.11 = (bf16[2,1,64,1280]{3,2,1,0:T(8,128)(2,1)}, bf16[2,1,64,1280]{3,2,1,0:T(8,128)(2,1)S(1)}, u32[]{:S(2)}, u32[]{:S(2)}) collective-permute-start(bf16[2,1,64,1280]{3,2,1,0:T(8,128)(2,1)} %get-tuple-element.206), channel_id=1, source_target_pairs={{0,2},{1,3},{2,0},{3,1},{4,6},{5,7},{6,4},{7,5},{8,10},{9,11},{10,... | collective-permute-start | bytes 983048 | tf_op jit(solution)/shard_map/ppermute | solution.py:19
  78.8 4.8 %convolution_convert_fusion = bf16[2,2,64,1280]{3,2,1,0:T(8,128)(2,1)S(1)} fusion(s32[]{:T(128)S(6)} %select_n.81, bf16[1,2,2,64,2048]{4,3,2,1,0:T(8,128)(2,1)} %bitcast.35, bf16[1,2,2,64,2048]{4,3,2,1,0:T(8,128)(2,1)} %bitcast.36, f32[2048]{0:T(1024)S(1)} %bitcast.366, bf16[2048,128]{1,0:T(8,128)(2,1)} %bitcast.352, bf16[2048,128]{1,0:T(8,128)(2,1)} %bitcast.356, ...), kind=kOutput, calls=%fused_computation.31 | convolution fusion | flops 1360330752 | bytes 8003588 | tf_op jit(solution)/shard_map/dot_general | solution.py:133
  83.7 1.3 fusion.65
  85.0 1.6 fusion.56
  86.6 12.7 %collective-permute-done.12 = bf16[2,1,64,1280]{3,2,1,0:T(8,128)(2,1)S(1)} collective-permute-done((bf16[2,1,64,1280]{3,2,1,0:T(8,128)(2,1)}, bf16[2,1,64,1280]{3,2,1,0:T(8,128)(2,1)S(1)}, u32[]{:S(2)}, u32[]{:S(2)}) %collective-permute-start.12) | collective-permute-done | bytes 327712 | tf_op jit(solution)/shard_map/ppermute | solution.py:19
  99.3 6.9 %collective-permute-done.11 = bf16[2,1,64,1280]{3,2,1,0:T(8,128)(2,1)S(1)} collective-permute-done((bf16[2,1,64,1280]{3,2,1,0:T(8,128)(2,1)}, bf16[2,1,64,1280]{3,2,1,0:T(8,128)(2,1)S(1)}, u32[]{:S(2)}, u32[]{:S(2)}) %collective-permute-start.11) | collective-permute-done | bytes 327712 | tf_op jit(solution)/shard_map/ppermute | solution.py:19
  106.5 2.0 collective-permute-start.18
  108.5 2.4 collective-permute-start.19
  110.9 9.8 %collective-permute-done.20 = bf16[2,2,64,1280]{3,2,1,0:T(8,128)(2,1)S(1)} collective-permute-done((bf16[2,2,64,1280]{3,2,1,0:T(8,128)(2,1)S(1)}, bf16[2,2,64,1280]{3,2,1,0:T(8,128)(2,1)S(1)}, u32[]{:S(2)}, u32[]{:S(2)}) %collective-permute-start.20) | collective-permute-done | bytes 655392 | tf_op jit(solution)/shard_map/ppermute | solution.py:19
  124.1 4.5 %shard_map.141 = bf16[256,1024]{1,0:T(8,128)(2,1)S(1)} custom-call(f32[128,1280]{1,0:T(8,128)S(1)} %bitcast.279, f32[128,1280]{1,0:T(8,128)S(1)} %bitcast.283, bf16[128,1280]{1,0:T(8,128)(2,1)S(1)} %bitcast.290, bf16[128,1280]{1,0:T(8,128)(2,1)S(1)} %bitcast.294, f32[256,1]{1,0:T(8,128)S(1)} %squeeze.177.inverse, f32[256,128]{1,0:T(8,128)S(1)} %pad_maximum_fusion.3.cosine, ...), custom_call_target="tpu_custom_call" | custom-call | flops 1073741824 | bytes 2097152 | tf_op jit(solution)/shard_map/pallas_call | solution.py:288
  128.8 2.8 %collective-permute-start.23 = (bf16[2,1,64,1280]{3,2,1,0:T(8,128)(2,1)}, bf16[2,1,64,1280]{3,2,1,0:T(8,128)(2,1)S(1)}, u32[]{:S(2)}, u32[]{:S(2)}) collective-permute-start(bf16[2,1,64,1280]{3,2,1,0:T(8,128)(2,1)} %get-tuple-element.203), channel_id=1, source_target_pairs={{0,2},{1,3},{2,0},{3,1},{4,6},{5,7},{6,4},{7,5},{8,10},{9,11},{10,... | collective-permute-start | bytes 983048 | tf_op jit(solution)/shard_map/ppermute | solution.py:19
  131.7 35.3 %collective-permute-done.23 = bf16[2,1,64,1280]{3,2,1,0:T(8,128)(2,1)S(1)} collective-permute-done((bf16[2,1,64,1280]{3,2,1,0:T(8,128)(2,1)}, bf16[2,1,64,1280]{3,2,1,0:T(8,128)(2,1)S(1)}, u32[]{:S(2)}, u32[]{:S(2)}) %collective-permute-start.23) | collective-permute-done | bytes 327712 | tf_op jit(solution)/shard_map/ppermute | solution.py:19
  168.2 1.3 pad_maximum_fusion.2
  170.3 2.2 fusion.28
  174.6 3.5 %collective-permute-start.28 = (bf16[256,256]{1,0:T(8,128)(2,1)S(1)}, bf16[256,256]{1,0:T(8,128)(2,1)S(1)}, u32[]{:S(2)}, u32[]{:S(2)}) collective-permute-start(bf16[256,256]{1,0:T(8,128)(2,1)S(1)} %shard_map.142.rest_0_), channel_id=1, source_target_pairs={{0,3},{1,2},{2,1},{3,0},{4,7},{5,6},{6,5},{7,4},{8,11},{9,10},{10,... | collective-permute-start | bytes 393224 | tf_op jit(solution)/shard_map/ppermute | solution.py:23
  178.1 3.5 %fusion.24 = f32[2,128,2048]{2,1,0:T(8,128)S(1)} fusion(bf16[2,128,1024]{2,1,0:T(8,128)(2,1)S(1)} %bitcast.315, bf16[1,1024,2048]{2,1,0:T(8,128)(2,1)} %param.18), kind=kOutput, calls=%fused_computation.26 | convolution fusion | flops 1073741824 | bytes 6815744 | tf_op jit(solution)/shard_map/dot_general | solution.py:311
  181.6 1.6 add_bitcast_fusion
  183.3 1.6 collective-permute-start.25
  184.8 1.8 collective-permute-done.27.rest_2_
  186.7 14.6 %shard_map.143 = bf16[256,1024]{1,0:T(8,128)(2,1)S(1)} custom-call(f32[128,1280]{1,0:T(8,128)S(1)} %bitcast.277, f32[128,1280]{1,0:T(8,128)S(1)} %bitcast.281, bf16[128,1280]{1,0:T(8,128)(2,1)S(1)} %bitcast.288, bf16[128,1280]{1,0:T(8,128)(2,1)S(1)} %bitcast.292, f32[256,1]{1,0:T(8,128)S(1)} %squeeze.178.inverse, f32[256,128]{1,0:T(8,128)S(1)} %pad_maximum_fusion.3.cosine, ...), custom_call_target="tpu_custom_call" | custom-call | flops 1073741824 | bytes 2097152 | tf_op jit(solution)/shard_map/pallas_call | solution.py:288
  201.4 3.0 %collective-permute-start.39 = (bf16[256,1024]{1,0:T(8,128)(2,1)S(1)}, bf16[256,1024]{1,0:T(8,128)(2,1)S(1)}, u32[]{:S(2)}, u32[]{:S(2)}) collective-permute-start(bf16[256,1024]{1,0:T(8,128)(2,1)S(1)} %shard_map.143), channel_id=1, source_target_pairs={{0,1},{1,0},{2,3},{3,2},{4,5},{5,4},{6,7},{7,6},{8,9},{9,8},{10,11... | collective-permute-start | bytes 1572872 | tf_op jit(solution)/shard_map/ppermute | solution.py:19
  204.7 1.6 collective-permute-start.29
  206.3 1.7 fusion.31
  210.9 1.6 collective-permute-start.34
  213.3 1.1 collective-permute-done.32
  218.0 1.5 collective-permute-done.34
  219.6 6.1 %collective-permute-done.33 = bf16[1,64,2048]{2,1,0:T(8,128)(2,1)S(1)} collective-permute-done((bf16[1,64,2048]{2,1,0:T(8,128)(2,1)S(1)}, bf16[1,64,2048]{2,1,0:T(8,128)(2,1)S(1)}, u32[]{:S(2)}, u32[]{:S(2)}) %collective-permute-start.33) | collective-permute-done | bytes 262176 | tf_op jit(solution)/shard_map/ppermute | solution.py:19
  227.0 1.6 collective-permute-start.37
  228.6 1.5 collective-permute-start.36
  231.4 1.1 collective-permute-done.40
  234.8 1.1 collective-permute-done.41
  235.9 1.5 collective-permute-start.46
  239.4 2.1 collective-permute-done.42
  242.8 1.6 collective-permute-start.45
  244.7 3.4 %collective-permute-done.43 = bf16[1,64,2048]{2,1,0:T(8,128)(2,1)S(1)} collective-permute-done((bf16[1,64,2048]{2,1,0:T(8,128)(2,1)S(1)}, bf16[1,64,2048]{2,1,0:T(8,128)(2,1)S(1)}, u32[]{:S(2)}, u32[]{:S(2)}) %collective-permute-start.43) | collective-permute-done | bytes 262176 | tf_op jit(solution)/shard_map/ppermute | solution.py:28
  248.1 1.9 collective-permute-done.46
  251.5 1.1 collective-permute-done.47
  252.8 1.6 collective-permute-start.50
  254.4 1.6 collective-permute-start.49
  256.1 5.1 %collective-permute-done.50 = bf16[1,64,2048]{2,1,0:T(8,128)(2,1)S(1)} collective-permute-done((bf16[1,64,2048]{2,1,0:T(8,128)(2,1)S(1)}, bf16[1,64,2048]{2,1,0:T(8,128)(2,1)S(1)}, u32[]{:S(2)}, u32[]{:S(2)}) %collective-permute-start.50) | collective-permute-done | bytes 262176 | tf_op jit(solution)/shard_map/ppermute | solution.py:19
  261.3 1.6 collective-permute-start.51
  262.9 1.3 reverse_select_fusion.2
  264.1 4.7 %collective-permute-done.51 = bf16[1,64,2048]{2,1,0:T(8,128)(2,1)S(1)} collective-permute-done((bf16[1,64,2048]{2,1,0:T(8,128)(2,1)S(1)}, bf16[1,64,2048]{2,1,0:T(8,128)(2,1)S(1)}, u32[]{:S(2)}, u32[]{:S(2)}) %collective-permute-start.51) | collective-permute-done | bytes 262176 | tf_op jit(solution)/shard_map/ppermute | solution.py:28
  269.2 1.2 reverse_select_fusion
  (198 shorter events, 33.1 us)
Async XLA Ops:
  0.6 3.8 %collective-permute-start = (bf16[256,2048]{1,0:T(8,128)(2,1)}, bf16[256,2048]{1,0:T(8,128)(2,1)S(1)}, u32[]{:S(2)}, u32[]{:S(2)}) collective-permute-start(bf16[256,2048]{1,0:T(8,128)(2,1)} %bitcast.295), channel_id=1, source_target_pairs={{0,4},{4,0},{8,12},{12,8},{1,5},{5,1},{9,13},{13,9},{2,6},{6,2},{1... | collective-permute-start | bytes 3145736 | tf_op jit(solution)/shard_map/ppermute | solution.py:19
  1.1 28.3 %collective-permute-start.3 = (bf16[256,2048]{1,0:T(8,128)(2,1)}, bf16[256,2048]{1,0:T(8,128)(2,1)}, u32[]{:S(2)}, u32[]{:S(2)}) collective-permute-start(bf16[256,2048]{1,0:T(8,128)(2,1)} %bitcast.296), channel_id=1, source_target_pairs={{0,8},{4,12},{8,0},{12,4},{1,9},{5,13},{9,1},{13,5},{2,10},{6,14},... | collective-permute-start | bytes 3145736 | tf_op jit(solution)/shard_map/ppermute | solution.py:19
  5.6 4.7 %copy-start.16 = (bf16[1,2048,1024]{2,1,0:T(8,128)(2,1)S(1)}, bf16[1,2048,1024]{2,1,0:T(8,128)(2,1)}, u32[]{:S(2)}) copy-start(bf16[1,2048,1024]{2,1,0:T(8,128)(2,1)} %param.15) | copy-start | bytes 12582916
  10.1 4.6 %collective-permute-start.2 = (bf16[256,2048]{1,0:T(8,128)(2,1)S(1)}, bf16[256,2048]{1,0:T(8,128)(2,1)S(1)}, u32[]{:S(2)}, u32[]{:S(2)}) collective-permute-start(bf16[256,2048]{1,0:T(8,128)(2,1)S(1)} %bitcast.303), channel_id=1, source_target_pairs={{0,4},{4,0},{8,12},{12,8},{1,5},{5,1},{9,13},{13,9},{2,6},{6,2},{1... | collective-permute-start | bytes 3145736 | tf_op jit(solution)/shard_map/ppermute | solution.py:19
  11.9 17.4 %collective-permute-start.1 = (bf16[2,2,64,1280]{3,2,1,0:T(8,128)(2,1)S(1)}, bf16[2,2,64,1280]{3,2,1,0:T(8,128)(2,1)S(1)}, u32[]{:S(2)}, u32[]{:S(2)}) collective-permute-start(bf16[2,2,64,1280]{3,2,1,0:T(8,128)(2,1)S(1)} %convolution_convert_fusion.3), channel_id=1, source_target_pairs={{0,1},{1,0},{2,3},{3,2},{4,5},{5,4},{6,7},{7,6},{8,9},{9,8},{10,11... | collective-permute-start | bytes 1966088 | tf_op jit(solution)/shard_map/ppermute | solution.py:19
  29.5 11.4 %collective-permute-start.4 = (bf16[256,2048]{1,0:T(8,128)(2,1)}, bf16[256,2048]{1,0:T(8,128)(2,1)S(1)}, u32[]{:S(2)}, u32[]{:S(2)}) collective-permute-start(bf16[256,2048]{1,0:T(8,128)(2,1)} %collective-permute-done.3), channel_id=1, source_target_pairs={{0,4},{4,0},{8,12},{12,8},{1,5},{5,1},{9,13},{13,9},{2,6},{6,2},{1... | collective-permute-start | bytes 3145736 | tf_op jit(solution)/shard_map/ppermute | solution.py:19
  29.7 4.4 %collective-permute-start.5 = (f32[2,256]{1,0:T(2,128)S(1)}, f32[2,256]{1,0:T(2,128)S(1)}, u32[]{:S(2)}, u32[]{:S(2)}) collective-permute-start(f32[2,256]{1,0:T(2,128)S(1)} %pad_maximum_fusion.5), channel_id=1, source_target_pairs={{0,1},{1,0},{2,3},{3,2},{4,5},{5,4},{6,7},{7,6},{8,9},{9,8},{10,11... | collective-permute-start | bytes 6152 | tf_op jit(solution)/shard_map/ppermute | solution.py:19
  31.5 17.8 %collective-permute-start.10 = (bf16[2,1,64,1280]{3,2,1,0:T(8,128)(2,1)S(1)}, bf16[2,1,64,1280]{3,2,1,0:T(8,128)(2,1)S(1)}, u32[]{:S(2)}, u32[]{:S(2)}) collective-permute-start(bf16[2,1,64,1280]{3,2,1,0:T(8,128)(2,1)S(1)} %get-tuple-element.208), channel_id=1, source_target_pairs={{0,2},{1,3},{2,0},{3,1},{4,6},{5,7},{6,4},{7,5},{8,10},{9,11},{10,... | collective-permute-start | bytes 983048 | tf_op jit(solution)/shard_map/ppermute | solution.py:19
  34.1 15.2 %collective-permute-start.9 = (f32[2,256]{1,0:T(2,128)S(1)}, f32[2,256]{1,0:T(2,128)S(1)}, u32[]{:S(2)}, u32[]{:S(2)}) collective-permute-start(f32[2,256]{1,0:T(2,128)S(1)} %add.259), channel_id=1, source_target_pairs={{0,2},{1,3},{2,0},{3,1},{4,6},{5,7},{6,4},{7,5},{8,10},{9,11},{10,... | collective-permute-start | bytes 6152 | tf_op jit(solution)/shard_map/ppermute | solution.py:19
  36.2 24.7 %collective-permute-start.8 = (bf16[2,2,64,1280]{3,2,1,0:T(8,128)(2,1)S(1)}, bf16[2,2,64,1280]{3,2,1,0:T(8,128)(2,1)S(1)}, u32[]{:S(2)}, u32[]{:S(2)}) collective-permute-start(bf16[2,2,64,1280]{3,2,1,0:T(8,128)(2,1)S(1)} %convolution_convert_fusion.2), channel_id=1, source_target_pairs={{0,1},{1,0},{2,3},{3,2},{4,5},{5,4},{6,7},{7,6},{8,9},{9,8},{10,11... | collective-permute-start | bytes 1966088 | tf_op jit(solution)/shard_map/ppermute | solution.py:19
  37.8 24.0 %collective-permute-start.7 = (bf16[256,2048]{1,0:T(8,128)(2,1)S(1)}, bf16[256,2048]{1,0:T(8,128)(2,1)}, u32[]{:S(2)}, u32[]{:S(2)}) collective-permute-start(bf16[256,2048]{1,0:T(8,128)(2,1)S(1)} %bitcast.307), channel_id=1, source_target_pairs={{0,8},{4,12},{8,0},{12,4},{1,9},{5,13},{9,1},{13,5},{2,10},{6,14},... | collective-permute-start | bytes 3145736 | tf_op jit(solution)/shard_map/ppermute | solution.py:19
  44.7 28.3 %collective-permute-start.6 = (bf16[2,2,64,1280]{3,2,1,0:T(8,128)(2,1)S(1)}, bf16[2,2,64,1280]{3,2,1,0:T(8,128)(2,1)S(1)}, u32[]{:S(2)}, u32[]{:S(2)}) collective-permute-start(bf16[2,2,64,1280]{3,2,1,0:T(8,128)(2,1)S(1)} %convolution_convert_fusion.1), channel_id=1, source_target_pairs={{0,1},{1,0},{2,3},{3,2},{4,5},{5,4},{6,7},{7,6},{8,9},{9,8},{10,11... | collective-permute-start | bytes 1966088 | tf_op jit(solution)/shard_map/ppermute | solution.py:19
  49.2 57.0 %copy-start.3 = (bf16[2,1,64,1280]{3,2,1,0:T(8,128)(2,1)}, bf16[2,1,64,1280]{3,2,1,0:T(8,128)(2,1)S(1)}, u32[]{:S(2)}) copy-start(bf16[2,1,64,1280]{3,2,1,0:T(8,128)(2,1)S(1)} %collective-permute-done.10) | copy-start | bytes 983044
  61.8 17.0 %collective-permute-start.13 = (bf16[256,2048]{1,0:T(8,128)(2,1)}, bf16[256,2048]{1,0:T(8,128)(2,1)}, u32[]{:S(2)}, u32[]{:S(2)}) collective-permute-start(bf16[256,2048]{1,0:T(8,128)(2,1)} %collective-permute-done.7), channel_id=1, source_target_pairs={{0,4},{4,0},{8,12},{12,8},{1,5},{5,1},{9,13},{13,9},{2,6},{6,2},{1... | collective-permute-start | bytes 3145736 | tf_op jit(solution)/shard_map/ppermute | solution.py:19
  61.9 11.9 %collective-permute-start.15 = (f32[2,256]{1,0:T(2,128)S(1)}, f32[2,256]{1,0:T(2,128)S(1)}, u32[]{:S(2)}, u32[]{:S(2)}) collective-permute-start(f32[2,256]{1,0:T(2,128)S(1)} %add.260), channel_id=1, source_target_pairs={{0,8},{4,12},{8,0},{12,4},{1,9},{5,13},{9,1},{13,5},{2,10},{6,14},... | collective-permute-start | bytes 6152 | tf_op jit(solution)/shard_map/ppermute | solution.py:19
  73.8 4.6 %collective-permute-start.14 = (f32[2,256]{1,0:T(2,128)S(1)}, f32[2,256]{1,0:T(2,128)S(1)}, u32[]{:S(2)}, u32[]{:S(2)}) collective-permute-start(f32[2,256]{1,0:T(2,128)S(1)} %add.260), channel_id=1, source_target_pairs={{0,4},{4,0},{8,12},{12,8},{1,5},{5,1},{9,13},{13,9},{2,6},{6,2},{1... | collective-permute-start | bytes 6152 | tf_op jit(solution)/shard_map/ppermute | solution.py:19
  73.8 4.7 %collective-permute-start.16 = (f32[2,256]{1,0:T(2,128)S(1)}, f32[2,256]{1,0:T(2,128)S(1)}, u32[]{:S(2)}, u32[]{:S(2)}) collective-permute-start(f32[2,256]{1,0:T(2,128)S(1)} %collective-permute-done.15), channel_id=1, source_target_pairs={{0,4},{4,0},{8,12},{12,8},{1,5},{5,1},{9,13},{13,9},{2,6},{6,2},{1... | collective-permute-start | bytes 6152 | tf_op jit(solution)/shard_map/ppermute | solution.py:19
  75.4 23.9 %collective-permute-start.12 = (bf16[2,1,64,1280]{3,2,1,0:T(8,128)(2,1)}, bf16[2,1,64,1280]{3,2,1,0:T(8,128)(2,1)S(1)}, u32[]{:S(2)}, u32[]{:S(2)}) collective-permute-start(bf16[2,1,64,1280]{3,2,1,0:T(8,128)(2,1)} %get-tuple-element.205), channel_id=1, source_target_pairs={{0,2},{1,3},{2,0},{3,1},{4,6},{5,7},{6,4},{7,5},{8,10},{9,11},{10,... | collective-permute-start | bytes 983048 | tf_op jit(solution)/shard_map/ppermute | solution.py:19
  75.5 30.8 %collective-permute-start.11 = (bf16[2,1,64,1280]{3,2,1,0:T(8,128)(2,1)}, bf16[2,1,64,1280]{3,2,1,0:T(8,128)(2,1)S(1)}, u32[]{:S(2)}, u32[]{:S(2)}) collective-permute-start(bf16[2,1,64,1280]{3,2,1,0:T(8,128)(2,1)} %get-tuple-element.206), channel_id=1, source_target_pairs={{0,2},{1,3},{2,0},{3,1},{4,6},{5,7},{6,4},{7,5},{8,10},{9,11},{10,... | collective-permute-start | bytes 983048 | tf_op jit(solution)/shard_map/ppermute | solution.py:19
  78.8 6.2 %copy-start.18 = (bf16[1,2048,1024]{2,1,0:T(8,128)(2,1)S(1)}, bf16[1,2048,1024]{2,1,0:T(8,128)(2,1)}, u32[]{:S(2)}) copy-start(bf16[1,2048,1024]{2,1,0:T(8,128)(2,1)} %param.21) | copy-start | bytes 12582916
  78.8 6.2 %copy-start.22 = (bf16[1,2048,128]{2,1,0:T(8,128)(2,1)S(1)}, bf16[1,2048,128]{2,1,0:T(8,128)(2,1)}, u32[]{:S(2)}) copy-start(bf16[1,2048,128]{2,1,0:T(8,128)(2,1)} %param.23) | copy-start | bytes 1572868
  78.8 6.2 %copy-start.24 = (bf16[1,2048,128]{2,1,0:T(8,128)(2,1)S(1)}, bf16[1,2048,128]{2,1,0:T(8,128)(2,1)}, u32[]{:S(2)}) copy-start(bf16[1,2048,128]{2,1,0:T(8,128)(2,1)} %param.22) | copy-start | bytes 1572868
  83.6 37.1 %collective-permute-start.20 = (bf16[2,2,64,1280]{3,2,1,0:T(8,128)(2,1)S(1)}, bf16[2,2,64,1280]{3,2,1,0:T(8,128)(2,1)S(1)}, u32[]{:S(2)}, u32[]{:S(2)}) collective-permute-start(bf16[2,2,64,1280]{3,2,1,0:T(8,128)(2,1)S(1)} %convolution_convert_fusion), channel_id=1, source_target_pairs={{0,1},{1,0},{2,3},{3,2},{4,5},{5,4},{6,7},{7,6},{8,9},{9,8},{10,11... | collective-permute-start | bytes 1966088 | tf_op jit(solution)/shard_map/ppermute | solution.py:19
  86.6 35.5 %copy-start.7 = (f32[256,1]{1,0:T(8,128)S(1)}, f32[256,1]{1,0:T(8,128)}, u32[]{:S(2)}) copy-start(f32[256,1]{1,0:T(8,128)} %convert_element_type.470.q_pos) | copy-start | bytes 3076
  99.3 11.6 %copy-start = (bf16[2,1,64,1280]{3,2,1,0:T(8,128)(2,1)}, bf16[2,1,64,1280]{3,2,1,0:T(8,128)(2,1)S(1)}, u32[]{:S(2)}) copy-start(bf16[2,1,64,1280]{3,2,1,0:T(8,128)(2,1)S(1)} %collective-permute-done.12) | copy-start | bytes 983044
  106.3 15.9 %copy-start.5 = (bf16[2,1,64,1280]{3,2,1,0:T(8,128)(2,1)}, bf16[2,1,64,1280]{3,2,1,0:T(8,128)(2,1)S(1)}, u32[]{:S(2)}) copy-start(bf16[2,1,64,1280]{3,2,1,0:T(8,128)(2,1)S(1)} %collective-permute-done.11) | copy-start | bytes 983044
  106.5 15.7 %collective-permute-start.17 = (bf16[256,256]{1,0:T(8,128)(2,1)S(1)}, bf16[256,256]{1,0:T(8,128)(2,1)S(1)}, u32[]{:S(2)}, u32[]{:S(2)}) collective-permute-start(bf16[256,256]{1,0:T(8,128)(2,1)S(1)} %shard_map.140.rest_0_), channel_id=1, source_target_pairs={{0,1},{1,0},{2,3},{3,2},{4,5},{5,4},{6,7},{7,6},{8,9},{9,8},{10,11... | collective-permute-start | bytes 393224 | tf_op jit(solution)/shard_map/ppermute | solution.py:23
  106.5 15.6 %collective-permute-start.18 = (bf16[256,256]{1,0:T(8,128)(2,1)S(1)}, bf16[256,256]{1,0:T(8,128)(2,1)S(1)}, u32[]{:S(2)}, u32[]{:S(2)}) collective-permute-start(bf16[256,256]{1,0:T(8,128)(2,1)S(1)} %shard_map.140.rest_0_), channel_id=1, source_target_pairs={{0,2},{1,3},{2,0},{3,1},{4,6},{5,7},{6,4},{7,5},{8,10},{9,11},{10,... | collective-permute-start | bytes 393224 | tf_op jit(solution)/shard_map/ppermute | solution.py:23
  108.5 13.6 %collective-permute-start.19 = (bf16[256,256]{1,0:T(8,128)(2,1)S(1)}, bf16[256,256]{1,0:T(8,128)(2,1)S(1)}, u32[]{:S(2)}, u32[]{:S(2)}) collective-permute-start(bf16[256,256]{1,0:T(8,128)(2,1)S(1)} %shard_map.140.rest_0_), channel_id=1, source_target_pairs={{0,3},{1,2},{2,1},{3,0},{4,7},{5,6},{6,5},{7,4},{8,11},{9,10},{10,... | collective-permute-start | bytes 393224 | tf_op jit(solution)/shard_map/ppermute | solution.py:23
  128.5 39.6 %collective-permute-start.22 = (bf16[256,1024]{1,0:T(8,128)(2,1)S(1)}, bf16[256,1024]{1,0:T(8,128)(2,1)}, u32[]{:S(2)}, u32[]{:S(2)}) collective-permute-start(bf16[256,1024]{1,0:T(8,128)(2,1)S(1)} %shard_map.141), channel_id=1, source_target_pairs={{0,2},{1,3},{2,0},{3,1},{4,6},{5,7},{6,4},{7,5},{8,10},{9,11},{10,... | collective-permute-start | bytes 1572872 | tf_op jit(solution)/shard_map/ppermute | solution.py:19
  128.6 39.6 %collective-permute-start.21 = (bf16[256,1024]{1,0:T(8,128)(2,1)S(1)}, bf16[256,1024]{1,0:T(8,128)(2,1)}, u32[]{:S(2)}, u32[]{:S(2)}) collective-permute-start(bf16[256,1024]{1,0:T(8,128)(2,1)S(1)} %shard_map.141), channel_id=1, source_target_pairs={{0,1},{1,0},{2,3},{3,2},{4,5},{5,4},{6,7},{7,6},{8,9},{9,8},{10,11... | collective-permute-start | bytes 1572872 | tf_op jit(solution)/shard_map/ppermute | solution.py:19
  128.8 38.2 %collective-permute-start.23 = (bf16[2,1,64,1280]{3,2,1,0:T(8,128)(2,1)}, bf16[2,1,64,1280]{3,2,1,0:T(8,128)(2,1)S(1)}, u32[]{:S(2)}, u32[]{:S(2)}) collective-permute-start(bf16[2,1,64,1280]{3,2,1,0:T(8,128)(2,1)} %get-tuple-element.203), channel_id=1, source_target_pairs={{0,2},{1,3},{2,0},{3,1},{4,6},{5,7},{6,4},{7,5},{8,10},{9,11},{10,... | collective-permute-start | bytes 983048 | tf_op jit(solution)/shard_map/ppermute | solution.py:19
  172.6 9.1 %collective-permute-start.24 = (bf16[2,128,2048]{2,1,0:T(8,128)(2,1)}, bf16[2,128,2048]{2,1,0:T(8,128)(2,1)}, u32[]{:S(2)}, u32[]{:S(2)}) collective-permute-start(bf16[2,128,2048]{2,1,0:T(8,128)(2,1)} %fusion.28), channel_id=1, source_target_pairs={{0,4},{4,0},{8,12},{12,8},{1,5},{5,1},{9,13},{13,9},{2,6},{6,2},{1... | collective-permute-start | bytes 3145736 | tf_op jit(solution)/shard_map/ppermute | solution.py:19
  173.6 11.2 %collective-permute-start.26 = (bf16[256,256]{1,0:T(8,128)(2,1)S(1)}, bf16[256,256]{1,0:T(8,128)(2,1)S(1)}, u32[]{:S(2)}, u32[]{:S(2)}) collective-permute-start(bf16[256,256]{1,0:T(8,128)(2,1)S(1)} %shard_map.142.rest_0_), channel_id=1, source_target_pairs={{0,1},{1,0},{2,3},{3,2},{4,5},{5,4},{6,7},{7,6},{8,9},{9,8},{10,11... | collective-permute-start | bytes 393224 | tf_op jit(solution)/shard_map/ppermute | solution.py:23
  173.7 13.0 %collective-permute-start.27 = (bf16[256,256]{1,0:T(8,128)(2,1)S(1)}, bf16[256,256]{1,0:T(8,128)(2,1)S(1)}, u32[]{:S(2)}, u32[]{:S(2)}) collective-permute-start(bf16[256,256]{1,0:T(8,128)(2,1)S(1)} %shard_map.142.rest_0_), channel_id=1, source_target_pairs={{0,2},{1,3},{2,0},{3,1},{4,6},{5,7},{6,4},{7,5},{8,10},{9,11},{10,... | collective-permute-start | bytes 393224 | tf_op jit(solution)/shard_map/ppermute | solution.py:23
  174.6 12.1 %collective-permute-start.28 = (bf16[256,256]{1,0:T(8,128)(2,1)S(1)}, bf16[256,256]{1,0:T(8,128)(2,1)S(1)}, u32[]{:S(2)}, u32[]{:S(2)}) collective-permute-start(bf16[256,256]{1,0:T(8,128)(2,1)S(1)} %shard_map.142.rest_0_), channel_id=1, source_target_pairs={{0,3},{1,2},{2,1},{3,0},{4,7},{5,6},{6,5},{7,4},{8,11},{9,10},{10,... | collective-permute-start | bytes 393224 | tf_op jit(solution)/shard_map/ppermute | solution.py:23
  178.1 32.0 %collective-permute-start.30 = (bf16[256,1024]{1,0:T(8,128)(2,1)}, bf16[256,1024]{1,0:T(8,128)(2,1)S(1)}, u32[]{:S(2)}, u32[]{:S(2)}) collective-permute-start(bf16[256,1024]{1,0:T(8,128)(2,1)} %collective-permute-done.22), channel_id=1, source_target_pairs={{0,1},{1,0},{2,3},{3,2},{4,5},{5,4},{6,7},{7,6},{8,9},{9,8},{10,11... | collective-permute-start | bytes 1572872 | tf_op jit(solution)/shard_map/ppermute | solution.py:19
  181.6 5.1 %copy-start.2 = (bf16[2,1,64,1280]{3,2,1,0:T(8,128)(2,1)S(1)}, bf16[2,1,64,1280]{3,2,1,0:T(8,128)(2,1)}, u32[]{:S(2)}) copy-start(bf16[2,1,64,1280]{3,2,1,0:T(8,128)(2,1)} %copy-done) | copy-start | bytes 983044
  181.6 5.1 %copy-start.8 = (f32[256,1]{1,0:T(8,128)S(1)}, f32[256,1]{1,0:T(8,128)}, u32[]{:S(2)}) copy-start(f32[256,1]{1,0:T(8,128)} %convert_element_type.470.q_pos) | copy-start | bytes 3076
  183.3 21.2 %collective-permute-start.25 = (bf16[1,128,2048]{2,1,0:T(8,128)(2,1)S(1)}, bf16[1,128,2048]{2,1,0:T(8,128)(2,1)S(1)}, u32[]{:S(2)}, u32[]{:S(2)}) collective-permute-start(bf16[1,128,2048]{2,1,0:T(8,128)(2,1)S(1)} %fusion.91), channel_id=1, source_target_pairs={{0,8},{4,12},{8,0},{12,4},{1,9},{5,13},{9,1},{13,5},{2,10},{6,14},... | collective-permute-start | bytes 1572872 | tf_op jit(solution)/shard_map/ppermute | solution.py:19
  201.4 5.0 %copy-start.11 = (bf16[1,1024,2048]{2,1,0:T(8,128)(2,1)S(1)}, bf16[1,1024,2048]{2,1,0:T(8,128)(2,1)}, u32[]{:S(2)}) copy-start(bf16[1,1024,2048]{2,1,0:T(8,128)(2,1)} %param.18) | copy-start | bytes 12582916
  201.4 24.9 %collective-permute-start.39 = (bf16[256,1024]{1,0:T(8,128)(2,1)S(1)}, bf16[256,1024]{1,0:T(8,128)(2,1)S(1)}, u32[]{:S(2)}, u32[]{:S(2)}) collective-permute-start(bf16[256,1024]{1,0:T(8,128)(2,1)S(1)} %shard_map.143), channel_id=1, source_target_pairs={{0,1},{1,0},{2,3},{3,2},{4,5},{5,4},{6,7},{7,6},{8,9},{9,8},{10,11... | collective-permute-start | bytes 1572872 | tf_op jit(solution)/shard_map/ppermute | solution.py:19
  204.4 28.3 %collective-permute-start.38 = (bf16[256,1024]{1,0:T(8,128)(2,1)S(1)}, bf16[256,1024]{1,0:T(8,128)(2,1)S(1)}, u32[]{:S(2)}, u32[]{:S(2)}) collective-permute-start(bf16[256,1024]{1,0:T(8,128)(2,1)S(1)} %shard_map.143), channel_id=1, source_target_pairs={{0,2},{1,3},{2,0},{3,1},{4,6},{5,7},{6,4},{7,5},{8,10},{9,11},{10,... | collective-permute-start | bytes 1572872 | tf_op jit(solution)/shard_map/ppermute | solution.py:19
  204.7 21.1 %collective-permute-start.29 = (bf16[2,64,2048]{2,1,0:T(8,128)(2,1)S(1)}, bf16[2,64,2048]{2,1,0:T(8,128)(2,1)S(1)}, u32[]{:S(2)}, u32[]{:S(2)}) collective-permute-start(bf16[2,64,2048]{2,1,0:T(8,128)(2,1)S(1)} %add_convert_fusion), channel_id=1, source_target_pairs={{0,16},{16,0},{1,17},{17,1},{2,18},{18,2},{3,19},{19,3},{4,20},{20... | collective-permute-start | bytes 1572872 | tf_op jit(solution)/shard_map/ppermute | solution.py:28
  208.0 2.0 collective-permute-start.31
  210.9 8.6 %collective-permute-start.34 = (bf16[1,64,2048]{2,1,0:T(8,128)(2,1)S(1)}, bf16[1,64,2048]{2,1,0:T(8,128)(2,1)S(1)}, u32[]{:S(2)}, u32[]{:S(2)}) collective-permute-start(bf16[1,64,2048]{2,1,0:T(8,128)(2,1)S(1)} %fusion.92), channel_id=1, source_target_pairs={{0,8},{4,12},{8,0},{12,4},{1,9},{5,13},{9,1},{13,5},{2,10},{6,14},... | collective-permute-start | bytes 786440 | tf_op jit(solution)/shard_map/ppermute | solution.py:19
  212.5 1.9 collective-permute-start.32
  215.4 2.0 collective-permute-start.35
  217.4 8.3 %collective-permute-start.33 = (bf16[1,64,2048]{2,1,0:T(8,128)(2,1)S(1)}, bf16[1,64,2048]{2,1,0:T(8,128)(2,1)S(1)}, u32[]{:S(2)}, u32[]{:S(2)}) collective-permute-start(bf16[1,64,2048]{2,1,0:T(8,128)(2,1)S(1)} %fusion.93), channel_id=1, source_target_pairs={{0,8},{4,12},{8,0},{12,4},{1,9},{5,13},{9,1},{13,5},{2,10},{6,14},... | collective-permute-start | bytes 786440 | tf_op jit(solution)/shard_map/ppermute | solution.py:19
  227.0 10.6 %collective-permute-start.37 = (bf16[1,64,2048]{2,1,0:T(8,128)(2,1)S(1)}, bf16[1,64,2048]{2,1,0:T(8,128)(2,1)S(1)}, u32[]{:S(2)}, u32[]{:S(2)}) collective-permute-start(bf16[1,64,2048]{2,1,0:T(8,128)(2,1)S(1)} %fusion.94), channel_id=1, source_target_pairs={{0,8},{4,12},{8,0},{12,4},{1,9},{5,13},{9,1},{13,5},{2,10},{6,14},... | collective-permute-start | bytes 786440 | tf_op jit(solution)/shard_map/ppermute | solution.py:19
  228.6 10.2 %collective-permute-start.36 = (bf16[1,64,2048]{2,1,0:T(8,128)(2,1)S(1)}, bf16[1,64,2048]{2,1,0:T(8,128)(2,1)S(1)}, u32[]{:S(2)}, u32[]{:S(2)}) collective-permute-start(bf16[1,64,2048]{2,1,0:T(8,128)(2,1)S(1)} %add_convert_fusion.10), channel_id=1, source_target_pairs={{0,16},{16,0},{1,17},{17,1},{2,18},{18,2},{3,19},{19,3},{4,20},{20... | collective-permute-start | bytes 786440 | tf_op jit(solution)/shard_map/ppermute | solution.py:28
  230.1 11.4 %collective-permute-start.42 = (bf16[1,64,2048]{2,1,0:T(8,128)(2,1)S(1)}, bf16[1,64,2048]{2,1,0:T(8,128)(2,1)S(1)}, u32[]{:S(2)}, u32[]{:S(2)}) collective-permute-start(bf16[1,64,2048]{2,1,0:T(8,128)(2,1)S(1)} %add_convert_fusion.9), channel_id=1, source_target_pairs={{0,16},{16,0},{1,17},{17,1},{2,18},{18,2},{3,19},{19,3},{4,20},{20... | collective-permute-start | bytes 786440 | tf_op jit(solution)/shard_map/ppermute | solution.py:28
  230.6 1.9 collective-permute-start.40
  233.4 5.2 %copy-start.15 = (bf16[1,256,2048]{2,1,0:T(8,128)(2,1)S(1)}, bf16[1,256,2048]{2,1,0:T(8,128)(2,1)}, u32[]{:S(2)}) copy-start(bf16[1,256,2048]{2,1,0:T(8,128)(2,1)} %param.19) | copy-start | bytes 3145732
  233.4 9.2 %collective-permute-start.44 = (bf16[1,64,2048]{2,1,0:T(8,128)(2,1)S(1)}, bf16[1,64,2048]{2,1,0:T(8,128)(2,1)S(1)}, u32[]{:S(2)}, u32[]{:S(2)}) collective-permute-start(bf16[1,64,2048]{2,1,0:T(8,128)(2,1)S(1)} %fusion.95), channel_id=1, source_target_pairs={{0,8},{4,12},{8,0},{12,4},{1,9},{5,13},{9,1},{13,5},{2,10},{6,14},... | collective-permute-start | bytes 786440 | tf_op jit(solution)/shard_map/ppermute | solution.py:19
  234.0 1.9 collective-permute-start.41
  235.9 14.0 %collective-permute-start.46 = (bf16[256,1024]{1,0:T(8,128)(2,1)S(1)}, bf16[256,1024]{1,0:T(8,128)(2,1)S(1)}, u32[]{:S(2)}, u32[]{:S(2)}) collective-permute-start(bf16[256,1024]{1,0:T(8,128)(2,1)S(1)} %collective-permute-done.38), channel_id=1, source_target_pairs={{0,1},{1,0},{2,3},{3,2},{4,5},{5,4},{6,7},{7,6},{8,9},{9,8},{10,11... | collective-permute-start | bytes 1572872 | tf_op jit(solution)/shard_map/ppermute | solution.py:19
  237.6 16.7 %collective-permute-start.48 = (bf16[1,64,2048]{2,1,0:T(8,128)(2,1)S(1)}, bf16[1,64,2048]{2,1,0:T(8,128)(2,1)S(1)}, u32[]{:S(2)}, u32[]{:S(2)}) collective-permute-start(bf16[1,64,2048]{2,1,0:T(8,128)(2,1)S(1)} %fusion.96), channel_id=1, source_target_pairs={{0,8},{4,12},{8,0},{12,4},{1,9},{5,13},{9,1},{13,5},{2,10},{6,14},... | collective-permute-start | bytes 786440 | tf_op jit(solution)/shard_map/ppermute | solution.py:19
  238.8 9.3 %collective-permute-start.43 = (bf16[1,64,2048]{2,1,0:T(8,128)(2,1)S(1)}, bf16[1,64,2048]{2,1,0:T(8,128)(2,1)S(1)}, u32[]{:S(2)}, u32[]{:S(2)}) collective-permute-start(bf16[1,64,2048]{2,1,0:T(8,128)(2,1)S(1)} %add_convert_fusion.8), channel_id=1, source_target_pairs={{0,16},{16,0},{1,17},{17,1},{2,18},{18,2},{3,19},{19,3},{4,20},{20... | collective-permute-start | bytes 786440 | tf_op jit(solution)/shard_map/ppermute | solution.py:28
  242.8 11.6 %collective-permute-start.45 = (bf16[1,64,2048]{2,1,0:T(8,128)(2,1)S(1)}, bf16[1,64,2048]{2,1,0:T(8,128)(2,1)S(1)}, u32[]{:S(2)}, u32[]{:S(2)}) collective-permute-start(bf16[1,64,2048]{2,1,0:T(8,128)(2,1)S(1)} %add_convert_fusion.7), channel_id=1, source_target_pairs={{0,16},{16,0},{1,17},{17,1},{2,18},{18,2},{3,19},{19,3},{4,20},{20... | collective-permute-start | bytes 786440 | tf_op jit(solution)/shard_map/ppermute | solution.py:28
  250.7 2.0 collective-permute-start.47
  252.8 8.4 %collective-permute-start.50 = (bf16[1,64,2048]{2,1,0:T(8,128)(2,1)S(1)}, bf16[1,64,2048]{2,1,0:T(8,128)(2,1)S(1)}, u32[]{:S(2)}, u32[]{:S(2)}) collective-permute-start(bf16[1,64,2048]{2,1,0:T(8,128)(2,1)S(1)} %fusion.97), channel_id=1, source_target_pairs={{0,8},{4,12},{8,0},{12,4},{1,9},{5,13},{9,1},{13,5},{2,10},{6,14},... | collective-permute-start | bytes 786440 | tf_op jit(solution)/shard_map/ppermute | solution.py:19
  254.4 9.7 %collective-permute-start.49 = (bf16[1,64,2048]{2,1,0:T(8,128)(2,1)S(1)}, bf16[1,64,2048]{2,1,0:T(8,128)(2,1)S(1)}, u32[]{:S(2)}, u32[]{:S(2)}) collective-permute-start(bf16[1,64,2048]{2,1,0:T(8,128)(2,1)S(1)} %add_convert_fusion.6), channel_id=1, source_target_pairs={{0,16},{16,0},{1,17},{17,1},{2,18},{18,2},{3,19},{19,3},{4,20},{20... | collective-permute-start | bytes 786440 | tf_op jit(solution)/shard_map/ppermute | solution.py:28
  261.3 7.6 %collective-permute-start.51 = (bf16[1,64,2048]{2,1,0:T(8,128)(2,1)S(1)}, bf16[1,64,2048]{2,1,0:T(8,128)(2,1)S(1)}, u32[]{:S(2)}, u32[]{:S(2)}) collective-permute-start(bf16[1,64,2048]{2,1,0:T(8,128)(2,1)S(1)} %add_convert_fusion.5), channel_id=1, source_target_pairs={{0,16},{16,0},{1,17},{17,1},{2,18},{18,2},{3,19},{19,3},{4,20},{20... | collective-permute-start | bytes 786440 | tf_op jit(solution)/shard_map/ppermute | solution.py:28
  (15 other events, 54.6 us)
